TPU v7x, 32 devices: a whole 2x2x4 slice. The times are simulated.
32 devices in a mesh: dp: 4 (over y, core), ctx: 8 (over z, x).
Axes of the slice: x: 2, y: 2, z: 4, core: 2. Of those that a mesh axis runs over, the one named last changes fastest.
Arguments:
- tokens: bfloat16 [4, 1024, 1024], P('dp', 'ctx'), may hold values from -6 to 6
- w_qkv: bfloat16 [1024, 3072], P(('dp', 'ctx')), may hold values from -0.1875 to 0.1875
- b_query: bfloat16 [1024], P(('dp', 'ctx')), may hold values from -3 to 3
- b_value: bfloat16 [1024], P(('dp', 'ctx')), may hold values from -3 to 3
- w_out: bfloat16 [1024, 1024], P(('dp', 'ctx')), may hold values from -3 to 3
- b_out: bfloat16 [1024], P(('dp', 'ctx')), may hold values from -3 to 3
- ln1_gain: bfloat16 [1024], P(('dp', 'ctx')), may hold values from 0.25 to 1.75
- ln1_bias: bfloat16 [1024], P(('dp', 'ctx')), may hold values from -3 to 3
- w_up: bfloat16 [1024, 4096], P(('dp', 'ctx')), may hold values from -0.1875 to 0.1875
- b_up: bfloat16 [4096], P(('dp', 'ctx')), may hold values from -3 to 3
- w_down: bfloat16 [4096, 1024], P(('dp', 'ctx')), may hold values from -0.09375 to 0.09375
- b_down: bfloat16 [1024], P(('dp', 'ctx')), may hold values from -3 to 3
- ln2_gain: bfloat16 [1024], P(('dp', 'ctx')), may hold values from 0.25 to 1.75
- ln2_bias: bfloat16 [1024], P(('dp', 'ctx')), may hold values from -3 to 3
- segment_ids: int32 [4, 1024], P('dp', 'ctx'), may hold values from 0 to 3, as said below
- pad_mask: int32 [4, 1024], P('dp', 'ctx'), may hold values 0 or 1
- cotangent: bfloat16 [4, 1024, 1024], P('dp', 'ctx'), may hold values from -6 to 6
Outputs:
- layer_out: bfloat16 [4, 1024, 1024], P('dp', 'ctx')
- input_grad: bfloat16 [4, 1024, 1024], P('dp', 'ctx')
- grad_w_qkv: float32 [1024, 3072], P(('dp', 'ctx'))
- grad_b_query: float32 [1024], P(('dp', 'ctx'))
- grad_b_value: float32 [1024], P(('dp', 'ctx'))
- grad_w_out: float32 [1024, 1024], P(('dp', 'ctx'))
- grad_b_out: float32 [1024], P(('dp', 'ctx'))
- grad_ln1_gain: float32 [1024], P(('dp', 'ctx'))
- grad_ln1_bias: float32 [1024], P(('dp', 'ctx'))
- grad_w_up: float32 [1024, 4096], P(('dp', 'ctx'))
- grad_b_up: float32 [4096], P(('dp', 'ctx'))
- grad_w_down: float32 [4096, 1024], P(('dp', 'ctx'))
- grad_b_down: float32 [1024], P(('dp', 'ctx'))
- grad_ln2_gain: float32 [1024], P(('dp', 'ctx'))
- grad_ln2_bias: float32 [1024], P(('dp', 'ctx'))
Inputs may be any that keep to these rules, and one draw needn't show every extreme that they name: `segment_ids`: along each sequence the document numbers never fall, and each of 0 to 3 appears.
All inputs are finite; a program needn't handle non-finite values. No bound on the sum of `pad_mask` on one device may be relied on, other than what follows from the above.
Results may differ from a plain program's by a relative error of at most 0.015.
Values may be sent and summed in bfloat16 or wider, within the bound.
No kernel may reach another device: no remote copies, remote signals or barrier semaphores. Data moves between devices by JAX's collectives and lax.ppermute only.
A program may use at most 320 MiB of HBM per device.

v0:
```python
from functools import partial

import jax
import jax.numpy as jnp
from jax import lax
from jax.sharding import PartitionSpec as P

HEADS = 16
HEAD = 64
WINDOW = 1024


MASKED = -1e30
EPSILON = 1e-05


def layer_norm(values, scales, offsets):
    average = jnp.mean(values, axis=-1, keepdims=True)
    centred = values - average
    variance = jnp.mean(centred * centred, axis=-1, keepdims=True)
    return centred * lax.rsqrt(variance + EPSILON) * scales + offsets


def matmul(left, right):
    return jnp.dot(left, right, preferred_element_type=jnp.float32)


def rows_product(left, right):
    return lax.dot_general(
        left, right, (((0,), (0,)), ((), ())), preferred_element_type=jnp.float32
    )


def cols_product(left, right):
    return lax.dot_general(
        left, right, (((1,), (1,)), ((), ())), preferred_element_type=jnp.float32
    )


def split_heads(matrix):
    return matrix.reshape(matrix.shape[0], HEADS, HEAD)


def allowed_keys(query_tags, query_place, key_tags, key_place):
    same_doc = query_tags[:, None] // 2 == key_tags[None, :] // 2
    distance = jnp.abs(query_place[:, None] - key_place[None, :])
    usable = (key_tags[None, :] % 2 == 1) | (distance == 0)
    return same_doc & (distance <= WINDOW // 2) & usable


def masked_scores(query_block, key_heads, query_tags, query_place, key_tags, key_place):
    raw = (
        jnp.einsum("qhd,khd->hqk", query_block, key_heads, preferred_element_type=jnp.float32)
        * 0.125
    )
    return jnp.where(allowed_keys(query_tags, query_place, key_tags, key_place)[None], raw, MASKED)


def attend_forward(
    query_heads, key_heads, value_heads, query_tags, query_place, key_tags, key_place
):
    row_count = query_heads.shape[0]
    block_rows = min(row_count, 512)

    def one_block(block_index):
        scores = masked_scores(query_heads, key_heads, query_tags, query_place, key_tags, key_place)
        totals = jax.nn.logsumexp(scores, axis=2)
        probs = jnp.exp(scores - totals[:, :, None]).astype(jnp.bfloat16)
        output = jnp.einsum("hqk,khd->qhd", probs, value_heads, preferred_element_type=jnp.float32)
        return (output, totals)

    outputs, totals = lax.map(one_block, jnp.arange(row_count // block_rows, dtype=jnp.int32))
    return (outputs.reshape(row_count, HEADS * HEAD), totals)


def attend_backward(
    query_heads,
    key_heads,
    value_heads,
    grad_heads,
    deltas,
    totals,
    query_tags,
    query_place,
    key_tags,
    key_place,
):
    row_count = query_heads.shape[0]
    block_rows = min(row_count, 512)

    def one_block(running, block_index):
        key_grad, value_grad = running
        scores = masked_scores(query_heads, key_heads, query_tags, query_place, key_tags, key_place)
        probs = jnp.exp(scores - totals[block_index][:, :, None])
        dprobs = jnp.einsum(
            "qhd,khd->hqk", grad_heads, value_heads, preferred_element_type=jnp.float32
        )
        dscores = (probs * (dprobs - deltas[:, :, None])).astype(jnp.bfloat16)
        query_grad = (
            jnp.einsum("hqk,khd->qhd", dscores, key_heads, preferred_element_type=jnp.float32)
            * 0.125
        )
        key_grad = (
            key_grad
            + jnp.einsum("hqk,qhd->khd", dscores, query_heads, preferred_element_type=jnp.float32)
            * 0.125
        )
        value_grad = value_grad + jnp.einsum(
            "hqk,qhd->khd",
            probs.astype(jnp.bfloat16),
            grad_heads,
            preferred_element_type=jnp.float32,
        )
        return ((key_grad, value_grad), query_grad)

    zeros = jnp.zeros(key_heads.shape, jnp.float32)
    (key_grad, value_grad), query_grads = lax.scan(
        one_block, (zeros, zeros), jnp.arange(row_count // block_rows, dtype=jnp.int32)
    )
    key_count = key_heads.shape[0]
    return (
        query_grads.reshape(row_count, HEADS * HEAD),
        key_grad.reshape(key_count, HEADS * HEAD),
        value_grad.reshape(key_count, HEADS * HEAD),
    )


def clip_window(whole, rows_here, seq_length, own_index):
    neighbours = (WINDOW // 2 + rows_here - 1) // rows_here
    key_span = min((2 * neighbours + 1) * rows_here, seq_length)
    first_key = jnp.clip((own_index - neighbours) * rows_here, 0, seq_length - key_span)
    window = tuple((lax.dynamic_slice_in_dim(member, first_key, key_span, 0) for member in whole))
    return (window, first_key)


def window_keys(items, rows_here, seq_length, own_index):
    whole = (
        lax.all_gather(items[0], "ctx", axis=0, tiled=True),
        lax.all_gather(items[1], "ctx", axis=0, tiled=True),
        lax.all_gather(items[2], "ctx", axis=0, tiled=True),
    )
    return clip_window(whole, rows_here, seq_length, own_index)


def window_keys_again(items, rows_here, seq_length, own_index):
    whole = (
        lax.all_gather(items[0], "ctx", axis=0, tiled=True),
        lax.all_gather(items[1], "ctx", axis=0, tiled=True),
        lax.all_gather(items[2], "ctx", axis=0, tiled=True),
    )
    return clip_window(whole, rows_here, seq_length, own_index)


def return_key_grads(key_grad, value_grad, rows_here, first_key):
    width = key_grad.shape[1]
    joined = jnp.concatenate([key_grad, value_grad], axis=1)
    key_span = joined.shape[0]
    count = rows_here * lax.axis_size("ctx")
    padding = jnp.zeros((count, 2 * width), jnp.float32)
    padded = jnp.concatenate([padding, joined, padding], axis=0)
    offset = jnp.clip(jnp.int32(0) - first_key + count, 0, key_span + count)
    summed = lax.psum_scatter(
        lax.dynamic_slice_in_dim(padded, offset, count, 0), "ctx", scatter_dimension=0, tiled=True
    )
    return (summed[:, :width], summed[:, width:])


def body(
    tokens,
    w_qkv,
    b_query,
    b_value,
    w_out,
    b_out,
    ln1_gain,
    ln1_bias,
    w_up,
    b_up,
    w_down,
    b_down,
    ln2_gain,
    ln2_bias,
    segment_ids,
    pad_mask,
    cotangent,
):
    weight_shards = (
        w_qkv,
        b_query,
        b_value,
        w_out,
        b_out,
        ln1_gain,
        ln1_bias,
        w_up,
        b_up,
        w_down,
        b_down,
        ln2_gain,
        ln2_bias,
    )
    gathered = (
        lax.all_gather(weight_shards[0], ("dp", "ctx"), axis=0, tiled=True),
        lax.all_gather(weight_shards[1], ("dp", "ctx"), axis=0, tiled=True),
        lax.all_gather(weight_shards[2], ("dp", "ctx"), axis=0, tiled=True),
        lax.all_gather(weight_shards[3], ("dp", "ctx"), axis=0, tiled=True),
        lax.all_gather(weight_shards[4], ("dp", "ctx"), axis=0, tiled=True),
        lax.all_gather(weight_shards[5], ("dp", "ctx"), axis=0, tiled=True),
        lax.all_gather(weight_shards[6], ("dp", "ctx"), axis=0, tiled=True),
        lax.all_gather(weight_shards[7], ("dp", "ctx"), axis=0, tiled=True),
        lax.all_gather(weight_shards[8], ("dp", "ctx"), axis=0, tiled=True),
        lax.all_gather(weight_shards[9], ("dp", "ctx"), axis=0, tiled=True),
        lax.all_gather(weight_shards[10], ("dp", "ctx"), axis=0, tiled=True),
        lax.all_gather(weight_shards[11], ("dp", "ctx"), axis=0, tiled=True),
        lax.all_gather(weight_shards[12], ("dp", "ctx"), axis=0, tiled=True),
    )
    (
        full_qkv,
        full_bquery,
        full_bvalue,
        full_out,
        full_bout,
        full_gain_one,
        full_bias_one,
        full_up,
        full_bup,
        full_down,
        full_bdown,
        full_gain_two,
        full_bias_two,
    ) = gathered
    rows_here = tokens.shape[1]
    seq_length = rows_here * lax.axis_size("ctx")
    own_index = lax.axis_index("ctx")
    inputs = tokens[0]
    inputs_wide = inputs.astype(jnp.float32)
    model_width = inputs.shape[1]
    token_tags = 2 * (segment_ids[0] + 1) + pad_mask[0]
    query_place = own_index * rows_here + jnp.arange(rows_here, dtype=jnp.int32)
    mixed = matmul(inputs, full_qkv)
    queries = (mixed[:, :model_width] + full_bquery.astype(jnp.float32)).astype(jnp.bfloat16)
    keys = mixed[:, model_width : 2 * model_width].astype(jnp.bfloat16)
    values = (mixed[:, 2 * model_width :] + full_bvalue.astype(jnp.float32)).astype(jnp.bfloat16)
    (key_window, value_window, tag_window), first_key = window_keys(
        (keys, values, token_tags), rows_here, seq_length, own_index
    )
    key_place = first_key + jnp.arange(key_window.shape[0], dtype=jnp.int32)
    attended, totals = attend_forward(
        split_heads(queries),
        split_heads(key_window),
        split_heads(value_window),
        token_tags,
        query_place,
        tag_window,
        key_place,
    )
    attended_low = attended.astype(jnp.bfloat16)
    first = inputs_wide + matmul(attended_low, full_out) + full_bout.astype(jnp.float32)
    normed, first_pull = jax.vjp(
        layer_norm, first, full_gain_one.astype(jnp.float32), full_bias_one.astype(jnp.float32)
    )
    normed_low = normed.astype(jnp.bfloat16)
    hidden = matmul(normed_low, full_up) + full_bup.astype(jnp.float32)
    active, gelu_pull = jax.vjp(partial(jax.nn.gelu, approximate=False), hidden)
    active_low = active.astype(jnp.bfloat16)
    second = normed + matmul(active_low, full_down) + full_bdown.astype(jnp.float32)
    result, second_pull = jax.vjp(
        layer_norm, second, full_gain_two.astype(jnp.float32), full_bias_two.astype(jnp.float32)
    )
    gathered = (
        lax.all_gather(weight_shards[0], ("dp", "ctx"), axis=0, tiled=True),
        lax.all_gather(weight_shards[1], ("dp", "ctx"), axis=0, tiled=True),
        lax.all_gather(weight_shards[2], ("dp", "ctx"), axis=0, tiled=True),
        lax.all_gather(weight_shards[3], ("dp", "ctx"), axis=0, tiled=True),
        lax.all_gather(weight_shards[4], ("dp", "ctx"), axis=0, tiled=True),
        lax.all_gather(weight_shards[5], ("dp", "ctx"), axis=0, tiled=True),
        lax.all_gather(weight_shards[6], ("dp", "ctx"), axis=0, tiled=True),
        lax.all_gather(weight_shards[7], ("dp", "ctx"), axis=0, tiled=True),
        lax.all_gather(weight_shards[8], ("dp", "ctx"), axis=0, tiled=True),
        lax.all_gather(weight_shards[9], ("dp", "ctx"), axis=0, tiled=True),
        lax.all_gather(weight_shards[10], ("dp", "ctx"), axis=0, tiled=True),
        lax.all_gather(weight_shards[11], ("dp", "ctx"), axis=0, tiled=True),
        lax.all_gather(weight_shards[12], ("dp", "ctx"), axis=0, tiled=True),
    )
    back_qkv = gathered[0]
    back_out = gathered[3]
    back_up = gathered[7]
    back_down = gathered[9]
    grad_second, grad_gain_two, grad_bias_two = second_pull(cotangent[0].astype(jnp.float32))
    grad_outcome = grad_second.astype(jnp.bfloat16)
    grad_wdown = rows_product(active_low, grad_outcome)
    grad_bdown = jnp.sum(grad_outcome.astype(jnp.float32), axis=0)
    (grad_active,) = gelu_pull(cols_product(grad_outcome, back_down))
    grad_hidden = grad_active.astype(jnp.bfloat16)
    grad_wup = rows_product(normed_low, grad_hidden)
    grad_bup = jnp.sum(grad_hidden.astype(jnp.float32), axis=0)
    grad_normed = grad_second + cols_product(grad_hidden, back_up)
    grad_first, grad_gain_one, grad_bias_one = first_pull(grad_normed)
    grad_branch = grad_first.astype(jnp.bfloat16)
    grad_wout = rows_product(attended_low, grad_branch)
    grad_bout = jnp.sum(grad_branch.astype(jnp.float32), axis=0)
    grad_attended = cols_product(grad_branch, back_out).astype(jnp.bfloat16)
    deltas = jnp.sum(
        (grad_attended.astype(jnp.float32) * attended).reshape(rows_here, HEADS, HEAD), axis=2
    ).T
    (key_again, value_again, tag_again), first_again = window_keys_again(
        (keys, values, token_tags), rows_here, seq_length, own_index
    )
    place_again = first_again + jnp.arange(key_again.shape[0], dtype=jnp.int32)
    grad_queries, key_grad, value_grad = attend_backward(
        split_heads(queries),
        split_heads(key_again),
        split_heads(value_again),
        split_heads(grad_attended),
        deltas,
        totals,
        token_tags,
        query_place,
        tag_again,
        place_again,
    )
    key_total, value_total = return_key_grads(key_grad, value_grad, rows_here, first_again)
    grad_query_low = grad_queries.astype(jnp.bfloat16)
    grad_value_low = value_total.astype(jnp.bfloat16)
    grad_mixed = jnp.concatenate(
        [grad_query_low, key_total.astype(jnp.bfloat16), grad_value_low], axis=1
    )
    grad_wqkv = rows_product(inputs, grad_mixed)
    grad_bquery = jnp.sum(grad_query_low.astype(jnp.float32), axis=0)
    grad_bvalue = jnp.sum(grad_value_low.astype(jnp.float32), axis=0)
    grad_inputs = grad_first + cols_product(grad_mixed, back_qkv)
    summed = (
        lax.psum_scatter(grad_wqkv, ("dp", "ctx"), scatter_dimension=0, tiled=True),
        lax.psum_scatter(grad_bquery, ("dp", "ctx"), scatter_dimension=0, tiled=True),
        lax.psum_scatter(grad_bvalue, ("dp", "ctx"), scatter_dimension=0, tiled=True),
        lax.psum_scatter(grad_wout, ("dp", "ctx"), scatter_dimension=0, tiled=True),
        lax.psum_scatter(grad_bout, ("dp", "ctx"), scatter_dimension=0, tiled=True),
        lax.psum_scatter(grad_gain_one, ("dp", "ctx"), scatter_dimension=0, tiled=True),
        lax.psum_scatter(grad_bias_one, ("dp", "ctx"), scatter_dimension=0, tiled=True),
        lax.psum_scatter(grad_wup, ("dp", "ctx"), scatter_dimension=0, tiled=True),
        lax.psum_scatter(grad_bup, ("dp", "ctx"), scatter_dimension=0, tiled=True),
        lax.psum_scatter(grad_wdown, ("dp", "ctx"), scatter_dimension=0, tiled=True),
        lax.psum_scatter(grad_bdown, ("dp", "ctx"), scatter_dimension=0, tiled=True),
        lax.psum_scatter(grad_gain_two, ("dp", "ctx"), scatter_dimension=0, tiled=True),
        lax.psum_scatter(grad_bias_two, ("dp", "ctx"), scatter_dimension=0, tiled=True),
    )
    return (
        result.astype(jnp.bfloat16)[None],
        grad_inputs.astype(jnp.bfloat16)[None],
        summed[0],
        summed[1],
        summed[2],
        summed[3],
        summed[4],
        summed[5],
        summed[6],
        summed[7],
        summed[8],
        summed[9],
        summed[10],
        summed[11],
        summed[12],
    )


def solution(mesh):
    in_specs = (
        P("dp", "ctx", None),
        P(("dp", "ctx"), None),
        P(("dp", "ctx")),
        P(("dp", "ctx")),
        P(("dp", "ctx"), None),
        P(("dp", "ctx")),
        P(("dp", "ctx")),
        P(("dp", "ctx")),
        P(("dp", "ctx"), None),
        P(("dp", "ctx")),
        P(("dp", "ctx"), None),
        P(("dp", "ctx")),
        P(("dp", "ctx")),
        P(("dp", "ctx")),
        P("dp", "ctx"),
        P("dp", "ctx"),
        P("dp", "ctx", None),
    )
    out_specs = (
        P("dp", "ctx", None),
        P("dp", "ctx", None),
        P(("dp", "ctx"), None),
        P(("dp", "ctx")),
        P(("dp", "ctx")),
        P(("dp", "ctx"), None),
        P(("dp", "ctx")),
        P(("dp", "ctx")),
        P(("dp", "ctx")),
        P(("dp", "ctx"), None),
        P(("dp", "ctx")),
        P(("dp", "ctx"), None),
        P(("dp", "ctx")),
        P(("dp", "ctx")),
        P(("dp", "ctx")),
    )
    return jax.shard_map(body, mesh=mesh, in_specs=in_specs, out_specs=out_specs, check_vma=False)
```

profile of v0, /device:TPU:0, one launch (start us, length us, event | category | flops | bytes accessed | tf_op | source)
XLA Modules:
  0.0 1638.9 jit_solution(4851907085369557591)
XLA Ops:
  8.0 75.2 %all-gather.9.cloned.1.call-done = bf16[1024,3072]{1,0:T(8,128)(2,1)} async-done(((bf16[32,3072]{1,0:T(8,128)(2,1)}), bf16[1024,3072]{1,0:T(8,128)(2,1)}) %all-gather.9.cloned.1.call-update) | async-done | bytes 6291472 | tf_op jit(solution)/shard_map/all_gather | solution.py:203
  83.2 3.9 fusion.32
  89.9 40.0 %all-reduce.18 = (bf16[1024]{0:T(1024)(128)(2,1)S(1)}, bf16[1024]{0:T(1024)(128)(2,1)S(1)}, bf16[1024]{0:T(1024)(128)(2,1)S(1)}, bf16[1024]{0:T(1024)(128)(2,1)S...) all-reduce(bf16[1024]{0:T(1024)(128)(2,1)S(1)} %dynamic-update-slic, ...), channel_id=1, replica_groups=mesh['dp'=4,'ctx'=8] {'dp','ctx'}, use_global_device_ids=true, to_apply=%add.2 | all-reduce | flops 8192 | bytes 32768
  129.9 0.8 fusion.22
  132.6 65.5 %all-gather.1 = bf16[32,1,128]{2,1,0:T(2,128)(2,1)S(1)} all-gather(bf16[1,1,128]{2,1,0:T(2,128)(2,1)S(1)} %bitcast.109), channel_id=1, replica_groups=mesh['dp'=4,'ctx'=8] {'dp','ctx'}, dimensions={0}, use_global_device_ids=true | all-gather | bytes 8448 | tf_op jit(solution)/shard_map/all_gather | solution.py:211
  198.1 16.4 all-gather
  215.1 2.9 copy.51
  218.1 4.0 copy.49
  222.0 1.7 fusion.4
  223.8 2.2 exponential_reduce_fusion
  226.0 1.3 copy-done
  227.3 2.2 fusion.39
  229.5 1.0 copy.53
  230.5 14.9 all-gather.15.cloned.1.call-done
  245.4 2.3 fusion.58
  247.9 76.6 %all-gather.17.cloned.1.call-done = bf16[1024,4096]{1,0:T(8,128)(2,1)} async-done(((bf16[32,4096]{1,0:T(8,128)(2,1)}), bf16[1024,4096]{1,0:T(8,128)(2,1)}) %all-gather.17.cloned.1.call-update) | async-done | bytes 8388624 | tf_op jit(solution)/shard_map/all_gather | solution.py:210
  324.5 9.8 multiply_convert_fusion.1
  334.3 69.1 %all-gather.19.cloned.1.call-done = bf16[4096,1024]{1,0:T(8,128)(2,1)} async-done(((bf16[128,1024]{1,0:T(8,128)(2,1)}), bf16[4096,1024]{1,0:T(8,128)(2,1)}) %all-gather.19.cloned.1.call-update) | async-done | bytes 8388624 | tf_op jit(solution)/shard_map/all_gather | solution.py:212
  403.4 5.3 fusion.59
  409.2 1.0 fusion.56
  410.4 5.9 convert_reduce_fusion
  416.4 3.1 multiply_reduce_fusion
  421.2 1.6 convert_multiply_fusion
  422.9 0.8 copy.52
  423.7 7.8 fusion.37
  431.5 2.0 copy.54
  433.5 1.1 bitcast_reduce_fusion
  434.7 6.3 multiply_convert_fusion
  440.9 3.1 convolution_multiply_fusion
  444.2 1.1 broadcast_in_dim.103
  445.2 12.3 fusion.1
  457.6 0.9 copy-done.12
  458.5 3.7 fusion.34
  462.3 9.5 fusion.52
  471.9 3.8 convert_reduce_fusion.5
  475.7 129.7 %reduce-scatter.8.cloned.1.call-done = f32[128,2048]{0,1:T(8,128)} async-done(((f32[1024,2048]{0,1:T(8,128)}), f32[128,2048]{0,1:T(8,128)}) %reduce-scatter.8.cloned.1.call-update) | async-done | bytes 1048592 | tf_op jit(solution)/shard_map/reduce_scatter | solution.py:162
  605.5 1.3 convert.8
  606.7 6.3 convolution_bitcast_fusion
  613.1 12.6 copy.56
  625.9 1.0 copy-done.2
  626.9 8.1 fusion.60
  635.1 0.9 copy-done.16
  636.3 41.4 %all-reduce.17 = (f32[1024]{0:T(1024)S(1)}, f32[1024]{0:T(1024)S(1)}, f32[1024]{0:T(1024)S(1)}, f32[1024]{0:T(1024)S(1)}, f32[1024]{0:T(1024)S(1)}, /*index=5*/f...) all-reduce(f32[1024]{0:T(1024)S(1)} %reduce_sum.217, ...), channel_id=5, replica_groups=mesh['dp'=4,'ctx'=8] {'dp','ctx'}, use_global_device_ids=true, to_apply=%region_14.15.clone | all-reduce | flops 12288 | bytes 98304
  683.0 5.7 fusion.15
  688.7 62.7 %reduce-scatter.10.cloned.1.call-done = f32[32,1024]{1,0:T(8,128)} async-done(((f32[1024,1024]{1,0:T(8,128)}), f32[32,1024]{1,0:T(8,128)}) %reduce-scatter.10.cloned.1.call-update) | async-done | bytes 131088 | tf_op jit(solution)/shard_map/reduce_scatter | solution.py:336
  751.4 358.5 %reduce-scatter.12.cloned.1.call-done = f32[32,4096]{1,0:T(8,128)} async-done(((f32[1024,4096]{1,0:T(8,128)}), f32[32,4096]{1,0:T(8,128)}) %reduce-scatter.12.cloned.1.call-update) | async-done | bytes 524304 | tf_op jit(solution)/shard_map/reduce_scatter | solution.py:340
  1109.9 162.2 %reduce-scatter.16.cloned.1.call-done = f32[32,3072]{1,0:T(8,128)} async-done(((f32[1024,3072]{1,0:T(8,128)}), f32[32,3072]{1,0:T(8,128)}) %reduce-scatter.16.cloned.1.call-update) | async-done | bytes 393232
  1272.1 360.1 %reduce-scatter.14.cloned.1.call-done = f32[128,1024]{1,0:T(8,128)} async-done(((f32[4096,1024]{1,0:T(8,128)}), f32[128,1024]{1,0:T(8,128)}) %reduce-scatter.14.cloned.1.call-update) | async-done | bytes 524304 | tf_op jit(solution)/shard_map/reduce_scatter | solution.py:342
  (157 shorter events, 14.7 us)
Async XLA Ops:
  7.2 76.0 %all-gather.9.cloned.1.call-start = ((), (), s32[]{:S(2)}) async-start(), calls=%async_computation.5 | async-start | bytes 6488064 | tf_op jit(solution)/shard_map/all_gather | solution.py:203
  7.9 80.1 %copy-start.25 = (bf16[32]{0:T(256)(128)(2,1)S(1)}, bf16[32]{0:T(256)(128)(2,1)}, u32[]{:S(2)}) copy-start(bf16[32]{0:T(256)(128)(2,1)} %param.20) | copy-start | bytes 196
  7.9 80.3 %copy-start.26 = (bf16[32]{0:T(256)(128)(2,1)S(1)}, bf16[32]{0:T(256)(128)(2,1)}, u32[]{:S(2)}) copy-start(bf16[32]{0:T(256)(128)(2,1)} %param.19) | copy-start | bytes 196
  7.9 80.5 %copy-start.27 = (bf16[32]{0:T(256)(128)(2,1)S(1)}, bf16[32]{0:T(256)(128)(2,1)}, u32[]{:S(2)}) copy-start(bf16[32]{0:T(256)(128)(2,1)} %param.22) | copy-start | bytes 196
  7.9 80.7 %copy-start.28 = (bf16[32]{0:T(256)(128)(2,1)S(1)}, bf16[32]{0:T(256)(128)(2,1)}, u32[]{:S(2)}) copy-start(bf16[32]{0:T(256)(128)(2,1)} %param.23) | copy-start | bytes 196
  8.0 81.0 %copy-start.29 = (bf16[32]{0:T(256)(128)(2,1)S(1)}, bf16[32]{0:T(256)(128)(2,1)}, u32[]{:S(2)}) copy-start(bf16[32]{0:T(256)(128)(2,1)} %param.24) | copy-start | bytes 196
  8.0 81.2 %copy-start.30 = (bf16[32]{0:T(256)(128)(2,1)S(1)}, bf16[32]{0:T(256)(128)(2,1)}, u32[]{:S(2)}) copy-start(bf16[32]{0:T(256)(128)(2,1)} %param.28) | copy-start | bytes 196
  8.0 81.4 %copy-start.31 = (bf16[32]{0:T(256)(128)(2,1)S(1)}, bf16[32]{0:T(256)(128)(2,1)}, u32[]{:S(2)}) copy-start(bf16[32]{0:T(256)(128)(2,1)} %param.29) | copy-start | bytes 196
  8.0 81.7 %copy-start.32 = (bf16[32]{0:T(256)(128)(2,1)S(1)}, bf16[32]{0:T(256)(128)(2,1)}, u32[]{:S(2)}) copy-start(bf16[32]{0:T(256)(128)(2,1)} %param.30) | copy-start | bytes 196
  8.0 207.1 %all-gather.13.cloned.1.call-start = ((), (), s32[]{:S(2)}) async-start(), calls=%async_computation.7 | async-start | bytes 2359296 | tf_op jit(solution)/shard_map/all_gather | solution.py:138
  87.1 45.4 %copy-start.22 = (bf16[128]{0:T(256)(128)(2,1)S(1)}, bf16[128]{0:T(256)(128)(2,1)}, u32[]{:S(2)}) copy-start(bf16[128]{0:T(256)(128)(2,1)} %param.26) | copy-start | bytes 772
  87.1 111.0 %copy-start.23 = (s32[1,128]{1,0:T(1,128)S(1)}, s32[1,128]{1,0:T(1,128)}, u32[]{:S(2)}) copy-start(s32[1,128]{1,0:T(1,128)} %param.32) | copy-start | bytes 1540
  87.1 111.0 %copy-start.24 = (s32[1,128]{1,0:T(1,128)S(1)}, s32[1,128]{1,0:T(1,128)}, u32[]{:S(2)}) copy-start(s32[1,128]{1,0:T(1,128)} %param.31) | copy-start | bytes 1540
  87.9 130.1 %all-gather.11.cloned.1.call-start = ((), (), s32[]{:S(2)}) async-start(), calls=%async_computation.6 | async-start | bytes 2359296 | tf_op jit(solution)/shard_map/all_gather | solution.py:139
  130.7 114.7 %all-gather.15.cloned.1.call-start = ((), (), s32[]{:S(2)}) async-start(), calls=%async_computation.8 | async-start | bytes 2162688 | tf_op jit(solution)/shard_map/all_gather | solution.py:206
  131.3 193.2 %all-gather.17.cloned.1.call-start = ((), (), s32[]{:S(2)}) async-start(), calls=%async_computation.9 | async-start | bytes 8650752 | tf_op jit(solution)/shard_map/all_gather | solution.py:210
  131.9 271.5 %all-gather.19.cloned.1.call-start = ((), (), s32[]{:S(2)}) async-start(), calls=%async_computation.10 | async-start | bytes 8650752 | tf_op jit(solution)/shard_map/all_gather | solution.py:212
  132.5 473.0 %reduce-scatter.8.cloned.1.call-start = ((), (), s32[]{:S(2)}) async-start(), calls=%async_computation.11 | async-start | bytes 9437184 | tf_op jit(solution)/shard_map/reduce_scatter | solution.py:162
  215.0 7.0 copy-start.13
  223.7 3.6 copy-start
  223.7 3.5 copy-start.18
  227.3 18.1 %copy-start.8 = (bf16[1,128,1024]{2,1,0:T(8,128)(2,1)S(1)}, bf16[1,128,1024]{2,1,0:T(8,128)(2,1)}, u32[]{:S(2)}) copy-start(bf16[1,128,1024]{2,1,0:T(8,128)(2,1)} %param.17) | copy-start | bytes 786436
  229.5 1.0 copy-start.6
  403.4 6.9 slice-start
  403.4 5.5 copy-start.15
  403.4 6.9 slice-start.1
  409.2 7.1 slice-start.2
  410.3 6.0 copy-start.19
  410.4 6.0 slice-start.3
  416.3 3.1 copy-start.7
  416.4 4.3 copy-start.17
  419.4 1.8 copy-start.3
  419.7 0.8 copy-start.4
  420.6 2.2 copy-start.11
  423.7 10.9 copy-start.21
  434.6 6.3 copy-start.14
  440.9 3.2 copy-start.1
  457.6 0.9 copy-start.12
  457.6 293.8 %reduce-scatter.10.cloned.1.call-start = ((), (), s32[]{:S(2)}) async-start(), calls=%async_computation.12 | async-start | bytes 4325376 | tf_op jit(solution)/shard_map/reduce_scatter | solution.py:336
  462.2 647.6 %reduce-scatter.12.cloned.1.call-start = ((), (), s32[]{:S(2)}) async-start(), calls=%async_computation.13 | async-start | bytes 17301504 | tf_op jit(solution)/shard_map/reduce_scatter | solution.py:340
  471.8 800.2 %reduce-scatter.16.cloned.1.call-start = ((), (), s32[]{:S(2)}) async-start(), calls=%async_computation.15 | async-start | bytes 12976128
  475.7 137.3 %copy-start.9 = (bf16[16,64,128]{2,1,0:T(8,128)(2,1)}, bf16[16,64,128]{2,1,0:T(8,128)(2,1)S(1)}, u32[]{:S(2)}) copy-start(bf16[16,64,128]{2,1,0:T(8,128)(2,1)S(1)} %get-tuple-element.182) | copy-start | bytes 786436
  625.7 1.2 copy-start.2
  625.7 1.3 copy-start.20
  625.7 1006.5 %reduce-scatter.14.cloned.1.call-start = ((), (), s32[]{:S(2)}) async-start(), calls=%async_computation.14 | async-start | bytes 17301504 | tf_op jit(solution)/shard_map/reduce_scatter | solution.py:342
  635.0 0.9 copy-start.16
  635.0 47.9 %copy-start.5 = (f32[128,1024]{1,0:T(8,128)S(1)}, f32[128,1024]{1,0:T(8,128)}, u32[]{:S(2)}) copy-start(f32[128,1024]{1,0:T(8,128)} %copy-done.4) | copy-start | bytes 1572868
  635.0 47.9 %copy-start.10 = (bf16[16,64,128]{2,1,0:T(8,128)(2,1)S(1)}, bf16[16,64,128]{2,1,0:T(8,128)(2,1)}, u32[]{:S(2)}) copy-start(bf16[16,64,128]{2,1,0:T(8,128)(2,1)} %copy-done.9) | copy-start | bytes 786436
Sparse Core Ops, SparseCore 0:
  11.0 72.1 all-gather.8
  88.0 48.7 all-gather.12
  139.5 47.8 all-gather.10
  190.2 55.0 all-gather.14
  248.2 76.2 all-gather.16
  327.3 76.0 all-gather.18
  457.7 147.6 reduce-scatter.7
  608.4 142.9 reduce-scatter.9
  754.3 355.4 reduce-scatter.11
  1117.4 154.6 reduce-scatter.15
  1274.9 357.1 reduce-scatter.13
where the time goes:
time: 1640 us
  waiting for transfers between devices  1310 us (80%)
  blocking collectives  163 us (10%)
  matrix products  90.1 us (5%)
  local copies, waits for them, and re-layouts  38.3 us (2%)
  other arithmetic  20.5 us (1%)
    reduce_scatter x1, waiting for transfers between devices, body(): lax.psum_scatter(grad_wdown, ('dp', 'ctx'), scatter_dimension=0, tiled=True)  360 us
    reduce_scatter x1, waiting for transfers between devices, body(): lax.psum_scatter(grad_wup, ('dp', 'ctx'), scatter_dimension=0, tiled=True)  359 us
    unnamed x12, waiting for transfers between devices  165 us
    reduce_scatter x1, waiting for transfers between devices, return_key_grads(): lax.psum_scatter(lax.dynamic_slice_in_dim(padded, offset, count, 0), 'ctx...  130 us
    unnamed x2, blocking collectives  81.4 us
    all_gather x1, waiting for transfers between devices, body(): lax.all_gather(weight_shards[7], ('dp', 'ctx'), axis=0, tiled=True)  76.6 us
    all_gather x1, waiting for transfers between devices, body(): lax.all_gather(weight_shards[0], ('dp', 'ctx'), axis=0, tiled=True)  75.2 us
    all_gather x1, waiting for transfers between devices, body(): lax.all_gather(weight_shards[9], ('dp', 'ctx'), axis=0, tiled=True)  69.1 us
  transfers between devices with their start and end apart: 11, of which 9 were waited for; matrix products, arithmetic and copies ran while one was open for 5% of the time, Pallas kernels for 0%

commit v1 on v0

--- a/solution.py
+++ b/solution.py
@@ -3,6 +3,7 @@
 import jax
 import jax.numpy as jnp
 from jax import lax
+from jax.sharding import Mesh
 from jax.sharding import PartitionSpec as P
 
 HEADS = 16
@@ -165,7 +166,7 @@
     return (summed[:, :width], summed[:, width:])
 
 
-def body(
+def general_body(
     tokens,
     w_qkv,
     b_query,
@@ -363,7 +364,251 @@
     )
 
 
-def solution(mesh):
+def swap(member, axes, code):
+    count = 1
+    for axis in axes:
+        count *= lax.axis_size(axis)
+    return lax.ppermute(member, axes, [(place, place ^ code) for place in range(count)])
+
+
+GROUP = ("y", "core", "x")
+CTX = ("z", "x")
+DP = ("y", "core")
+EVERY = ("y", "core", "z", "x")
+
+
+def group_gather(block):
+    plane = [block] + [swap(block, ("y", "x"), code) for code in range(1, 4)]
+    return plane + [swap(member, ("core",), 1) for member in plane]
+
+
+def group_scatter(parts):
+    near = [
+        parts[code] + swap(parts[code + 4].astype(jnp.bfloat16), ("core",), 1).astype(jnp.float32)
+        for code in range(4)
+    ]
+    total = near[0]
+    for code in range(1, 4):
+        total = total + swap(near[code].astype(jnp.bfloat16), ("y", "x"), code).astype(jnp.float32)
+    return total
+
+
+def exchange_sum(parts, axes):
+    moved = lax.all_to_all(parts.astype(jnp.bfloat16), axes, 0, 0, tiled=True)
+    count = 1
+    for axis in axes:
+        count *= lax.axis_size(axis)
+    moved = moved.reshape((count, moved.shape[0] // count) + moved.shape[1:])
+    return jnp.sum(moved.astype(jnp.float32), axis=0)
+
+
+def heads_body(
+    tokens,
+    w_qkv,
+    b_query,
+    b_value,
+    w_out,
+    b_out,
+    ln1_gain,
+    ln1_bias,
+    w_up,
+    b_up,
+    w_down,
+    b_down,
+    ln2_gain,
+    ln2_bias,
+    segment_ids,
+    pad_mask,
+    cotangent,
+):
+    bf16, f32 = jnp.bfloat16, jnp.float32
+    inputs = tokens[0]
+    rows, width = inputs.shape
+    n_ctx = lax.axis_size(CTX)
+    n_z = lax.axis_size("z")
+    length = rows * n_ctx
+    heads_here = HEADS // n_ctx
+    cols = heads_here * HEAD
+    shard = w_qkv.shape[0]
+    units = w_down.shape[0]
+    ff = w_up.shape[1]
+    own_ctx = lax.axis_index(CTX)
+    own_dp = lax.axis_index(DP)
+
+    tags_here = (2 * (segment_ids[0] + 1) + pad_mask[0]).astype(bf16)
+    packed = jnp.concatenate(
+        [b_query, b_value, b_out, ln1_gain, ln1_bias, b_down, ln2_gain, ln2_bias, b_up, tags_here]
+    )
+    small = lax.all_gather(packed[None], EVERY, axis=0, tiled=True)
+    vectors = [small[:, i * shard : (i + 1) * shard].reshape(width).astype(f32) for i in range(8)]
+    bquery, bvalue, bout, gain_one, bias_one, bdown, gain_two, bias_two = vectors
+    n_dp = lax.axis_size(DP)
+    up_parts = small[:, 8 * shard : 8 * shard + units].reshape(n_dp, n_z, 2, units)
+    bup = lax.dynamic_slice(
+        up_parts, (own_dp, 0, lax.axis_index("x"), 0), (1, n_z, 1, units)
+    ).reshape(n_z * units).astype(f32)
+    tags = lax.dynamic_slice(
+        small[:, 8 * shard + units :].reshape(n_dp, length), (own_dp, 0), (1, length)
+    )[0].astype(jnp.int32)
+
+    qkv = w_qkv.reshape(shard, 3, n_ctx, cols).transpose(2, 0, 1, 3).reshape(n_ctx * shard, 3 * cols)
+    qkv = lax.all_to_all(qkv, CTX, 0, 0, tiled=True)
+    qkv = lax.all_gather(qkv, DP, axis=0, tiled=True)
+    whole = lax.all_gather(inputs, CTX, axis=0, tiled=True)
+    full_out = lax.all_gather(w_out, EVERY, axis=0, tiled=True)
+
+    up = w_up.reshape(shard, 2, 2, n_z, 2, units).transpose(1, 2, 4, 0, 3, 5)
+    up = lax.all_to_all(up.reshape(8 * shard, n_z * units), GROUP, 0, 0, tiled=True)
+    up = lax.all_gather(up, "z", axis=0, tiled=True)
+    up = up.reshape(n_z, 2, 2, 2, shard, n_z * units).transpose(1, 2, 0, 3, 4, 5)
+    up = up.reshape(width, n_z * units)
+    down = lax.all_gather(w_down, "z", axis=0, tiled=True)
+
+    mixed = matmul(whole, qkv)
+    query_bias = lax.dynamic_slice(bquery, (own_ctx * cols,), (cols,))
+    value_bias = lax.dynamic_slice(bvalue, (own_ctx * cols,), (cols,))
+    queries = (mixed[:, :cols] + query_bias).astype(bf16).reshape(length, heads_here, HEAD)
+    keys = mixed[:, cols : 2 * cols].astype(bf16).reshape(length, heads_here, HEAD)
+    values = (mixed[:, 2 * cols :] + value_bias).astype(bf16).reshape(length, heads_here, HEAD)
+    place = jnp.arange(length, dtype=jnp.int32)
+    scores = masked_scores(queries, keys, tags, place, tags, place)
+    totals = jax.nn.logsumexp(scores, axis=2)
+    probs = jnp.exp(scores - totals[:, :, None])
+    probs_low = probs.astype(bf16)
+    attended = jnp.einsum("hqk,khd->qhd", probs_low, values, preferred_element_type=f32)
+    moved = lax.all_to_all(attended.reshape(length, cols).astype(bf16), CTX, 0, 0, tiled=True)
+    attended_low = moved.reshape(n_ctx, rows, cols).transpose(1, 0, 2).reshape(rows, width)
+
+    first = inputs.astype(f32) + matmul(attended_low, full_out) + bout
+    normed, first_pull = jax.vjp(layer_norm, first, gain_one, bias_one)
+    normed_all = jnp.concatenate(group_gather(normed.astype(bf16)), axis=0)
+    hidden = matmul(normed_all, up) + bup
+    active, gelu_pull = jax.vjp(partial(jax.nn.gelu, approximate=False), hidden)
+    active_low = active.astype(bf16)
+    outcome = matmul(active_low, down)
+    second = normed + group_scatter(jnp.split(outcome, 8)) + bdown
+    result, second_pull = jax.vjp(layer_norm, second, gain_two, bias_two)
+
+    grad_second, grad_gain_two, grad_bias_two = second_pull(cotangent[0].astype(f32))
+    grad_z = grad_second.astype(bf16)
+    grad_bdown = jnp.sum(grad_z.astype(f32), axis=0)
+    grad_z_all = jnp.concatenate(group_gather(grad_z), axis=0)
+    (grad_active,) = gelu_pull(cols_product(grad_z_all, down))
+    grad_hidden = grad_active.astype(bf16)
+    back = cols_product(grad_hidden, up)
+    grad_normed = grad_second + group_scatter(jnp.split(back, 8))
+    grad_wdown = rows_product(active_low, grad_z_all)
+    grad_bup = jnp.sum(grad_hidden.astype(f32), axis=0)
+    down_parts = jnp.concatenate(
+        [grad_wdown, jnp.broadcast_to(grad_bup[:, None], (n_z * units, 128))], axis=1
+    )
+    down_sum = exchange_sum(down_parts, ("z",))
+    grad_wdown_out, grad_bup_out = down_sum[:, :width], down_sum[:, width]
+    grad_wup = rows_product(normed_all, grad_hidden)
+    up_sum = exchange_sum(
+        grad_wup.reshape(2, 2, n_z, 2, shard, n_z * units)
+        .transpose(2, 0, 1, 3, 4, 5)
+        .reshape(n_z, 8 * shard, n_z * units)
+        .reshape(n_z * 8 * shard, n_z * units),
+        ("z",),
+    )
+    up_sum = lax.all_to_all(up_sum, GROUP, 0, 0, tiled=True)
+    grad_wup_out = (
+        up_sum.reshape(2, 2, 2, shard, n_z, units).transpose(3, 0, 1, 4, 2, 5).reshape(shard, ff)
+    )
+
+    grad_first, grad_gain_one, grad_bias_one = first_pull(grad_normed)
+    grad_branch = grad_first.astype(bf16)
+    grad_bout = jnp.sum(grad_branch.astype(f32), axis=0)
+    grad_attended = cols_product(grad_branch, full_out).astype(bf16)
+    moved = grad_attended.reshape(rows, n_ctx, cols).transpose(1, 0, 2).reshape(length, cols)
+    moved = lax.all_to_all(moved, CTX, 0, 0, tiled=True)
+    grad_heads = moved.reshape(length, heads_here, HEAD)
+
+    grad_wout = rows_product(attended_low, grad_branch)
+    extra = jnp.stack(
+        [grad_bout, grad_gain_one, grad_bias_one, grad_bdown, grad_gain_two, grad_bias_two], axis=1
+    )
+    extra = jnp.pad(extra, ((0, 0), (0, 122)))
+    out_parts = jnp.concatenate([grad_wout, extra], axis=1)
+    out_sum = exchange_sum(out_parts, EVERY)
+    grad_wout_out = out_sum[:, :width]
+    thin = out_sum[:, width:]
+
+    deltas = jnp.sum(
+        grad_heads.astype(f32) * attended.reshape(length, heads_here, HEAD), axis=2
+    ).T
+    dprobs = jnp.einsum("qhd,khd->hqk", grad_heads, values, preferred_element_type=f32)
+    dscores = (probs * (dprobs - deltas[:, :, None])).astype(bf16)
+    grad_queries = jnp.einsum("hqk,khd->qhd", dscores, keys, preferred_element_type=f32) * 0.125
+    grad_keys = jnp.einsum("hqk,qhd->khd", dscores, queries, preferred_element_type=f32) * 0.125
+    grad_values = jnp.einsum("hqk,qhd->khd", probs_low, grad_heads, preferred_element_type=f32)
+    grad_mixed = jnp.concatenate(
+        [v.astype(bf16).reshape(length, cols) for v in (grad_queries, grad_keys, grad_values)],
+        axis=1,
+    )
+    grad_bias = jnp.sum(grad_mixed.astype(f32), axis=0)
+    grad_qkv = rows_product(whole, grad_mixed)
+    grad_qkv = jnp.concatenate(
+        [
+            grad_qkv.reshape(n_dp, n_ctx * shard, 3 * cols),
+            jnp.broadcast_to(grad_bias, (n_dp, 16, 3 * cols)),
+        ],
+        axis=1,
+    ).reshape(-1, 3 * cols)
+    qkv_sum = exchange_sum(grad_qkv, DP)
+    qkv_rows = qkv_sum[: n_ctx * shard].reshape(n_ctx, shard, 3 * cols)
+    qkv_bias = jnp.broadcast_to(qkv_sum[n_ctx * shard :][:8], (n_ctx, 8, 3 * cols))
+    qkv_sum = jnp.concatenate([qkv_rows, qkv_bias], axis=1).reshape(-1, 3 * cols)
+    qkv_sum = lax.all_to_all(qkv_sum, CTX, 0, 0, tiled=True).reshape(n_ctx, shard + 8, 3, cols)
+    grad_wqkv_out = qkv_sum[:, :shard].transpose(1, 2, 0, 3).reshape(shard, 3 * width)
+    bias_sum = qkv_sum[:, shard].transpose(1, 0, 2).reshape(3, width)
+    first_own = (own_dp * n_ctx + own_ctx) * shard
+    bias_own = lax.dynamic_slice(bias_sum, (0, first_own), (3, shard))
+
+    input_parts = cols_product(grad_mixed, qkv)
+    grad_inputs = grad_first + exchange_sum(input_parts, CTX)
+    return (
+        result.astype(bf16)[None],
+        grad_inputs.astype(bf16)[None],
+        grad_wqkv_out,
+        bias_own[0],
+        bias_own[2],
+        grad_wout_out,
+        thin[:, 0],
+        thin[:, 1],
+        thin[:, 2],
+        grad_wup_out,
+        grad_bup_out,
+        grad_wdown_out,
+        thin[:, 3],
+        thin[:, 4],
+        thin[:, 5],
+    )
+
+
+def call_heads(mesh, *arrays):
+    grid = Mesh(mesh.devices.reshape(2, 2, 4, 2), EVERY)
+    rows, lone, block = P(EVERY, None), P(EVERY), P(DP, CTX, None)
+    in_specs = (
+        block, rows, lone, lone, rows, lone, lone, lone, rows, lone, rows, lone, lone, lone,
+        P(DP, CTX), P(DP, CTX), block,
+    )
+    out_specs = (
+        block, block, rows, lone, lone, rows, lone, lone, lone, rows, lone, rows, lone, lone, lone,
+    )
+    return jax.shard_map(
+        heads_body, mesh=grid, in_specs=in_specs, out_specs=out_specs, check_vma=False
+    )(*arrays)
+
+
+def call(mesh, *arrays):
+    if mesh.shape["dp"] == 4 and mesh.shape["ctx"] == 8 and arrays[0].shape[1] <= 1024:
+        return call_heads(mesh, *arrays)
+    return general_call(mesh)(*arrays)
+
+
+def general_call(mesh):
     in_specs = (
         P("dp", "ctx", None),
         P(("dp", "ctx"), None),
@@ -400,4 +645,8 @@
         P(("dp", "ctx")),
         P(("dp", "ctx")),
     )
-    return jax.shard_map(body, mesh=mesh, in_specs=in_specs, out_specs=out_specs, check_vma=False)
+    return jax.shard_map(general_body, mesh=mesh, in_specs=in_specs, out_specs=out_specs, check_vma=False)
+
+
+def solution(mesh):
+    return partial(call, mesh)

time: 1640 us -> 508 us (0.31)
  waiting for transfers between devices: 1310 us -> 229 us
  blocking collectives: 163 us -> 83.5 us
  starting transfers between devices: 0.61 us -> 62.5 us
  matrix products: 90.1 us -> 50.2 us
    reduce_scatter x4 -> x0, waiting for transfers between devices: 911 us -> none  [the longest x1 360 us: body(): lax.psum_scatter(grad_wdown, ('dp', 'ctx'), scatter_dimension=0, tiled=True)]
    all_gather x6 -> x4, waiting for transfers between devices: 236 us -> 31 us  [the longest x1 16.1 us: heads_body(): down = lax.all_gather(w_down, 'z', axis=0, tiled=True)]
    unnamed x12 -> x4, waiting for transfers between devices: 165 us -> 2.06 us
    all_to_all x0 -> x11, waiting for transfers between devices: none -> 156 us  [the longest x5 127 us: exchange_sum(): moved = lax.all_to_all(parts.astype(jnp.bfloat16), axes, 0, 0, tiled=True)]
    unnamed x2 -> x0, blocking collectives: 81.4 us -> none
    all_to_all x0 -> x11, starting transfers between devices: none -> 44.5 us  [the longest x5 19.4 us: exchange_sum(): moved = lax.all_to_all(parts.astype(jnp.bfloat16), axes, 0, 0, tiled=True)]
    ppermute x0 -> x28, waiting for transfers between devices: none -> 39.7 us  [swap(): lax.ppermute(member, axes, [(place, place ^ code) for place in range(coun...]
    dot_general x4, matrix products: 27.6 us -> 8.56 us  [rows_product(): lax.dot_general(left, right, (((0,), (0,)), ((), ())), preferred_element_...]
  transfers between devices with their start and end apart: 11 -> 43, of which waited for: 9 -> 28; matrix products, arithmetic and copies ran while one was open for 5% -> 17% of each run, Pallas kernels for 0% -> 0%
where the time goes in v1:
time: 508 us; the launch traced here: 498 us
  waiting for transfers between devices  229 us (45%)
  blocking collectives  83.5 us (16%)
  starting transfers between devices  62.5 us (12%)
  matrix products  50.2 us (10%)
  local copies, waits for them, and re-layouts  34 us (7%)
  other arithmetic  23.5 us (5%)
  between operations  15.2 us (3%)
    all_to_all x5, waiting for transfers between devices, exchange_sum(): moved = lax.all_to_all(parts.astype(jnp.bfloat16), axes, 0, 0, tiled=True)  127 us
    all_gather x1, blocking collectives, heads_body(): small = lax.all_gather(packed[None], EVERY, axis=0, tiled=True)  68.6 us
    ppermute x28, waiting for transfers between devices, swap(): lax.ppermute(member, axes, [(place, place ^ code) for place in range(coun...  39.7 us
    all_to_all x5, starting transfers between devices, exchange_sum(): moved = lax.all_to_all(parts.astype(jnp.bfloat16), axes, 0, 0, tiled=True)  19.4 us
    ppermute x28, starting transfers between devices, swap(): lax.ppermute(member, axes, [(place, place ^ code) for place in range(coun...  17.8 us
    all_gather x1, waiting for transfers between devices, heads_body(): down = lax.all_gather(w_down, 'z', axis=0, tiled=True)  16.1 us
    all_gather x1, blocking collectives, heads_body(): qkv = lax.all_gather(qkv, DP, axis=0, tiled=True)  14.9 us
    all_gather x1, waiting for transfers between devices, heads_body(): up = lax.all_gather(up, 'z', axis=0, tiled=True)  14.9 us
  transfers between devices with their start and end apart: 43, of which 28 were waited for; matrix products, arithmetic and copies ran while one was open for 17% of the time, Pallas kernels for 0%

profile of v1, /device:TPU:0, one launch (start us, length us, event | category | flops | bytes accessed | tf_op | source)
XLA Modules:
  0.0 498.0 jit_solution(15495751708415521985)
XLA Ops:
  9.8 7.3 %all-to-all-start = ((bf16[8,32,384]{2,1,0:T(8,128)(2,1)}), bf16[8,32,384]{2,1,0:T(8,128)(2,1)S(1)}, u32[]{:S(2)}, u32[]{:S(2)}) async-start(bf16[8,32,384]{2,1,0:T(8,128)(2,1)} %all_to_all.56), calls=%async_computation | async-start | bytes 393216 | tf_op jit(solution)/shard_map/all_to_all | solution.py:455
  18.5 6.1 %concatenate.33 = bf16[512]{0:T(512)(128)(2,1)S(1)} concatenate(bf16[32]{0:T(256)(128)(2,1)} %param.19, bf16[32]{0:T(256)(128)(2,1)} %param.20, bf16[32]{0:T(256)(128)(2,1)} %param.22, bf16[32]{0:T(256)(128)(2,1)} %param.23, bf16[32]{0:T(256)(128)(2,1)} %param.24, bf16[32]{0:T(256)(128)(2,1)} %param.28, bf16[32]{0:T(256)(128)(2,1)} %param.29, bf16[32]{0:T(256)(128)(2,1)} %param.30, ...), dimensions={0} | concatenate | bytes 2048 | tf_op jit(solution)/shard_map/concatenate | solution.py:439
  24.6 68.6 %all-gather.2 = bf16[32,1,512]{2,1,0:T(2,128)(2,1)S(1)} all-gather(bf16[1,1,512]{2,1,0:T(2,128)(2,1)S(1)} %reshape.474), channel_id=3, replica_groups=mesh['y'=2,'core'=2,'z'=4,'x'=2] {'y','core','z','x'}, dimensions={0}, use_global_device_ids=true | all-gather | bytes 33792 | tf_op jit(solution)/shard_map/all_gather | solution.py:442
  94.8 2.3 fusion.5
  97.2 3.4 all-to-all-start.2
  100.6 14.9 %all_gather.19 = bf16[1024,384]{1,0:T(8,128)(2,1)} all-gather(bf16[256,384]{1,0:T(8,128)(2,1)S(1)} %bitcast.170), channel_id=1, replica_groups=mesh['y'=2,'core'=2,'z'=4,'x'=2] {'y','core'}, dimensions={0}, use_global_device_ids=true | all-gather | bytes 983040 | tf_op jit(solution)/shard_map/all_gather | solution.py:456
  115.5 2.8 fusion.10
  118.5 1.9 fusion.1
  120.4 2.0 exponential_reduce_fusion
  123.6 3.3 fusion.71
  127.7 3.4 all-to-all-start.1
  132.2 8.7 %all-to-all-done.1 = bf16[8,128,128]{1,2,0:T(8,128)(2,1)S(1)} async-done(((bf16[8,128,128]{1,2,0:T(8,128)(2,1)}), bf16[8,128,128]{1,2,0:T(8,128)(2,1)S(1)}, u32[]{:S(2)}, u32[]{:S(2)}) %all-to-all-start.1) | async-done | bytes 262176 | tf_op jit(solution)/shard_map/all_to_all | solution.py:479
  140.9 2.3 fusion.72
  147.9 14.9 %all-gather.10.cloned.1.call-done = bf16[1024,512]{1,0:T(8,128)(2,1)} async-done(((bf16[256,512]{1,0:T(8,128)(2,1)}), bf16[1024,512]{1,0:T(8,128)(2,1)}) %all-gather.10.cloned.1.call-update) | async-done | bytes 1048592 | tf_op jit(solution)/shard_map/all_gather | solution.py:462
  168.4 7.2 %multiply_convert_fusion.1 = (bf16[1024,512]{1,0:T(8,128)(2,1)S(1)}, f32[1024,512]{1,0:T(8,128)}, f32[1024,512]{1,0:T(8,128)}) fusion(f32[512]{0:T(512)S(1)} %bitcast.185, bf16[1024,1024]{1,0:T(8,128)(2,1)S(1)} %constant_dynamic-update-slice_fusion, bf16[1024,512]{1,0:T(8,128)(2,1)S(1)} %bitcast.143), kind=kOutput, calls=%fused_computation.24 | convolution fusion | flops 1108344832 | bytes 8390656 | tf_op jit(solution)/shard_map/dot_general | solution.py:26
  175.5 16.1 %all-gather.12.cloned.1.call-done = bf16[512,1024]{1,0:T(8,128)(2,1)} async-done(((bf16[128,1024]{1,0:T(8,128)(2,1)}), bf16[512,1024]{1,0:T(8,128)(2,1)}) %all-gather.12.cloned.1.call-update) | async-done | bytes 1048592 | tf_op jit(solution)/shard_map/all_gather | solution.py:465
  191.6 2.5 fusion.73
  202.5 5.8 %collective-permute-done.9 = bf16[128,1024]{1,0:T(8,128)(2,1)} collective-permute-done((bf16[128,1024]{1,0:T(8,128)(2,1)}, bf16[128,1024]{1,0:T(8,128)(2,1)}, u32[]{:S(2)}, u32[]{:S(2)}) %collective-permute-start.9) | collective-permute-done | bytes 262176 | tf_op jit(solution)/shard_map/ppermute | solution.py:371
  208.3 5.8 %collective-permute-done.13 = bf16[128,1024]{1,0:T(8,128)(2,1)} collective-permute-done((bf16[128,1024]{1,0:T(8,128)(2,1)}, bf16[128,1024]{1,0:T(8,128)(2,1)}, u32[]{:S(2)}, u32[]{:S(2)}) %collective-permute-start.13) | collective-permute-done | bytes 262176 | tf_op jit(solution)/shard_map/ppermute | solution.py:371
  215.5 1.7 fusion.64
  222.4 6.4 %collective-permute-done.16 = bf16[128,1024]{1,0:T(8,128)(2,1)S(1)} collective-permute-done((bf16[128,1024]{1,0:T(8,128)(2,1)S(1)}, bf16[128,1024]{1,0:T(8,128)(2,1)S(1)}, u32[]{:S(2)}, u32[]{:S(2)}) %collective-permute-start.16) | collective-permute-done | bytes 262176 | tf_op jit(solution)/shard_map/ppermute | solution.py:371
  228.8 2.7 collective-permute-done.15
  233.6 2.0 fusion.58
  243.2 5.7 %collective-permute-done.23 = bf16[128,1024]{1,0:T(8,128)(2,1)S(1)} collective-permute-done((bf16[128,1024]{1,0:T(8,128)(2,1)S(1)}, bf16[128,1024]{1,0:T(8,128)(2,1)S(1)}, u32[]{:S(2)}, u32[]{:S(2)}) %collective-permute-start.23) | collective-permute-done | bytes 262176 | tf_op jit(solution)/shard_map/ppermute | solution.py:371
  248.9 4.9 collective-permute-done.27
  257.7 4.1 all-to-all-start.3
  261.8 3.1 convolution_convert_fusion.3
  266.0 4.0 all-to-all-done.3
  270.0 4.5 all-to-all-start.8
  274.9 5.5 %multiply_convert_fusion = bf16[2,1024,1024]{1,2,0:T(8,128)(2,1)S(1)} fusion(f32[2,1024,1024]{1,2,0:T(8,128)} %copy-done.1, f32[2,1024]{1,0:T(2,128)S(1)} %bitcast.184, f32[2,1024]{1,0:T(2,128)S(1)} %log_add_fusion, pred[1024,1024]{0,1:T(8,128)(4,1)} %copy-done.6, bf16[1024,2,64]{0,2,1:T(8,128)(2,1)S(1)} %reshape.449, bf16[1024,2,64]{0,2,1:T(8,128)(2,1)} %bitcast.179), kind=kOutput, calls=%fused_computation | convolution fusion | flops 281018368 | bytes 14172160 | tf_op jit(solution)/shard_map/qhd,khd->hqk/dot_general | solution.py:541
  283.1 6.0 %convolution_convert_fusion.4 = bf16[2,64,1024]{2,1,0:T(8,128)(2,1)S(1)} fusion(bf16[1024,2,64]{0,2,1:T(8,128)(2,1)S(1)} %reshape.449, f32[2,1024,1024]{1,2,0:T(8,128)} %copy-done.1, f32[2,1024]{1,0:T(2,128)S(1)} %log_add_fusion, pred[1024,1024]{0,1:T(8,128)(4,1)S(1)} %copy-done.7), kind=kOutput, calls=%fused_computation.50 | convolution fusion | flops 276955136 | bytes 9969664 | tf_op jit(solution)/shard_map/hqk,qhd->khd/dot_general | solution.py:545
  289.1 1.9 fusion.20
  293.7 3.5 all-to-all-done.8
  297.2 4.2 all-to-all-start.5
  301.4 2.9 convolution_convert_fusion.2
  305.6 8.1 %all-to-all-done.5 = bf16[4,272,384]{2,1,0:T(8,128)(2,1)} async-done(((bf16[4,272,384]{2,1,0:T(8,128)(2,1)}), bf16[4,272,384]{2,1,0:T(8,128)(2,1)}, u32[]{:S(2)}, u32[]{:S(2)}) %all-to-all-start.5) | async-done | bytes 835616 | tf_op jit(solution)/shard_map/all_to_all | solution.py:397
  313.7 3.5 all-to-all-start.10
  317.2 2.2 convert_reduce_fusion.3
  319.4 26.4 %all-to-all-done.10 = bf16[4,128,1152]{2,1,0:T(8,128)(2,1)S(1)} async-done(((bf16[4,128,1152]{2,1,0:T(8,128)(2,1)}), bf16[4,128,1152]{2,1,0:T(8,128)(2,1)S(1)}, u32[]{:S(2)}, u32[]{:S(2)}) %all-to-all-start.10) | async-done | bytes 1179680 | tf_op jit(solution)/shard_map/all_to_all | solution.py:397
  345.8 3.5 all-to-all-start.9
  351.5 6.9 %all-to-all-done.9 = f32[8,32,512]{2,1,0:T(8,128)S(1)} async-done(((f32[8,32,512]{2,1,0:T(8,128)}), f32[8,32,512]{2,1,0:T(8,128)S(1)}, u32[]{:S(2)}, u32[]{:S(2)}) %all-to-all-start.9) | async-done | bytes 524320 | tf_op jit(solution)/shard_map/all_to_all | solution.py:515
  358.5 3.5 all-to-all-start.6
  362.0 3.9 convolution_convert_fusion
  365.8 9.9 %all-to-all-done.6 = f32[8,40,384]{2,1,0:T(8,128)S(1)} async-done(((f32[8,40,384]{2,1,0:T(8,128)}), f32[8,40,384]{2,1,0:T(8,128)S(1)}, u32[]{:S(2)}, u32[]{:S(2)}) %all-to-all-start.6) | async-done | bytes 491552 | tf_op jit(solution)/shard_map/all_to_all | solution.py:563
  376.6 3.8 all-to-all-start.4
  384.9 43.9 %all-to-all-done.4 = bf16[8,128,1024]{2,1,0:T(8,128)(2,1)S(1)} async-done(((bf16[8,128,1024]{2,1,0:T(8,128)(2,1)}), bf16[8,128,1024]{2,1,0:T(8,128)(2,1)S(1)}, u32[]{:S(2)}, u32[]{:S(2)}) %all-to-all-start.4) | async-done | bytes 2097184 | tf_op jit(solution)/shard_map/all_to_all | solution.py:397
  430.1 3.4 all-to-all-start.7
  444.4 44.9 %all-to-all-done.7 = bf16[32,32,1152]{2,1,0:T(8,128)(2,1)S(1)} async-done(((bf16[32,32,1152]{2,1,0:T(8,128)(2,1)}), bf16[32,32,1152]{2,1,0:T(8,128)(2,1)S(1)}, u32[]{:S(2)}, u32[]{:S(2)}) %all-to-all-start.7) | async-done | bytes 2359328 | tf_op jit(solution)/shard_map/all_to_all | solution.py:397
  (247 shorter events, 76.7 us)
Async XLA Ops:
  7.2 86.5 %copy-start.25 = (bf16[32,4096]{1,0:T(8,128)(2,1)S(1)}, bf16[32,4096]{1,0:T(8,128)(2,1)}, u32[]{:S(2)}) copy-start(bf16[32,4096]{1,0:T(8,128)(2,1)} %param.25) | copy-start | bytes 786436
  7.2 108.3 %all-gather.14.cloned.1.call-start = ((), (), s32[]{:S(2)}) async-start(), calls=%async_computation.14 | async-start | bytes 2359296 | tf_op jit(solution)/shard_map/all_gather | solution.py:457
  9.8 87.3 %all-to-all-start = ((bf16[8,32,384]{2,1,0:T(8,128)(2,1)}), bf16[8,32,384]{2,1,0:T(8,128)(2,1)S(1)}, u32[]{:S(2)}, u32[]{:S(2)}) async-start(bf16[8,32,384]{2,1,0:T(8,128)(2,1)} %all_to_all.56), calls=%async_computation | async-start | bytes 393216 | tf_op jit(solution)/shard_map/all_to_all | solution.py:455
  17.1 115.1 %all-gather.8.cloned.1.call-start = ((), (), s32[]{:S(2)}) async-start(), calls=%async_computation.11 | async-start | bytes 2162688 | tf_op jit(solution)/shard_map/all_gather | solution.py:458
  97.1 25.3 %copy-start.6 = (pred[1024,1024]{0,1:T(8,128)(4,1)}, pred[1024,1024]{0,1:T(8,128)(4,1)S(1)}, u32[]{:S(2)}) copy-start(pred[1024,1024]{0,1:T(8,128)(4,1)S(1)} %fusion.5) | copy-start | bytes 3145732
  97.2 30.6 %all-to-all-start.2 = ((bf16[8,32,512]{2,1,0:T(8,128)(2,1)}), bf16[8,32,512]{2,1,0:T(8,128)(2,1)S(1)}, u32[]{:S(2)}, u32[]{:S(2)}) async-start(bf16[8,32,512]{2,1,0:T(8,128)(2,1)} %all_to_all.60), calls=%async_computation.2 | async-start | bytes 524288 | tf_op jit(solution)/shard_map/all_to_all | solution.py:461
  123.6 17.2 %copy-start.23 = (bf16[1,128,1024]{2,1,0:T(8,128)(2,1)S(1)}, bf16[1,128,1024]{2,1,0:T(8,128)(2,1)}, u32[]{:S(2)}) copy-start(bf16[1,128,1024]{2,1,0:T(8,128)(2,1)} %param.17) | copy-start | bytes 786436
  127.7 13.1 %all-to-all-start.1 = ((bf16[8,128,128]{1,2,0:T(8,128)(2,1)}), bf16[8,128,128]{1,2,0:T(8,128)(2,1)S(1)}, u32[]{:S(2)}, u32[]{:S(2)}) async-start(bf16[8,128,128]{1,2,0:T(8,128)(2,1)} %copy.84), calls=%async_computation.1 | async-start | bytes 524288 | tf_op jit(solution)/shard_map/all_to_all | solution.py:479
  131.2 31.6 %all-gather.10.cloned.1.call-start = ((), (), s32[]{:S(2)}) async-start(), calls=%async_computation.12 | async-start | bytes 1310720 | tf_op jit(solution)/shard_map/all_gather | solution.py:462
  131.9 59.7 %all-gather.12.cloned.1.call-start = ((), (), s32[]{:S(2)}) async-start(), calls=%async_computation.13 | async-start | bytes 1310720 | tf_op jit(solution)/shard_map/all_gather | solution.py:465
  144.3 20.0 %collective-permute-start.2 = (bf16[128,1024]{1,0:T(8,128)(2,1)S(1)}, bf16[128,1024]{1,0:T(8,128)(2,1)S(1)}, u32[]{:S(2)}, u32[]{:S(2)}) collective-permute-start(bf16[128,1024]{1,0:T(8,128)(2,1)S(1)} %get-tuple-element.42), channel_id=1, source_target_pairs={{0,17},{1,16},{16,1},{17,0},{2,19},{3,18},{18,3},{19,2},{4,21},{5,... | collective-permute-start | bytes 786440 | tf_op jit(solution)/shard_map/ppermute | solution.py:371
  145.8 19.0 %collective-permute-start.1 = (bf16[128,1024]{1,0:T(8,128)(2,1)S(1)}, bf16[128,1024]{1,0:T(8,128)(2,1)S(1)}, u32[]{:S(2)}, u32[]{:S(2)}) collective-permute-start(bf16[128,1024]{1,0:T(8,128)(2,1)S(1)} %get-tuple-element.42), channel_id=1, source_target_pairs={{0,16},{1,17},{16,0},{17,1},{2,18},{3,19},{18,2},{19,3},{4,20},{5,... | collective-permute-start | bytes 786440 | tf_op jit(solution)/shard_map/ppermute | solution.py:371
  147.2 17.7 %collective-permute-start = (bf16[128,1024]{1,0:T(8,128)(2,1)S(1)}, bf16[128,1024]{1,0:T(8,128)(2,1)S(1)}, u32[]{:S(2)}, u32[]{:S(2)}) collective-permute-start(bf16[128,1024]{1,0:T(8,128)(2,1)S(1)} %get-tuple-element.42), channel_id=1, source_target_pairs={{0,1},{1,0},{16,17},{17,16},{2,3},{3,2},{18,19},{19,18},{4,5},{5,4... | collective-permute-start | bytes 786440 | tf_op jit(solution)/shard_map/ppermute | solution.py:371
  164.2 1.6 collective-permute-start.3
  164.3 2.7 collective-permute-start.6
  164.8 2.2 collective-permute-start.5
  164.9 2.1 collective-permute-start.4
  195.1 1.5 collective-permute-start.12
  195.1 1.9 collective-permute-start.10
  195.6 2.1 collective-permute-start.8
  195.7 6.9 %collective-permute-start.7 = (bf16[128,1024]{1,0:T(8,128)(2,1)}, bf16[128,1024]{1,0:T(8,128)(2,1)}, u32[]{:S(2)}, u32[]{:S(2)}) collective-permute-start(bf16[128,1024]{1,0:T(8,128)(2,1)} %get-tuple-element.56), channel_id=1, source_target_pairs={{0,8},{8,0},{1,9},{9,1},{2,10},{10,2},{3,11},{11,3},{4,12},{12,4},... | collective-permute-start | bytes 786440 | tf_op jit(solution)/shard_map/ppermute | solution.py:371
  198.8 18.6 %copy-start.12 = (bf16[1,128,1024]{2,1,0:T(8,128)(2,1)S(1)}, bf16[1,128,1024]{2,1,0:T(8,128)(2,1)}, u32[]{:S(2)}) copy-start(bf16[1,128,1024]{2,1,0:T(8,128)(2,1)} %param.33) | copy-start | bytes 786436
  198.8 9.5 %collective-permute-start.9 = (bf16[128,1024]{1,0:T(8,128)(2,1)}, bf16[128,1024]{1,0:T(8,128)(2,1)}, u32[]{:S(2)}, u32[]{:S(2)}) collective-permute-start(bf16[128,1024]{1,0:T(8,128)(2,1)} %get-tuple-element.49), channel_id=1, source_target_pairs={{0,1},{1,0},{16,17},{17,16},{2,3},{3,2},{18,19},{19,18},{4,5},{5,4... | collective-permute-start | bytes 786440 | tf_op jit(solution)/shard_map/ppermute | solution.py:371
  200.3 13.8 %collective-permute-start.13 = (bf16[128,1024]{1,0:T(8,128)(2,1)}, bf16[128,1024]{1,0:T(8,128)(2,1)}, u32[]{:S(2)}, u32[]{:S(2)}) collective-permute-start(bf16[128,1024]{1,0:T(8,128)(2,1)} %get-tuple-element.50), channel_id=1, source_target_pairs={{0,17},{1,16},{16,1},{17,0},{2,19},{3,18},{18,3},{19,2},{4,21},{5,... | collective-permute-start | bytes 786440 | tf_op jit(solution)/shard_map/ppermute | solution.py:371
  201.7 13.7 %collective-permute-start.11 = (bf16[128,1024]{1,0:T(8,128)(2,1)}, bf16[128,1024]{1,0:T(8,128)(2,1)}, u32[]{:S(2)}, u32[]{:S(2)}) collective-permute-start(bf16[128,1024]{1,0:T(8,128)(2,1)} %get-tuple-element.51), channel_id=1, source_target_pairs={{0,16},{1,17},{16,0},{17,1},{2,18},{3,19},{18,2},{19,3},{4,20},{5,... | collective-permute-start | bytes 786440 | tf_op jit(solution)/shard_map/ppermute | solution.py:371
  218.8 9.9 %collective-permute-start.16 = (bf16[128,1024]{1,0:T(8,128)(2,1)S(1)}, bf16[128,1024]{1,0:T(8,128)(2,1)S(1)}, u32[]{:S(2)}, u32[]{:S(2)}) collective-permute-start(bf16[128,1024]{1,0:T(8,128)(2,1)S(1)} %get-tuple-element.29), channel_id=1, source_target_pairs={{0,17},{1,16},{16,1},{17,0},{2,19},{3,18},{18,3},{19,2},{4,21},{5,... | collective-permute-start | bytes 786440 | tf_op jit(solution)/shard_map/ppermute | solution.py:371
  220.4 11.2 %collective-permute-start.15 = (bf16[128,1024]{1,0:T(8,128)(2,1)S(1)}, bf16[128,1024]{1,0:T(8,128)(2,1)S(1)}, u32[]{:S(2)}, u32[]{:S(2)}) collective-permute-start(bf16[128,1024]{1,0:T(8,128)(2,1)S(1)} %get-tuple-element.29), channel_id=1, source_target_pairs={{0,16},{1,17},{16,0},{17,1},{2,18},{3,19},{18,2},{19,3},{4,20},{5,... | collective-permute-start | bytes 786440 | tf_op jit(solution)/shard_map/ppermute | solution.py:371
  221.9 9.7 %collective-permute-start.14 = (bf16[128,1024]{1,0:T(8,128)(2,1)S(1)}, bf16[128,1024]{1,0:T(8,128)(2,1)S(1)}, u32[]{:S(2)}, u32[]{:S(2)}) collective-permute-start(bf16[128,1024]{1,0:T(8,128)(2,1)S(1)} %get-tuple-element.29), channel_id=1, source_target_pairs={{0,1},{1,0},{16,17},{17,16},{2,3},{3,2},{18,19},{19,18},{4,5},{5,4... | collective-permute-start | bytes 786440 | tf_op jit(solution)/shard_map/ppermute | solution.py:371
  222.4 9.7 %collective-permute-start.17 = (bf16[128,1024]{1,0:T(8,128)(2,1)S(1)}, bf16[128,1024]{1,0:T(8,128)(2,1)S(1)}, u32[]{:S(2)}, u32[]{:S(2)}) collective-permute-start(bf16[128,1024]{1,0:T(8,128)(2,1)S(1)} %get-tuple-element.29), channel_id=1, source_target_pairs={{0,8},{8,0},{1,9},{9,1},{2,10},{10,2},{3,11},{11,3},{4,12},{12,4},... | collective-permute-start | bytes 786440 | tf_op jit(solution)/shard_map/ppermute | solution.py:371
  228.8 4.7 collective-permute-start.20
  231.5 1.9 collective-permute-start.19
  231.5 1.9 collective-permute-start.18
  237.0 1.6 collective-permute-start.26
  237.2 1.8 collective-permute-start.24
  237.6 1.8 collective-permute-start.22
  237.7 5.5 %collective-permute-start.21 = (bf16[128,1024]{1,0:T(8,128)(2,1)S(1)}, bf16[128,1024]{1,0:T(8,128)(2,1)S(1)}, u32[]{:S(2)}, u32[]{:S(2)}) collective-permute-start(bf16[128,1024]{1,0:T(8,128)(2,1)S(1)} %get-tuple-element.52), channel_id=1, source_target_pairs={{0,8},{8,0},{1,9},{9,1},{2,10},{10,2},{3,11},{11,3},{4,12},{12,4},... | collective-permute-start | bytes 786440 | tf_op jit(solution)/shard_map/ppermute | solution.py:371
  239.6 9.2 %collective-permute-start.23 = (bf16[128,1024]{1,0:T(8,128)(2,1)S(1)}, bf16[128,1024]{1,0:T(8,128)(2,1)S(1)}, u32[]{:S(2)}, u32[]{:S(2)}) collective-permute-start(bf16[128,1024]{1,0:T(8,128)(2,1)S(1)} %get-tuple-element.46), channel_id=1, source_target_pairs={{0,1},{1,0},{16,17},{17,16},{2,3},{3,2},{18,19},{19,18},{4,5},{5,4... | collective-permute-start | bytes 786440 | tf_op jit(solution)/shard_map/ppermute | solution.py:371
  240.5 13.2 %collective-permute-start.27 = (bf16[128,1024]{1,0:T(8,128)(2,1)S(1)}, bf16[128,1024]{1,0:T(8,128)(2,1)S(1)}, u32[]{:S(2)}, u32[]{:S(2)}) collective-permute-start(bf16[128,1024]{1,0:T(8,128)(2,1)S(1)} %get-tuple-element.47), channel_id=1, source_target_pairs={{0,17},{1,16},{16,1},{17,0},{2,19},{3,18},{18,3},{19,2},{4,21},{5,... | collective-permute-start | bytes 786440 | tf_op jit(solution)/shard_map/ppermute | solution.py:371
  241.7 13.4 %collective-permute-start.25 = (bf16[128,1024]{1,0:T(8,128)(2,1)S(1)}, bf16[128,1024]{1,0:T(8,128)(2,1)S(1)}, u32[]{:S(2)}, u32[]{:S(2)}) collective-permute-start(bf16[128,1024]{1,0:T(8,128)(2,1)S(1)} %get-tuple-element.48), channel_id=1, source_target_pairs={{0,16},{1,17},{16,0},{17,1},{2,18},{3,19},{18,2},{19,3},{4,20},{5,... | collective-permute-start | bytes 786440 | tf_op jit(solution)/shard_map/ppermute | solution.py:371
  257.7 12.3 %all-to-all-start.3 = ((bf16[8,128,128]{1,2,0:T(8,128)(2,1)}), bf16[8,128,128]{1,2,0:T(8,128)(2,1)S(1)}, u32[]{:S(2)}, u32[]{:S(2)}) async-start(bf16[8,128,128]{1,2,0:T(8,128)(2,1)} %bitcast.23), calls=%async_computation.3 | async-start | bytes 524288 | tf_op jit(solution)/shard_map/all_to_all | solution.py:525
  270.0 27.2 %all-to-all-start.8 = ((bf16[4,256,512]{2,1,0:T(8,128)(2,1)}), bf16[4,256,512]{2,1,0:T(8,128)(2,1)}, u32[]{:S(2)}, u32[]{:S(2)}) async-start(bf16[4,256,512]{2,1,0:T(8,128)(2,1)} %bitcast.141), calls=%async_computation.8 | async-start | bytes 2097152 | tf_op jit(solution)/shard_map/all_to_all | solution.py:397
  297.2 16.5 %all-to-all-start.5 = ((bf16[4,272,384]{2,1,0:T(8,128)(2,1)}), bf16[4,272,384]{2,1,0:T(8,128)(2,1)}, u32[]{:S(2)}, u32[]{:S(2)}) async-start(bf16[4,272,384]{2,1,0:T(8,128)(2,1)} %pad_maximum_fusion.2), calls=%async_computation.5 | async-start | bytes 1671168 | tf_op jit(solution)/shard_map/all_to_all | solution.py:397
  313.7 32.1 %all-to-all-start.10 = ((bf16[4,128,1152]{2,1,0:T(8,128)(2,1)}), bf16[4,128,1152]{2,1,0:T(8,128)(2,1)S(1)}, u32[]{:S(2)}, u32[]{:S(2)}) async-start(bf16[4,128,1152]{2,1,0:T(8,128)(2,1)} %pad_maximum_fusion.1), calls=%async_computation.10 | async-start | bytes 2359296 | tf_op jit(solution)/shard_map/all_to_all | solution.py:397
  345.8 30.8 %copy-start.5 = (bf16[4,128,1152]{2,1,0:T(8,128)(2,1)}, bf16[4,128,1152]{2,1,0:T(8,128)(2,1)S(1)}, u32[]{:S(2)}) copy-start(bf16[4,128,1152]{2,1,0:T(8,128)(2,1)S(1)} %all-to-all-done.10) | copy-start | bytes 3538948
  345.8 12.7 %all-to-all-start.9 = ((f32[8,32,512]{2,1,0:T(8,128)}), f32[8,32,512]{2,1,0:T(8,128)S(1)}, u32[]{:S(2)}, u32[]{:S(2)}) async-start(f32[8,32,512]{2,1,0:T(8,128)} %bitcast.51), calls=%async_computation.9 | async-start | bytes 1048576 | tf_op jit(solution)/shard_map/all_to_all | solution.py:515
  358.5 17.3 %all-to-all-start.6 = ((f32[8,40,384]{2,1,0:T(8,128)}), f32[8,40,384]{2,1,0:T(8,128)S(1)}, u32[]{:S(2)}, u32[]{:S(2)}) async-start(f32[8,40,384]{2,1,0:T(8,128)} %pad_maximum_fusion.4), calls=%async_computation.6 | async-start | bytes 983040 | tf_op jit(solution)/shard_map/all_to_all | solution.py:563
  376.6 52.2 %all-to-all-start.4 = ((bf16[8,128,1024]{2,1,0:T(8,128)(2,1)}), bf16[8,128,1024]{2,1,0:T(8,128)(2,1)S(1)}, u32[]{:S(2)}, u32[]{:S(2)}) async-start(bf16[8,128,1024]{2,1,0:T(8,128)(2,1)} %bitcast.153), calls=%async_computation.4 | async-start | bytes 4194304 | tf_op jit(solution)/shard_map/all_to_all | solution.py:397
  430.1 59.1 %all-to-all-start.7 = ((bf16[32,32,1152]{2,1,0:T(8,128)(2,1)}), bf16[32,32,1152]{2,1,0:T(8,128)(2,1)S(1)}, u32[]{:S(2)}, u32[]{:S(2)}) async-start(bf16[32,32,1152]{2,1,0:T(8,128)(2,1)} %pad_maximum_fusion), calls=%async_computation.7 | async-start | bytes 4718592 | tf_op jit(solution)/shard_map/all_to_all | solution.py:397
  (28 other events, 167.3 us)
Sparse Core Ops, SparseCore 0:
  10.1 52.4 all-gather.13
  65.6 56.3 all-gather.7
  134.1 28.5 all-gather.9
  164.2 27.4 all-gather.11

commit v2 on v0

--- a/solution.py
+++ b/solution.py
@@ -3,6 +3,9 @@
 import jax
 import jax.numpy as jnp
 from jax import lax
+from jax.experimental import pallas as pl
+from jax.experimental.pallas import tpu as pltpu
+from jax.sharding import Mesh
 from jax.sharding import PartitionSpec as P
 
 HEADS = 16
@@ -165,7 +168,7 @@
     return (summed[:, :width], summed[:, width:])
 
 
-def body(
+def general_body(
     tokens,
     w_qkv,
     b_query,
@@ -363,7 +366,605 @@
     )
 
 
-def solution(mesh):
+GROUP = ("y", "core", "x")
+CTX = ("z", "x")
+DP = ("y", "core")
+EVERY = ("y", "core", "z", "x")
+bf16, f32 = jnp.bfloat16, jnp.float32
+
+
+def swap(member, axes, code):
+    count = 1
+    for axis in axes:
+        count *= lax.axis_size(axis)
+    return lax.ppermute(member, axes, [(place, place ^ code) for place in range(count)])
+
+
+def like(shape, kind):
+    return jax.ShapeDtypeStruct(shape, kind)
+
+
+def local(kernel, outs, place, *operands, scratch=(), flops=0):
+    whole = pl.BlockSpec(memory_space=pltpu.VMEM)
+    moved = sum(v.size * v.dtype.itemsize for v in operands)
+    moved += sum(o.size * jnp.dtype(o.dtype).itemsize for o in outs)
+    return pl.pallas_call(
+        kernel,
+        out_shape=list(outs),
+        in_specs=[pl.BlockSpec(memory_space=pltpu.SMEM)] + [whole] * len(operands),
+        out_specs=[whole] * len(outs),
+        scratch_shapes=list(scratch),
+        cost_estimate=pl.CostEstimate(flops=flops, bytes_accessed=moved, transcendentals=0),
+        compiler_params=pltpu.CompilerParams(vmem_limit_bytes=48 << 20),
+    )(place, *operands)
+
+
+def pair_product(left, right):
+    return lax.dot_general(
+        left, right, (((0,), (0,)), ((), ())), preferred_element_type=jnp.float32
+    )
+
+
+def plane_gather(block):
+    return [block] + [swap(block, ("y", "x"), code) for code in range(1, 4)]
+
+
+def group_gather(block):
+    plane = plane_gather(block)
+    return plane + [swap(member, ("core",), 1) for member in plane]
+
+
+def merge_kernel(place, near, far, own, *sent):
+    rows = own.shape[0]
+    for code in range(4):
+        part = pl.ds(code * rows, rows)
+        total = near[part, :].astype(f32) + far[part, :].astype(f32)
+        if code == 0:
+            own[...] = total
+        else:
+            sent[code - 1][...] = total.astype(bf16)
+
+
+def group_scatter(near, far, place):
+    rows, width = near.shape[0] // 4, near.shape[1]
+    crossed = swap(far, ("core",), 1)
+    outs = [like((rows, width), f32)] + [like((rows, width), bf16)] * 3
+    own, *sent = local(merge_kernel, outs, place, near, crossed)
+    return [own] + [swap(sent[code - 1], ("y", "x"), code) for code in range(1, 4)]
+
+
+def sum_over_z(parts):
+    total = parts[0].astype(f32)
+    for code in range(1, 4):
+        total = total + swap(parts[code], ("z",), code).astype(f32)
+    return total
+
+
+def ctx_gather(block):
+    line = [block] + [swap(block, ("z",), code) for code in range(1, 4)]
+    return [piece for member in line for piece in (member, swap(member, ("x",), 1))]
+
+
+def out_gather(block):
+    line = jnp.stack([block] + [swap(block, ("z",), code) for code in range(1, 4)])
+    both = [line, swap(line, ("y",), 1)]
+    both = jnp.stack(both)
+    far = swap(both, ("x",), 1)
+    return [both, far, swap(both, ("core",), 1), swap(far, ("core",), 1)]
+
+
+def order_kernel(place, p00, p01, p10, p11, up_ref, out_ref, up_out):
+    rows = p00.shape[2]
+    own = place[0]
+    for core in range(2):
+        for x in range(2):
+            piece = ((p00, p01), (p10, p11))[core][x]
+            for y in range(2):
+                for z in range(4):
+                    at = own ^ (y * 16 + core * 8 + z * 2 + x)
+                    out_ref[pl.ds(at * rows, rows), :] = piece[y, z]
+    for y in range(2):
+        for core in range(2):
+            for z in range(4):
+                for x in range(2):
+                    at = y * 16 + core * 8 + z * 2 + x
+                    block = up_ref[pl.ds((z * 8 + y * 4 + core * 2 + x) * rows, rows), :]
+                    up_out[pl.ds(at * rows, rows), :] = block
+
+
+def allowed_here(query_tags, query_place, key_tags, key_place):
+    same_doc = (query_tags >> 1) == (key_tags >> 1)
+    distance = jnp.abs(query_place - key_place)
+    usable = ((key_tags & 1) == 1) | (distance == 0)
+    return same_doc & (distance <= WINDOW // 2) & usable
+
+
+def places(own_ctx, rows, shape, axis, start=0):
+    index = lax.broadcasted_iota(jnp.int32, shape, axis) + start
+    return ((index // rows) ^ own_ctx) * rows + index % rows
+
+
+def attend_kernel(
+    place, *refs, n_blocks, rows, cols
+):
+    blocks, refs = refs[:n_blocks], refs[n_blocks:]
+    pieces, refs = refs[:4], refs[4:]
+    bias, tags_col, tags_row, q_ref, k_ref, v_ref, att_ref, msg_ref, lse_ref, qkv_ref = refs[:10]
+    own_dp, own_ctx = place[1], place[2]
+    shard = 32
+    for m, piece in enumerate(pieces):
+        for c in range(n_blocks):
+            at = ((own_dp ^ m) * n_blocks + c) * shard
+            qkv_ref[pl.ds(at, shard), :] = piece[c, :shard, :]
+    for j, block in enumerate(blocks):
+        part = pl.ds(j * rows, rows)
+        mixed = matmul(block[...], qkv_ref[...]) + bias[...]
+        q_ref[part, :] = mixed[:, :cols].astype(bf16)
+        k_ref[part, :] = mixed[:, cols : 2 * cols].astype(bf16)
+        v_ref[part, :] = mixed[:, 2 * cols :].astype(bf16)
+    length = n_blocks * rows
+    chunk = 2 * rows
+
+    def step(index, carry):
+        part = pl.ds(index * chunk, chunk)
+        allowed = allowed_here(
+            tags_col[part, :],
+            places(own_ctx, rows, (chunk, 1), 0, index * chunk),
+            tags_row[...],
+            places(own_ctx, rows, (1, length), 1),
+        )
+        found = []
+        for head in range(cols // HEAD):
+            lanes = slice(head * HEAD, (head + 1) * HEAD)
+            scores = cols_product(q_ref[part, lanes], k_ref[:, lanes]) * 0.125
+            scores = jnp.where(allowed, scores, MASKED)
+            top = jnp.max(scores, axis=1, keepdims=True)
+            weights = jnp.exp(scores - top)
+            mass = jnp.sum(weights, axis=1, keepdims=True)
+            found.append(matmul(weights.astype(bf16), v_ref[:, lanes]) / mass)
+            total = top + jnp.log(mass)
+            lse_ref[pl.ds(head, 1), part] = jnp.broadcast_to(total, (chunk, 128)).T[:1, :]
+        attended = jnp.concatenate(found, axis=1)
+        att_ref[part, :] = attended
+        for half in range(2):
+            at = ((index * 2 + half) ^ own_ctx) * rows
+            msg_ref[pl.ds(at, rows), :] = attended[half * rows : (half + 1) * rows].astype(bf16)
+        return carry
+
+    lax.fori_loop(0, length // chunk, step, 0)
+
+
+def branch_kernel(place, moved, w_out, inputs, vectors, normed_ref, low_ref, hat_ref, rate_ref):
+    groups, rows, cols = moved.shape
+    total = inputs[...].astype(f32) + vectors[2:3, :]
+    for c in range(groups):
+        total = total + matmul(moved[c], w_out[pl.ds(c * cols, cols), :])
+    centred = total - jnp.mean(total, axis=1, keepdims=True)
+    rate = lax.rsqrt(jnp.mean(centred * centred, axis=1, keepdims=True) + EPSILON)
+    hat = centred * rate
+    normed = hat * vectors[3:4, :] + vectors[4:5, :]
+    normed_ref[...] = normed
+    low_ref[...] = normed.astype(bf16)
+    hat_ref[...] = hat
+    rate_ref[...] = jnp.broadcast_to(rate, rate_ref.shape)
+
+
+def forward_kernel(place, *refs):
+    blocks = refs[:8]
+    up, bias, down, hidden_ref, active_ref, near, far = refs[8:]
+    rows = blocks[0].shape[0]
+    for pair in range(4):
+        lines = jnp.concatenate([blocks[2 * pair][...], blocks[2 * pair + 1][...]], axis=0)
+        part = pl.ds(pair * 2 * rows, 2 * rows)
+        hidden = matmul(lines, up[...]) + bias[...]
+        hidden_ref[part, :] = hidden
+        active = (0.5 * hidden * (1 + lax.erf(hidden * 0.7071067811865476))).astype(bf16)
+        active_ref[part, :] = active
+        target = near if pair < 2 else far
+        target[pl.ds(pair % 2 * 2 * rows, 2 * rows), :] = matmul(active, down[...]).astype(bf16)
+
+
+def second_kernel(
+    place, normed, own, p1, p2, p3, vectors, cotangent, result_ref, grad_ref, low_ref, sums_ref
+):
+    second = normed[...] + own[...] + p1[...].astype(f32) + p2[...].astype(f32)
+    second = second + p3[...].astype(f32) + vectors[5:6, :]
+    centred = second - jnp.mean(second, axis=1, keepdims=True)
+    rate = lax.rsqrt(jnp.mean(centred * centred, axis=1, keepdims=True) + EPSILON)
+    hat = centred * rate
+    gain = vectors[6:7, :]
+    result_ref[...] = (hat * gain + vectors[7:8, :]).astype(bf16)
+    grad = cotangent[...].astype(f32)
+    scaled = grad * gain
+    mean_scaled = jnp.mean(scaled, axis=1, keepdims=True)
+    mean_hat = jnp.mean(scaled * hat, axis=1, keepdims=True)
+    grad_second = rate * (scaled - mean_scaled - hat * mean_hat)
+    grad_ref[...] = grad_second
+    low = grad_second.astype(bf16)
+    low_ref[...] = low
+    sums_ref[0:1, :] = jnp.sum(low.astype(f32), axis=0, keepdims=True)
+    sums_ref[1:2, :] = jnp.sum(grad * hat, axis=0, keepdims=True)
+    sums_ref[2:3, :] = jnp.sum(grad, axis=0, keepdims=True)
+
+
+def backward_kernel(place, *refs):
+    blocks = refs[:8]
+    up, down, slope, grad_ref, near, far = refs[8:]
+    rows = blocks[0].shape[0]
+    for pair in range(4):
+        lines = jnp.concatenate([blocks[2 * pair][...], blocks[2 * pair + 1][...]], axis=0)
+        part = pl.ds(pair * 2 * rows, 2 * rows)
+        grad = (slope[part, :] * cols_product(lines, down[...])).astype(bf16)
+        grad_ref[part, :] = grad
+        target = near if pair < 2 else far
+        target[pl.ds(pair % 2 * 2 * rows, 2 * rows), :] = cols_product(grad, up[...]).astype(bf16)
+
+
+def ff_grads_kernel(place, *refs):
+    grads, normed = refs[:8], refs[8:16]
+    active, grad_hidden, down_ref, up_ref, lines, sums = refs[16:]
+    own_z = place[3]
+    rows, width = grads[0].shape
+    units = active.shape[1]
+    shard = units // 4
+    for j in range(8):
+        lines[pl.ds(j * rows, rows), :] = grads[j][...]
+    total = jnp.sum(grad_hidden[...].astype(f32), axis=0, keepdims=True)
+    for z in range(4):
+        at = own_z ^ z
+        part = slice(z * shard, (z + 1) * shard)
+        down_ref[at, :shard, :] = pair_product(active[:, part], lines[...]).astype(bf16)
+        down_ref[at, shard:, :shard] = jnp.broadcast_to(total[:, part], (16, shard)).astype(bf16)
+        down_ref[at, shard:, shard:] = jnp.zeros((16, width - shard), bf16)
+    for j in range(8):
+        lines[pl.ds(j * rows, rows), :] = normed[j][...]
+    for quarter in range(4):
+        span = 8 * 32
+        part = slice(quarter * span, (quarter + 1) * span)
+        found = pair_product(lines[:, part], grad_hidden[...]).astype(bf16)
+        for z in range(4):
+            for x in range(2):
+                piece = found[(z * 2 + x) * 32 : (z * 2 + x + 1) * 32]
+                up_ref[own_z ^ z, pl.ds((quarter * 2 + x) * 32, 32), :] = piece
+
+
+def first_kernel(
+    place, grad_second, own, p1, p2, p3, vectors, hat_ref, rate_ref, w_out, grad_ref, low_ref, msg_ref,
+    sums_ref,
+):
+    grad = grad_second[...] + own[...] + p1[...].astype(f32) + p2[...].astype(f32)
+    grad = grad + p3[...].astype(f32)
+    hat = hat_ref[...]
+    scaled = grad * vectors[3:4, :]
+    mean_scaled = jnp.mean(scaled, axis=1, keepdims=True)
+    mean_hat = jnp.mean(scaled * hat, axis=1, keepdims=True)
+    grad_first = rate_ref[:, :1] * (scaled - mean_scaled - hat * mean_hat)
+    grad_ref[...] = grad_first
+    low = grad_first.astype(bf16)
+    low_ref[...] = low
+    groups, rows, cols = msg_ref.shape
+    for c in range(groups):
+        msg_ref[c] = cols_product(low, w_out[pl.ds(c * cols, cols), :]).astype(bf16)
+    sums_ref[0:1, :] = jnp.sum(low.astype(f32), axis=0, keepdims=True)
+    sums_ref[1:2, :] = jnp.sum(grad * hat, axis=0, keepdims=True)
+    sums_ref[2:3, :] = jnp.sum(grad, axis=0, keepdims=True)
+
+
+def out_grad_kernel(place, moved, low, near, far, parts):
+    groups, rows, cols = moved.shape
+    own_y, own_core, own_x = place[4], place[5], place[6]
+    for c in range(groups):
+        found = pair_product(moved[c], low[...]).astype(bf16)
+        for m in range(4):
+            y, core, z, x = c // 4, c // 2 % 2, c % 2 * 2 + m // 2, m % 2
+            code = (core ^ own_core) * 4 + (y ^ own_y) * 2 + (x ^ own_x)
+            parts[code, pl.ds(z * 32, 32), :] = found[m * 32 : (m + 1) * 32]
+    for code in range(4):
+        near[pl.ds(code * rows, rows), :] = parts[code]
+        far[pl.ds(code * rows, rows), :] = parts[code + 4]
+
+
+def attend_grad_kernel(
+    place, moved, q_ref, k_ref, v_ref, att_ref, lse_ref, tags_col, tags_row, qkv_ref,
+    mixed_ref, sums_ref, m0, m1, m2, m3, m4, m5, m6, m7, key_grad, value_grad, back,
+):
+    messages = (m0, m1, m2, m3, m4, m5, m6, m7)
+    groups, rows, cols = moved.shape
+    length = groups * rows
+    own_ctx = place[2]
+    for j in range(groups):
+        back[pl.ds(j * rows, rows), :] = moved[own_ctx ^ j]
+    key_grad[...] = jnp.zeros(key_grad.shape, f32)
+    value_grad[...] = jnp.zeros(value_grad.shape, f32)
+    chunk = 2 * rows
+
+    def step(index, carry):
+        part = pl.ds(index * chunk, chunk)
+        allowed = allowed_here(
+            tags_row[:, part],
+            places(own_ctx, rows, (1, chunk), 1, index * chunk),
+            tags_col[...],
+            places(own_ctx, rows, (length, 1), 0),
+        )
+        weighted = (back[part, :].astype(f32) * att_ref[part, :]).T
+        found = []
+        for head in range(cols // HEAD):
+            lanes = slice(head * HEAD, (head + 1) * HEAD)
+            delta = jnp.sum(weighted[lanes, :], axis=0, keepdims=True)
+            scores = cols_product(k_ref[:, lanes], q_ref[part, lanes]) * 0.125
+            probs = jnp.where(allowed, jnp.exp(scores - lse_ref[pl.ds(head, 1), part]), 0.0)
+            grads = cols_product(v_ref[:, lanes], back[part, lanes])
+            grads = (probs * (grads - delta)).astype(bf16)
+            value_grad[:, lanes] += matmul(probs.astype(bf16), back[part, lanes])
+            key_grad[:, lanes] += matmul(grads, q_ref[part, lanes])
+            found.append(pair_product(grads, k_ref[:, lanes]) * 0.125)
+        mixed_ref[part, :cols] = jnp.concatenate(found, axis=1).astype(bf16)
+        return carry
+
+    lax.fori_loop(0, length // chunk, step, 0)
+    mixed_ref[:, cols : 2 * cols] = (key_grad[...] * 0.125).astype(bf16)
+    mixed_ref[:, 2 * cols :] = value_grad[...].astype(bf16)
+    sums_ref[...] = jnp.sum(mixed_ref[...].astype(f32), axis=0, keepdims=True)
+    for j in range(groups):
+        part = cols_product(mixed_ref[pl.ds(j * rows, rows), :], qkv_ref[...])
+        messages[j][...] = part.astype(messages[j].dtype)
+
+
+def qkv_grad_kernel(place, *refs):
+    blocks = refs[:8]
+    mixed, sums, near, far, lines = refs[8:]
+    own_dp = place[1]
+    rows = blocks[0].shape[0]
+    for j in range(8):
+        lines[pl.ds(j * rows, rows), :] = blocks[j][...]
+    span = lines.shape[1] // 4
+    for ky in range(2):
+        for kc in range(2):
+            start = pl.multiple_of((own_dp ^ (ky * 2 + kc)) * span, span)
+            found = pair_product(lines[:, pl.ds(start, span)], mixed[...]).astype(bf16)
+            target = far if kc else near
+            target[ky, :span, :] = found
+            target[ky, span:, :] = jnp.broadcast_to(sums[...], (16, mixed.shape[1])).astype(bf16)
+
+
+def dp_sum(near, far):
+    crossed = swap(far, ("core",), 1).astype(f32)
+    total = near.astype(f32) + crossed
+    return total[0] + swap(total[1].astype(bf16), ("y",), 1).astype(f32)
+
+
+def ctx_sum(parts):
+    line = [None] * 4
+    for code in (3, 2, 1, 0):
+        crossed = swap(parts[2 * code + 1], ("x",), 1)
+        line[code] = parts[2 * code].astype(f32) + crossed.astype(f32)
+        if code:
+            line[code] = swap(line[code].astype(bf16), ("z",), code).astype(f32)
+    return line[0] + line[1] + line[2] + line[3]
+
+
+def up_final_kernel(place, moved, out):
+    groups, shard, wide = moved.shape
+    units = wide // 4
+    for g in range(groups):
+        for z in range(4):
+            at = ((g // 2 * 4 + z) * 2 + g % 2) * units
+            out[:, at : at + units] = moved[g, :, z * units : (z + 1) * units].astype(f32)
+
+
+def qkv_final_kernel(place, moved, out):
+    groups, _, wide = moved.shape
+    shard, cols = out.shape[0], wide // 3
+    for c in range(groups):
+        for kind in range(3):
+            at = (kind * groups + c) * cols
+            out[:, at : at + cols] = moved[c, :shard, kind * cols : (kind + 1) * cols].astype(f32)
+
+
+def heads_body(
+    tokens, w_qkv, b_query, b_value, w_out, b_out, ln1_gain, ln1_bias, w_up, b_up, w_down, b_down,
+    ln2_gain, ln2_bias, segment_ids, pad_mask, cotangent,
+):
+    inputs = tokens[0]
+    rows, width = inputs.shape
+    n_ctx = lax.axis_size(CTX)
+    n_dp = lax.axis_size(DP)
+    n_z = lax.axis_size("z")
+    length = rows * n_ctx
+    cols = width // n_ctx
+    shard = w_qkv.shape[0]
+    units = w_down.shape[0]
+    wide = n_z * units
+    own_ctx = lax.axis_index(CTX)
+    own_dp = lax.axis_index(DP)
+    own = lax.axis_index(EVERY)
+    place = jnp.stack(
+        [own, own_dp, own_ctx, lax.axis_index("z")] + [lax.axis_index(a) for a in GROUP]
+    ).astype(jnp.int32)
+
+    blocks = ctx_gather(inputs)
+    tags_here = (2 * (segment_ids[0] + 1) + pad_mask[0]).astype(bf16)
+    packed = jnp.concatenate(
+        [b_query, b_value, b_out, ln1_gain, ln1_bias, b_down, ln2_gain, ln2_bias, b_up, tags_here]
+    )
+    packed = jnp.pad(packed, (0, 6 * cols - packed.size)).reshape(2, 3 * cols)
+    qkv = w_qkv.reshape(shard, 3, n_ctx, cols).transpose(2, 0, 1, 3).reshape(n_ctx, shard, 3 * cols)
+    packed = jnp.broadcast_to(jnp.pad(packed, ((0, 14), (0, 0))), (n_ctx, 16, 3 * cols))
+    qkv = jnp.concatenate([qkv, packed], axis=1)
+    qkv = lax.all_to_all(qkv, CTX, 0, 0, tiled=True)
+    qkv_y = swap(qkv, ("y",), 1)
+    pieces = [qkv, swap(qkv, ("core",), 1), qkv_y, swap(qkv_y, ("core",), 1)]
+    small = jnp.stack([piece[:, shard : shard + 2] for piece in pieces])
+    small = jnp.take(small, own_dp ^ jnp.arange(n_dp), axis=0).reshape(n_dp * n_ctx, 6 * cols)
+    vectors = small[:, : 8 * shard].reshape(-1, 8, shard).transpose(1, 0, 2).reshape(8, width)
+    vectors = vectors.astype(f32)
+    at = 8 * shard
+    bias_up = small[:, at : at + units].reshape(n_dp, n_z, 2, units)
+    bias_up = lax.dynamic_slice(bias_up, (own_dp, 0, lax.axis_index("x"), 0), (1, n_z, 1, units))
+    bias_up = bias_up.reshape(1, wide).astype(f32)
+    at += units
+    tags = small[:, at : at + rows].reshape(n_dp, n_ctx, rows)
+    tags = lax.dynamic_slice(tags, (own_dp, 0, 0), (1, n_ctx, rows))[0].astype(jnp.int32)
+    tags = jnp.take(tags, own_ctx ^ jnp.arange(n_ctx), axis=0)
+    tags_row, tags_col = tags.reshape(1, length), tags.reshape(length, 1)
+    bias = lax.dynamic_slice(vectors, (0, own_ctx * cols), (2, cols))
+    bias = jnp.concatenate([bias[:1], jnp.zeros((1, cols), f32), bias[1:]], axis=1)
+
+    up = w_up.reshape(shard, 2, 2, n_z, 2, units).transpose(1, 2, 4, 0, 3, 5)
+    up = lax.all_to_all(up.reshape(8 * shard, wide), GROUP, 0, 0, tiled=True)
+    up = lax.all_gather(up, "z", axis=0, tiled=True)
+    down = lax.all_gather(w_down, "z", axis=0, tiled=True)
+    full_out, full_up = local(
+        order_kernel, [like((width, width), bf16), like((width, wide), bf16)], place,
+        *out_gather(w_out), up,
+    )
+
+    queries, keys, values, attended, message, totals, full_qkv = local(
+        partial(attend_kernel, n_blocks=n_ctx, rows=rows, cols=cols),
+        [like((length, cols), bf16)] * 3
+        + [
+            like((length, cols), f32),
+            like((length, cols), bf16),
+            like((8, length), f32),
+            like((width, 3 * cols), bf16),
+        ],
+        place, *blocks, *pieces, bias, tags_col, tags_row,
+        flops=8 * length * length * cols,
+    )
+    moved = lax.all_to_all(message, CTX, 0, 0, tiled=True).reshape(n_ctx, rows, cols)
+    normed, normed_low, hat, rate = local(
+        branch_kernel,
+        [like((rows, width), f32), like((rows, width), bf16), like((rows, width), f32)]
+        + [like((rows, 128), f32)],
+        place, moved, full_out, inputs, vectors, flops=2 * rows * width * width,
+    )
+    normed_all = group_gather(normed_low)
+    hidden, active, near, far = local(
+        forward_kernel,
+        [like((8 * rows, wide), f32), like((8 * rows, wide), bf16)]
+        + [like((4 * rows, width), bf16)] * 2,
+        place, *normed_all, full_up, bias_up, down, flops=32 * rows * width * wide,
+    )
+    parts = group_scatter(near, far, place)
+    result, grad_second, grad_z, sums_two = local(
+        second_kernel,
+        [like((rows, width), bf16), like((rows, width), f32), like((rows, width), bf16)]
+        + [like((8, width), f32)],
+        place, normed, *parts, vectors, cotangent[0],
+    )
+
+    slope = 0.5 * (1 + lax.erf(hidden * 0.7071067811865476)) + hidden * (
+        jnp.exp(-0.5 * hidden * hidden) * 0.3989422804014327
+    )
+    grad_z_all = group_gather(grad_z)
+    grad_hidden, near, far = local(
+        backward_kernel,
+        [like((8 * rows, wide), bf16)] + [like((4 * rows, width), bf16)] * 2,
+        place, *grad_z_all, full_up, down, slope, flops=32 * rows * width * wide,
+    )
+    parts = group_scatter(near, far, place)
+    grad_first, grad_branch, message, sums_one = local(
+        first_kernel,
+        [like((rows, width), f32), like((rows, width), bf16), like((n_ctx, rows, cols), bf16)]
+        + [like((8, width), f32)],
+        place, grad_second, *parts, vectors, hat, rate, full_out, flops=2 * rows * width * width,
+    )
+    grad_moved = lax.all_to_all(message, CTX, 0, 0, tiled=True)
+    down_parts, up_parts = local(
+        ff_grads_kernel,
+        [like((n_z, units + 16, width), bf16), like((n_z, 8 * shard, wide), bf16)],
+        place, *grad_z_all, *normed_all, active, grad_hidden,
+        scratch=[pltpu.VMEM((8 * rows, width), bf16), pltpu.VMEM((8, 128), f32)],
+        flops=32 * rows * width * wide,
+    )
+    down_sum = sum_over_z(list(down_parts))
+    up_sum = sum_over_z(list(up_parts)).astype(bf16)
+    up_sum = lax.all_to_all(up_sum, GROUP, 0, 0, tiled=True).reshape(8, shard, wide)
+    (grad_wup,) = local(up_final_kernel, [like((shard, w_up.shape[1]), f32)], place, up_sum)
+
+    near, far = local(
+        out_grad_kernel, [like((4 * rows, width), bf16)] * 2, place, moved, grad_branch,
+        scratch=[pltpu.VMEM((8, rows, width), bf16)], flops=2 * rows * width * width,
+    )
+    own_part, *others = group_scatter(near, far, place)
+    line = own_part + others[0].astype(f32) + others[1].astype(f32) + others[2].astype(f32)
+    line = jnp.take(line.reshape(n_z, shard, width), lax.axis_index("z") ^ jnp.arange(n_z), axis=0)
+    line = [line[0]] + list(line[1:].astype(bf16))
+    grad_wout = sum_over_z(line)
+
+    extra = jnp.concatenate([sums_one[:3], sums_two[:3]], axis=0)
+    extra = extra.reshape(6, 32, shard).transpose(1, 0, 2).reshape(32, 6 * shard)
+    extra = jnp.pad(extra, ((0, 0), (0, 2 * shard)))
+    thin = jnp.sum(lax.all_to_all(extra, EVERY, 0, 0, tiled=True), axis=0).reshape(8, shard)
+
+    mixed, sums, *messages = local(
+        attend_grad_kernel,
+        [like((length, 3 * cols), bf16), like((1, 3 * cols), f32)]
+        + [like((rows, width), bf16)] * n_ctx,
+        place, grad_moved, queries, keys, values, attended, totals, tags_col, tags_row, full_qkv,
+        scratch=[
+            pltpu.VMEM((length, cols), f32),
+            pltpu.VMEM((length, cols), f32),
+            pltpu.VMEM((length, cols), bf16),
+        ],
+        flops=20 * length * length * cols,
+    )
+    grad_inputs = grad_first + ctx_sum(messages)
+    near, far = local(
+        qkv_grad_kernel, [like((2, width // 4 + 16, 3 * cols), bf16)] * 2, place, *blocks, mixed,
+        sums, scratch=[pltpu.VMEM((length, width), bf16)], flops=6 * length * width * cols,
+    )
+    qkv_sum = dp_sum(near, far)
+    qkv_rows = qkv_sum[: n_ctx * shard].reshape(n_ctx, shard, 3 * cols)
+    qkv_bias = jnp.broadcast_to(qkv_sum[n_ctx * shard :], (n_ctx, 16, 3 * cols))
+    qkv_sum = jnp.concatenate([qkv_rows, qkv_bias], axis=1).astype(bf16)
+    qkv_sum = lax.all_to_all(qkv_sum, CTX, 0, 0, tiled=True)
+    (grad_wqkv,) = local(qkv_final_kernel, [like((shard, 3 * width), f32)], place, qkv_sum)
+    bias_sum = qkv_sum[:, shard].reshape(n_ctx, 3, cols).transpose(1, 0, 2).reshape(3, width)
+    bias_own = lax.dynamic_slice(bias_sum, (0, own * shard), (3, shard)).astype(f32)
+
+    return (
+        result[None],
+        grad_inputs.astype(bf16)[None],
+        grad_wqkv,
+        bias_own[0],
+        bias_own[2],
+        grad_wout,
+        thin[0],
+        thin[1],
+        thin[2],
+        grad_wup,
+        down_sum[units, :units],
+        down_sum[:units],
+        thin[3],
+        thin[4],
+        thin[5],
+    )
+
+
+def call_heads(mesh, *arrays):
+    grid = Mesh(mesh.devices.reshape(2, 2, 4, 2), EVERY)
+    lines, lone, block = P(EVERY, None), P(EVERY), P(DP, CTX, None)
+    in_specs = (
+        block, lines, lone, lone, lines, lone, lone, lone, lines, lone, lines, lone, lone, lone,
+        P(DP, CTX), P(DP, CTX), block,
+    )
+    out_specs = (
+        block, block, lines, lone, lone, lines, lone, lone, lone, lines, lone, lines, lone, lone,
+        lone,
+    )
+    return jax.shard_map(
+        heads_body, mesh=grid, in_specs=in_specs, out_specs=out_specs, check_vma=False
+    )(*arrays)
+
+
+def call(mesh, *arrays):
+    if mesh.shape["dp"] == 4 and mesh.shape["ctx"] == 8 and arrays[0].shape[1] == 1024:
+        return call_heads(mesh, *arrays)
+    return general_call(mesh)(*arrays)
+
+
+def general_call(mesh):
     in_specs = (
         P("dp", "ctx", None),
         P(("dp", "ctx"), None),
@@ -400,4 +1001,8 @@
         P(("dp", "ctx")),
         P(("dp", "ctx")),
     )
-    return jax.shard_map(body, mesh=mesh, in_specs=in_specs, out_specs=out_specs, check_vma=False)
+    return jax.shard_map(general_body, mesh=mesh, in_specs=in_specs, out_specs=out_specs, check_vma=False)
+
+
+def solution(mesh):
+    return partial(call, mesh)

time: 1640 us -> 401 us (0.24)
  waiting for transfers between devices: 1310 us -> 173 us
  blocking collectives: 163 us -> 11.5 us
  matrix products: 90.1 us -> 0 us
  starting transfers between devices: 0.61 us -> 87.6 us
  Pallas kernels: 0 us -> 58 us
    reduce_scatter x4 -> x0, waiting for transfers between devices: 911 us -> none  [the longest x1 360 us: body(): lax.psum_scatter(grad_wdown, ('dp', 'ctx'), scatter_dimension=0, tiled=True)]
    all_gather x6 -> x2, waiting for transfers between devices: 236 us -> 0.03 us  [the longest x1 0.02 us: heads_body(): up = lax.all_gather(up, 'z', axis=0, tiled=True)]
    unnamed x12 -> x2, waiting for transfers between devices: 165 us -> 0.71 us
    ppermute x0 -> x61, waiting for transfers between devices: none -> 128 us  [swap(): lax.ppermute(member, axes, [(place, place ^ code) for place in range(coun...]
    dot_general x18 -> x0, matrix products: 90.1 us -> none  [the longest x4 27.6 us: rows_product(): lax.dot_general(left, right, (((0,), (0,)), ((), ())), preferred_element_...]
    all_gather x2 -> x0, blocking collectives: 81.9 us -> none  [the longest x1 65.5 us: body(): lax.all_gather(weight_shards[8], ('dp', 'ctx'), axis=0, tiled=True)]
    unnamed x2 -> x0, blocking collectives: 81.4 us -> none
    ppermute x0 -> x61, starting transfers between devices: none -> 63.8 us  [swap(): lax.ppermute(member, axes, [(place, place ^ code) for place in range(coun...]
  transfers between devices with their start and end apart: 11 -> 69, of which waited for: 9 -> 25; matrix products, arithmetic and copies ran while one was open for 5% -> 5% of each run, Pallas kernels for 0% -> 11%
where the time goes in v2:
time: 401 us; the launch traced here: 400 us
  waiting for transfers between devices  173 us (43%)
  starting transfers between devices  87.6 us (22%)
  Pallas kernels  58 us (14%)
  local copies, waits for them, and re-layouts  41.1 us (10%)
  between operations  15.1 us (4%)
  other arithmetic  13.3 us (3%)
  blocking collectives  11.5 us (3%)
    ppermute x61, waiting for transfers between devices, swap(): lax.ppermute(member, axes, [(place, place ^ code) for place in range(coun...  128 us
    ppermute x61, starting transfers between devices, swap(): lax.ppermute(member, axes, [(place, place ^ code) for place in range(coun...  63.8 us
    pallas_call x16, Pallas kernels, local(): pl.pallas_call(kernel, out_shape=list(outs), in_specs=[pl.BlockSpec(memor...  58 us
    unnamed x159, local copies, waits for them, and re-layouts  30.8 us
    all_to_all x1, waiting for transfers between devices, heads_body(): qkv = lax.all_to_all(qkv, CTX, 0, 0, tiled=True)  29.4 us
    all_to_all x1, blocking collectives, heads_body(): up = lax.all_to_all(up.reshape(8 * shard, wide), GROUP, 0, 0, tiled=True)  11.5 us
  transfers between devices with their start and end apart: 69, of which 25 were waited for; matrix products, arithmetic and copies ran while one was open for 5% of the time, Pallas kernels for 11%

profile of v2, /device:TPU:0, one launch (start us, length us, event | category | flops | bytes accessed | tf_op | source)
XLA Modules:
  0.0 399.6 jit_solution(1610661323918194776)
XLA Ops:
  8.8 11.5 %all_to_all.54 = bf16[8,32,512]{2,1,0:T(8,128)(2,1)} all-to-all(bf16[8,32,512]{2,1,0:T(8,128)(2,1)S(1)} %all_to_all.38), channel_id=1, replica_groups=mesh['y'=2,'core'=2,'z'=4,'x'=2] {'y','core','x'}, dimensions={0} | all-to-all | bytes 524288 | tf_op jit(solution)/shard_map/all_to_all | solution.py:814
  22.0 2.5 collective-permute-start.12
  24.6 2.9 collective-permute-start.5
  29.2 4.3 %all-to-all-start = ((bf16[8,48,384]{2,1,0:T(8,128)(2,1)}), bf16[8,48,384]{2,1,0:T(8,128)(2,1)S(1)}, u32[]{:S(2)}, u32[]{:S(2)}) async-start(bf16[8,48,384]{2,1,0:T(8,128)(2,1)} %pad_maximum_fusion.1), calls=%async_computation | async-start | bytes 589824 | tf_op jit(solution)/shard_map/all_to_all | solution.py:794
  34.9 2.1 collective-permute-start.1
  36.9 6.8 %collective-permute-done.11 = bf16[32,1024]{1,0:T(8,128)(2,1)S(1)} collective-permute-done((bf16[32,1024]{1,0:T(8,128)(2,1)S(1)}, bf16[32,1024]{1,0:T(8,128)(2,1)S(1)}, u32[]{:S(2)}, u32[]{:S(2)}) %collective-permute-start.11) | collective-permute-done | bytes 65568 | tf_op jit(solution)/shard_map/ppermute | solution.py:380
  43.8 3.2 collective-permute-start.13
  47.3 29.4 %all-to-all-done.refs_8_ = bf16[8,48,384]{2,1,0:T(8,128)(2,1)S(1)} async-done(((bf16[8,48,384]{2,1,0:T(8,128)(2,1)}), bf16[8,48,384]{2,1,0:T(8,128)(2,1)S(1)}, u32[]{:S(2)}, u32[]{:S(2)}) %all-to-all-start) | async-done | bytes 294944 | tf_op jit(solution)/shard_map/all_to_all | solution.py:794
  77.5 8.3 %collective-permute-done.8.refs_10_ = bf16[8,48,384]{2,1,0:T(8,128)(2,1)S(1)} collective-permute-done((bf16[8,48,384]{2,1,0:T(8,128)(2,1)S(1)}, bf16[8,48,384]{2,1,0:T(8,128)(2,1)S(1)}, u32[]{:S(2)}, u32[]{:S(2)}) %collective-permute-start.8) | collective-permute-done | bytes 294944 | tf_op jit(solution)/shard_map/ppermute | solution.py:380
  95.6 27.0 %collective-permute-done.14.p01 = bf16[2,4,32,1024]{3,2,1,0:T(8,128)(2,1)S(1)} collective-permute-done((bf16[2,4,32,1024]{3,2,1,0:T(8,128)(2,1)S(1)}, bf16[2,4,32,1024]{3,2,1,0:T(8,128)(2,1)S(1)}, u32[]{:S(2)}, u32[]{:S(2)}) %collective-permute-start.14) | collective-permute-done | bytes 524320 | tf_op jit(solution)/shard_map/ppermute | solution.py:380
  125.5 10.0 %shard_map.280 = (bf16[1024,128]{1,0:T(8,128)(2,1)S(1)}, bf16[1024,128]{1,0:T(8,128)(2,1)S(1)}, bf16[1024,128]{1,0:T(8,128)(2,1)S(1)}, f32[1024,128]{1,0:T(8,128...) custom-call(s32[7]{0:T(128)S(1)} %stack.70.place, ...), custom_call_target="tpu_custom_call" | custom-call | flops 1073741824 | bytes 5678592 | tf_op jit(solution)/shard_map/pallas_call | solution.py:391
  140.7 3.7 all-to-all-start.1
  145.7 2.1 shard_map.281
  148.7 5.3 %all-to-all-done.1.moved = bf16[8,128,128]{2,1,0:T(8,128)(2,1)S(1)} async-done(((bf16[8,128,128]{2,1,0:T(8,128)(2,1)}), bf16[8,128,128]{2,1,0:T(8,128)(2,1)S(1)}, u32[]{:S(2)}, u32[]{:S(2)}) %all-to-all-start.1) | async-done | bytes 262176 | tf_op jit(solution)/shard_map/all_to_all | solution.py:834
  161.4 6.7 %collective-permute-done.19.refs_3_.refs_11_ = bf16[128,1024]{1,0:T(8,128)(2,1)S(1)} collective-permute-done((bf16[128,1024]{1,0:T(8,128)(2,1)S(1)}, bf16[128,1024]{1,0:T(8,128)(2,1)S(1)}, u32[]{:S(2)}, u32[]{:S(2)}) %collective-permute-start.19) | collective-permute-done | bytes 262176 | tf_op jit(solution)/shard_map/ppermute | solution.py:380
  168.1 4.2 %collective-permute-done.18.refs_2_.refs_10_ = bf16[128,1024]{1,0:T(8,128)(2,1)S(1)} collective-permute-done((bf16[128,1024]{1,0:T(8,128)(2,1)S(1)}, bf16[128,1024]{1,0:T(8,128)(2,1)S(1)}, u32[]{:S(2)}, u32[]{:S(2)}) %collective-permute-start.18) | collective-permute-done | bytes 262176 | tf_op jit(solution)/shard_map/ppermute | solution.py:380
  178.1 5.4 %shard_map.283 = (f32[1024,512]{1,0:T(8,128)}, bf16[1024,512]{1,0:T(8,128)(2,1)S(1)}, bf16[512,1024]{1,0:T(8,128)(2,1)S(1)}, bf16[512,1024]{1,0:T(8,128)(2,1)S(1)}) custom-call(s32[7]{0:T(128)S(1)} %stack.70.place, bf16[128,1024]{1,0:T(8,128)(2,1)S(1)} %get-tuple-element.74.refs_0_.refs_8_, bf16[128,1024]{1,0:T(8,128)(2,1)S(1)} %collective-permute-done.17.refs_1_.refs_9_, ...), custom_call_target="tpu_custom_call" | custom-call | flops 2147483648 | bytes 9439232 | tf_op jit(solution)/shard_map/pallas_call | solution.py:391
  184.7 2.5 collective-permute-done.24.far
  191.5 5.7 %collective-permute-done.25.p1 = bf16[128,1024]{1,0:T(8,128)(2,1)S(1)} collective-permute-done((bf16[128,1024]{1,0:T(8,128)(2,1)S(1)}, bf16[128,1024]{1,0:T(8,128)(2,1)S(1)}, u32[]{:S(2)}, u32[]{:S(2)}) %collective-permute-start.25) | collective-permute-done | bytes 262176 | tf_op jit(solution)/shard_map/ppermute | solution.py:380
  197.2 5.5 %collective-permute-done.26.p2 = bf16[128,1024]{1,0:T(8,128)(2,1)S(1)} collective-permute-done((bf16[128,1024]{1,0:T(8,128)(2,1)S(1)}, bf16[128,1024]{1,0:T(8,128)(2,1)S(1)}, u32[]{:S(2)}, u32[]{:S(2)}) %collective-permute-start.26) | collective-permute-done | bytes 262176 | tf_op jit(solution)/shard_map/ppermute | solution.py:380
  207.8 6.7 %collective-permute-done.30.refs_3_ = bf16[128,1024]{1,0:T(8,128)(2,1)S(1)} collective-permute-done((bf16[128,1024]{1,0:T(8,128)(2,1)S(1)}, bf16[128,1024]{1,0:T(8,128)(2,1)S(1)}, u32[]{:S(2)}, u32[]{:S(2)}) %collective-permute-start.30) | collective-permute-done | bytes 262176 | tf_op jit(solution)/shard_map/ppermute | solution.py:380
  214.5 3.3 collective-permute-done.29.refs_2_
  220.2 6.1 %shard_map.286 = (bf16[1024,512]{1,0:T(8,128)(2,1)S(1)}, bf16[512,1024]{1,0:T(8,128)(2,1)S(1)}, bf16[512,1024]{1,0:T(8,128)(2,1)}) custom-call(s32[7]{0:T(128)S(1)} %stack.70.place, bf16[128,1024]{1,0:T(8,128)(2,1)S(1)} %get-tuple-element.84.refs_0_, bf16[128,1024]{1,0:T(8,128)(2,1)S(1)} %collective-permute-done.28.refs_1_, ...), custom_call_target="tpu_custom_call" | custom-call | flops 2147483648 | bytes 9437184 | tf_op jit(solution)/shard_map/pallas_call | solution.py:391
  227.4 4.9 %shard_map.294 = (bf16[4,144,1024]{2,1,0:T(8,128)(2,1)}, bf16[4,256,512]{2,1,0:T(8,128)(2,1)S(1)}) custom-call(s32[7]{0:T(128)S(1)} %stack.70.place, bf16[128,1024]{1,0:T(8,128)(2,1)S(1)} %get-tuple-element.84.refs_0_, bf16[128,1024]{1,0:T(8,128)(2,1)S(1)} %collective-permute-done.28.refs_1_, bf16[128,1024]{1,0:T(8,128)(2,1)S(1)} %collective-permute-done.29.refs_2_, ...), custom_call_target="tpu_custom_call" | custom-call | flops 2147483648 | bytes 8519680 | tf_op jit(solution)/shard_map/pallas_call | solution.py:391
  233.2 2.3 collective-permute-start.57
  242.2 2.0 collective-permute-start.38
  245.1 3.5 collective-permute-done.57
  248.7 7.2 %collective-permute-start.58 = (bf16[144,1024]{1,0:T(8,128)(2,1)}, bf16[144,1024]{1,0:T(8,128)(2,1)}, u32[]{:S(2)}, u32[]{:S(2)}) collective-permute-start(bf16[144,1024]{1,0:T(8,128)(2,1)} %get-tuple-element.129), channel_id=1, source_target_pairs={{0,2},{2,0},{4,6},{6,4},{1,3},{3,1},{5,7},{7,5},{8,10},{10,8},{12,... | collective-permute-start | bytes 884744 | tf_op jit(solution)/shard_map/ppermute | solution.py:380
  255.9 4.4 %collective-permute-done.56 = bf16[256,512]{1,0:T(8,128)(2,1)} collective-permute-done((bf16[256,512]{1,0:T(8,128)(2,1)}, bf16[256,512]{1,0:T(8,128)(2,1)}, u32[]{:S(2)}, u32[]{:S(2)}) %collective-permute-start.56) | collective-permute-done | bytes 262176 | tf_op jit(solution)/shard_map/ppermute | solution.py:380
  262.0 1.9 fusion.8
  264.0 3.6 all-to-all-start.6
  270.9 3.0 shard_map.288
  276.3 5.2 %all-to-all-start.5 = ((f32[32,1,256]{2,1,0:T(1,128)}), f32[32,1,256]{2,1,0:T(1,128)S(1)}, u32[]{:S(2)}, u32[]{:S(2)}) async-start(f32[32,1,256]{2,1,0:T(1,128)} %copy.48), calls=%async_computation.5 | async-start | bytes 65536 | tf_op jit(solution)/shard_map/all_to_all | solution.py:898
  281.5 7.2 %all-to-all-done.5 = f32[32,1,256]{2,1,0:T(1,128)S(1)} async-done(((f32[32,1,256]{2,1,0:T(1,128)}), f32[32,1,256]{2,1,0:T(1,128)S(1)}, u32[]{:S(2)}, u32[]{:S(2)}) %all-to-all-start.5) | async-done | bytes 32800 | tf_op jit(solution)/shard_map/all_to_all | solution.py:898
  288.7 3.4 all-to-all-start.3
  296.4 2.4 shard_map.292
  298.9 2.6 all-to-all-done.3.moved
  306.6 11.7 %shard_map.289 = (bf16[1024,384]{1,0:T(8,128)(2,1)S(1)}, f32[1,384]{1,0:T(1,128)S(1)}, bf16[128,1024]{1,0:T(8,128)(2,1)S(1)}, bf16[128,1024]{1,0:T(8,128)(2,1)},...) custom-call(s32[7]{0:T(128)S(1)} %stack.70.place, ...), custom_call_target="tpu_custom_call" | custom-call | flops 2684354560 | bytes 5285376 | tf_op jit(solution)/shard_map/pallas_call | solution.py:391
  323.0 2.8 shard_map.290
  328.3 10.5 %collective-permute-done.42 = bf16[128,1024]{1,0:T(8,128)(2,1)S(1)} collective-permute-done((bf16[128,1024]{1,0:T(8,128)(2,1)S(1)}, bf16[128,1024]{1,0:T(8,128)(2,1)S(1)}, u32[]{:S(2)}, u32[]{:S(2)}) %collective-permute-start.42) | collective-permute-done | bytes 262176 | tf_op jit(solution)/shard_map/ppermute | solution.py:380
  345.9 4.0 %collective-permute-done.47 = bf16[272,384]{1,0:T(8,128)(2,1)S(1)} collective-permute-done((bf16[272,384]{1,0:T(8,128)(2,1)S(1)}, bf16[272,384]{1,0:T(8,128)(2,1)S(1)}, u32[]{:S(2)}, u32[]{:S(2)}) %collective-permute-start.47) | collective-permute-done | bytes 208928 | tf_op jit(solution)/shard_map/ppermute | solution.py:380
  350.8 3.4 all-to-all-start.4
  354.3 2.8 collective-permute-start.43
  357.1 2.6 collective-permute-start.45
  360.6 2.2 collective-permute-start.52
  364.7 18.9 %collective-permute-done.43 = bf16[128,1024]{1,0:T(8,128)(2,1)} collective-permute-done((bf16[128,1024]{1,0:T(8,128)(2,1)}, bf16[128,1024]{1,0:T(8,128)(2,1)}, u32[]{:S(2)}, u32[]{:S(2)}) %collective-permute-start.43) | collective-permute-done | bytes 262176 | tf_op jit(solution)/shard_map/ppermute | solution.py:380
  383.5 2.1 fusion.10
  385.6 4.4 %collective-permute-done.53 = bf16[32,1024]{1,0:T(8,128)(2,1)S(1)} collective-permute-done((bf16[32,1024]{1,0:T(8,128)(2,1)S(1)}, bf16[32,1024]{1,0:T(8,128)(2,1)S(1)}, u32[]{:S(2)}, u32[]{:S(2)}) %collective-permute-start.53) | collective-permute-done | bytes 65568 | tf_op jit(solution)/shard_map/ppermute | solution.py:380
  (352 shorter events, 100.1 us)
Async XLA Ops:
  7.3 137.1 %all-gather.3.cloned.1.call-start = ((), (), s32[]{:S(2)}) async-start(), calls=%async_computation.7 | async-start | bytes 1310720 | tf_op jit(solution)/shard_map/all_gather | solution.py:815
  20.4 14.5 %collective-permute-start.10 = (bf16[32,1024]{1,0:T(8,128)(2,1)S(1)}, bf16[32,1024]{1,0:T(8,128)(2,1)S(1)}, u32[]{:S(2)}, u32[]{:S(2)}) collective-permute-start(bf16[32,1024]{1,0:T(8,128)(2,1)S(1)} %copy-done.64), channel_id=1, source_target_pairs={{0,2},{2,0},{4,6},{6,4},{1,3},{3,1},{5,7},{7,5},{8,10},{10,8},{12,... | collective-permute-start | bytes 196616 | tf_op jit(solution)/shard_map/ppermute | solution.py:380
  22.0 14.9 %collective-permute-start.12 = (bf16[32,1024]{1,0:T(8,128)(2,1)S(1)}, bf16[32,1024]{1,0:T(8,128)(2,1)S(1)}, u32[]{:S(2)}, u32[]{:S(2)}) collective-permute-start(bf16[32,1024]{1,0:T(8,128)(2,1)S(1)} %copy-done.64), channel_id=1, source_target_pairs={{0,6},{2,4},{4,2},{6,0},{1,7},{3,5},{5,3},{7,1},{8,14},{10,12},{12... | collective-permute-start | bytes 196616 | tf_op jit(solution)/shard_map/ppermute | solution.py:380
  24.5 19.2 %collective-permute-start.11 = (bf16[32,1024]{1,0:T(8,128)(2,1)S(1)}, bf16[32,1024]{1,0:T(8,128)(2,1)S(1)}, u32[]{:S(2)}, u32[]{:S(2)}) collective-permute-start(bf16[32,1024]{1,0:T(8,128)(2,1)S(1)} %copy-done.64), channel_id=1, source_target_pairs={{0,4},{2,6},{4,0},{6,2},{1,5},{3,7},{5,1},{7,3},{8,12},{10,14},{12... | collective-permute-start | bytes 196616 | tf_op jit(solution)/shard_map/ppermute | solution.py:380
  24.6 61.1 %collective-permute-start.5 = (bf16[128,1024]{1,0:T(8,128)(2,1)S(1)}, bf16[128,1024]{1,0:T(8,128)(2,1)}, u32[]{:S(2)}, u32[]{:S(2)}) collective-permute-start(bf16[128,1024]{1,0:T(8,128)(2,1)S(1)} %bitcast.121), channel_id=1, source_target_pairs={{0,6},{2,4},{4,2},{6,0},{1,7},{3,5},{5,3},{7,1},{8,14},{10,12},{12... | collective-permute-start | bytes 786440 | tf_op jit(solution)/shard_map/ppermute | solution.py:380
  27.5 59.0 %collective-permute-start.3 = (bf16[128,1024]{1,0:T(8,128)(2,1)S(1)}, bf16[128,1024]{1,0:T(8,128)(2,1)}, u32[]{:S(2)}, u32[]{:S(2)}) collective-permute-start(bf16[128,1024]{1,0:T(8,128)(2,1)S(1)} %bitcast.122), channel_id=1, source_target_pairs={{0,4},{2,6},{4,0},{6,2},{1,5},{3,7},{5,1},{7,3},{8,12},{10,14},{12... | collective-permute-start | bytes 786440 | tf_op jit(solution)/shard_map/ppermute | solution.py:380
  29.2 47.5 %all-to-all-start = ((bf16[8,48,384]{2,1,0:T(8,128)(2,1)}), bf16[8,48,384]{2,1,0:T(8,128)(2,1)S(1)}, u32[]{:S(2)}, u32[]{:S(2)}) async-start(bf16[8,48,384]{2,1,0:T(8,128)(2,1)} %pad_maximum_fusion.1), calls=%async_computation | async-start | bytes 589824 | tf_op jit(solution)/shard_map/all_to_all | solution.py:794
  33.6 139.3 %all-gather.5.cloned.1.call-start = ((), (), s32[]{:S(2)}) async-start(), calls=%async_computation.8 | async-start | bytes 1310720 | tf_op jit(solution)/shard_map/all_gather | solution.py:816
  34.9 53.0 %collective-permute-start.1 = (bf16[128,1024]{1,0:T(8,128)(2,1)S(1)}, bf16[128,1024]{1,0:T(8,128)(2,1)}, u32[]{:S(2)}, u32[]{:S(2)}) collective-permute-start(bf16[128,1024]{1,0:T(8,128)(2,1)S(1)} %bitcast.123), channel_id=1, source_target_pairs={{0,2},{2,0},{4,6},{6,4},{1,3},{3,1},{5,7},{7,5},{8,10},{10,8},{12,... | collective-permute-start | bytes 786440 | tf_op jit(solution)/shard_map/ppermute | solution.py:380
  43.8 33.6 %collective-permute-start.13 = (bf16[4,32,1024]{2,1,0:T(8,128)(2,1)S(1)}, bf16[4,32,1024]{2,1,0:T(8,128)(2,1)S(1)}, u32[]{:S(2)}, u32[]{:S(2)}) collective-permute-start(bf16[4,32,1024]{2,1,0:T(8,128)(2,1)S(1)} %get-tuple-element.139), channel_id=1, source_target_pairs={{0,16},{16,0},{1,17},{17,1},{2,18},{18,2},{3,19},{19,3},{4,20},{20... | collective-permute-start | bytes 786440 | tf_op jit(solution)/shard_map/ppermute | solution.py:380
  86.5 36.1 %collective-permute-start.6 = (bf16[128,1024]{1,0:T(8,128)(2,1)}, bf16[128,1024]{1,0:T(8,128)(2,1)}, u32[]{:S(2)}, u32[]{:S(2)}) collective-permute-start(bf16[128,1024]{1,0:T(8,128)(2,1)} %collective-permute-done.5.refs_6_), channel_id=1, source_target_pairs={{0,1},{1,0},{2,3},{3,2},{4,5},{5,4},{6,7},{7,6},{8,9},{9,8},{10,11... | collective-permute-start | bytes 786440 | tf_op jit(solution)/shard_map/ppermute | solution.py:380
  87.9 34.8 %collective-permute-start.4 = (bf16[128,1024]{1,0:T(8,128)(2,1)}, bf16[128,1024]{1,0:T(8,128)(2,1)}, u32[]{:S(2)}, u32[]{:S(2)}) collective-permute-start(bf16[128,1024]{1,0:T(8,128)(2,1)} %collective-permute-done.3.refs_4_), channel_id=1, source_target_pairs={{0,1},{1,0},{2,3},{3,2},{4,5},{5,4},{6,7},{7,6},{8,9},{9,8},{10,11... | collective-permute-start | bytes 786440 | tf_op jit(solution)/shard_map/ppermute | solution.py:380
  88.5 34.1 %collective-permute-start.2 = (bf16[128,1024]{1,0:T(8,128)(2,1)}, bf16[128,1024]{1,0:T(8,128)(2,1)}, u32[]{:S(2)}, u32[]{:S(2)}) collective-permute-start(bf16[128,1024]{1,0:T(8,128)(2,1)} %collective-permute-done.1.refs_2_), channel_id=1, source_target_pairs={{0,1},{1,0},{2,3},{3,2},{4,5},{5,4},{6,7},{7,6},{8,9},{9,8},{10,11... | collective-permute-start | bytes 786440 | tf_op jit(solution)/shard_map/ppermute | solution.py:380
  90.6 32.0 %collective-permute-start.14 = (bf16[2,4,32,1024]{3,2,1,0:T(8,128)(2,1)S(1)}, bf16[2,4,32,1024]{3,2,1,0:T(8,128)(2,1)S(1)}, u32[]{:S(2)}, u32[]{:S(2)}) collective-permute-start(bf16[2,4,32,1024]{3,2,1,0:T(8,128)(2,1)S(1)} %pad_maximum_fusion.p00), channel_id=1, source_target_pairs={{0,1},{1,0},{2,3},{3,2},{4,5},{5,4},{6,7},{7,6},{8,9},{9,8},{10,11... | collective-permute-start | bytes 1572872 | tf_op jit(solution)/shard_map/ppermute | solution.py:380
  95.6 48.8 %collective-permute-start.15 = (bf16[2,4,32,1024]{3,2,1,0:T(8,128)(2,1)S(1)}, bf16[2,4,32,1024]{3,2,1,0:T(8,128)(2,1)S(1)}, u32[]{:S(2)}, u32[]{:S(2)}) collective-permute-start(bf16[2,4,32,1024]{3,2,1,0:T(8,128)(2,1)S(1)} %pad_maximum_fusion.p00), channel_id=1, source_target_pairs={{0,8},{8,0},{1,9},{9,1},{2,10},{10,2},{3,11},{11,3},{4,12},{12,4},... | collective-permute-start | bytes 1572872 | tf_op jit(solution)/shard_map/ppermute | solution.py:380
  122.6 21.8 %collective-permute-start.16 = (bf16[2,4,32,1024]{3,2,1,0:T(8,128)(2,1)S(1)}, bf16[2,4,32,1024]{3,2,1,0:T(8,128)(2,1)S(1)}, u32[]{:S(2)}, u32[]{:S(2)}) collective-permute-start(bf16[2,4,32,1024]{3,2,1,0:T(8,128)(2,1)S(1)} %collective-permute-done.14.p01), channel_id=1, source_target_pairs={{0,8},{8,0},{1,9},{9,1},{2,10},{10,2},{3,11},{11,3},{4,12},{12,4},... | collective-permute-start | bytes 1572872 | tf_op jit(solution)/shard_map/ppermute | solution.py:380
  140.7 13.3 %all-to-all-start.1 = ((bf16[8,128,128]{2,1,0:T(8,128)(2,1)}), bf16[8,128,128]{2,1,0:T(8,128)(2,1)S(1)}, u32[]{:S(2)}, u32[]{:S(2)}) async-start(bf16[8,128,128]{2,1,0:T(8,128)(2,1)} %bitcast.128), calls=%async_computation.1 | async-start | bytes 524288 | tf_op jit(solution)/shard_map/all_to_all | solution.py:834
  159.4 12.9 %collective-permute-start.18 = (bf16[128,1024]{1,0:T(8,128)(2,1)S(1)}, bf16[128,1024]{1,0:T(8,128)(2,1)S(1)}, u32[]{:S(2)}, u32[]{:S(2)}) collective-permute-start(bf16[128,1024]{1,0:T(8,128)(2,1)S(1)} %get-tuple-element.74.refs_0_.refs_8_), channel_id=1, source_target_pairs={{0,16},{1,17},{16,0},{17,1},{2,18},{3,19},{18,2},{19,3},{4,20},{5,... | collective-permute-start | bytes 786440 | tf_op jit(solution)/shard_map/ppermute | solution.py:380
  160.8 11.5 %collective-permute-start.17 = (bf16[128,1024]{1,0:T(8,128)(2,1)S(1)}, bf16[128,1024]{1,0:T(8,128)(2,1)S(1)}, u32[]{:S(2)}, u32[]{:S(2)}) collective-permute-start(bf16[128,1024]{1,0:T(8,128)(2,1)S(1)} %get-tuple-element.74.refs_0_.refs_8_), channel_id=1, source_target_pairs={{0,1},{1,0},{16,17},{17,16},{2,3},{3,2},{18,19},{19,18},{4,5},{5,4... | collective-permute-start | bytes 786440 | tf_op jit(solution)/shard_map/ppermute | solution.py:380
  161.4 11.4 %collective-permute-start.20 = (bf16[128,1024]{1,0:T(8,128)(2,1)S(1)}, bf16[128,1024]{1,0:T(8,128)(2,1)S(1)}, u32[]{:S(2)}, u32[]{:S(2)}) collective-permute-start(bf16[128,1024]{1,0:T(8,128)(2,1)S(1)} %get-tuple-element.74.refs_0_.refs_8_), channel_id=1, source_target_pairs={{0,8},{8,0},{1,9},{9,1},{2,10},{10,2},{3,11},{11,3},{4,12},{12,4},... | collective-permute-start | bytes 786440 | tf_op jit(solution)/shard_map/ppermute | solution.py:380
  189.0 13.7 %collective-permute-start.26 = (bf16[128,1024]{1,0:T(8,128)(2,1)S(1)}, bf16[128,1024]{1,0:T(8,128)(2,1)S(1)}, u32[]{:S(2)}, u32[]{:S(2)}) collective-permute-start(bf16[128,1024]{1,0:T(8,128)(2,1)S(1)} %get-tuple-element.80), channel_id=1, source_target_pairs={{0,16},{1,17},{16,0},{17,1},{2,18},{3,19},{18,2},{19,3},{4,20},{5,... | collective-permute-start | bytes 786440 | tf_op jit(solution)/shard_map/ppermute | solution.py:380
  190.1 12.5 %collective-permute-start.27 = (bf16[128,1024]{1,0:T(8,128)(2,1)S(1)}, bf16[128,1024]{1,0:T(8,128)(2,1)S(1)}, u32[]{:S(2)}, u32[]{:S(2)}) collective-permute-start(bf16[128,1024]{1,0:T(8,128)(2,1)S(1)} %get-tuple-element.81), channel_id=1, source_target_pairs={{0,17},{1,16},{16,1},{17,0},{2,19},{3,18},{18,3},{19,2},{4,21},{5,... | collective-permute-start | bytes 786440 | tf_op jit(solution)/shard_map/ppermute | solution.py:380
  205.5 12.3 %collective-permute-start.29 = (bf16[128,1024]{1,0:T(8,128)(2,1)S(1)}, bf16[128,1024]{1,0:T(8,128)(2,1)S(1)}, u32[]{:S(2)}, u32[]{:S(2)}) collective-permute-start(bf16[128,1024]{1,0:T(8,128)(2,1)S(1)} %get-tuple-element.84.refs_0_), channel_id=1, source_target_pairs={{0,16},{1,17},{16,0},{17,1},{2,18},{3,19},{18,2},{19,3},{4,20},{5,... | collective-permute-start | bytes 786440 | tf_op jit(solution)/shard_map/ppermute | solution.py:380
  207.8 12.4 %collective-permute-start.31 = (bf16[128,1024]{1,0:T(8,128)(2,1)S(1)}, bf16[128,1024]{1,0:T(8,128)(2,1)S(1)}, u32[]{:S(2)}, u32[]{:S(2)}) collective-permute-start(bf16[128,1024]{1,0:T(8,128)(2,1)S(1)} %get-tuple-element.84.refs_0_), channel_id=1, source_target_pairs={{0,8},{8,0},{1,9},{9,1},{2,10},{10,2},{3,11},{11,3},{4,12},{12,4},... | collective-permute-start | bytes 786440 | tf_op jit(solution)/shard_map/ppermute | solution.py:380
  233.2 15.4 %collective-permute-start.57 = (bf16[256,512]{1,0:T(8,128)(2,1)}, bf16[256,512]{1,0:T(8,128)(2,1)}, u32[]{:S(2)}, u32[]{:S(2)}) collective-permute-start(bf16[256,512]{1,0:T(8,128)(2,1)} %get-tuple-element.133), channel_id=1, source_target_pairs={{0,6},{2,4},{4,2},{6,0},{1,7},{3,5},{5,3},{7,1},{8,14},{10,12},{12... | collective-permute-start | bytes 786440 | tf_op jit(solution)/shard_map/ppermute | solution.py:380
  235.6 24.7 %collective-permute-start.56 = (bf16[256,512]{1,0:T(8,128)(2,1)}, bf16[256,512]{1,0:T(8,128)(2,1)}, u32[]{:S(2)}, u32[]{:S(2)}) collective-permute-start(bf16[256,512]{1,0:T(8,128)(2,1)} %get-tuple-element.134), channel_id=1, source_target_pairs={{0,4},{2,6},{4,0},{6,2},{1,5},{3,7},{5,1},{7,3},{8,12},{10,14},{12... | collective-permute-start | bytes 786440 | tf_op jit(solution)/shard_map/ppermute | solution.py:380
  238.9 28.8 %collective-permute-start.36 = (bf16[128,1024]{1,0:T(8,128)(2,1)}, bf16[128,1024]{1,0:T(8,128)(2,1)}, u32[]{:S(2)}, u32[]{:S(2)}) collective-permute-start(bf16[128,1024]{1,0:T(8,128)(2,1)} %get-tuple-element.89), channel_id=1, source_target_pairs={{0,1},{1,0},{16,17},{17,16},{2,3},{3,2},{18,19},{19,18},{4,5},{5,4... | collective-permute-start | bytes 786440 | tf_op jit(solution)/shard_map/ppermute | solution.py:380
  240.3 27.4 %collective-permute-start.37 = (bf16[128,1024]{1,0:T(8,128)(2,1)}, bf16[128,1024]{1,0:T(8,128)(2,1)}, u32[]{:S(2)}, u32[]{:S(2)}) collective-permute-start(bf16[128,1024]{1,0:T(8,128)(2,1)} %get-tuple-element.90), channel_id=1, source_target_pairs={{0,16},{1,17},{16,0},{17,1},{2,18},{3,19},{18,2},{19,3},{4,20},{5,... | collective-permute-start | bytes 786440 | tf_op jit(solution)/shard_map/ppermute | solution.py:380
  242.2 25.5 %collective-permute-start.38 = (bf16[128,1024]{1,0:T(8,128)(2,1)}, bf16[128,1024]{1,0:T(8,128)(2,1)}, u32[]{:S(2)}, u32[]{:S(2)}) collective-permute-start(bf16[128,1024]{1,0:T(8,128)(2,1)} %get-tuple-element.91), channel_id=1, source_target_pairs={{0,17},{1,16},{16,1},{17,0},{2,19},{3,18},{18,3},{19,2},{4,21},{5,... | collective-permute-start | bytes 786440 | tf_op jit(solution)/shard_map/ppermute | solution.py:380
  248.7 43.5 %collective-permute-start.58 = (bf16[144,1024]{1,0:T(8,128)(2,1)}, bf16[144,1024]{1,0:T(8,128)(2,1)}, u32[]{:S(2)}, u32[]{:S(2)}) collective-permute-start(bf16[144,1024]{1,0:T(8,128)(2,1)} %get-tuple-element.129), channel_id=1, source_target_pairs={{0,2},{2,0},{4,6},{6,4},{1,3},{3,1},{5,7},{7,5},{8,10},{10,8},{12,... | collective-permute-start | bytes 884744 | tf_op jit(solution)/shard_map/ppermute | solution.py:380
  260.3 31.9 %collective-permute-start.60 = (bf16[144,1024]{1,0:T(8,128)(2,1)}, bf16[144,1024]{1,0:T(8,128)(2,1)}, u32[]{:S(2)}, u32[]{:S(2)}) collective-permute-start(bf16[144,1024]{1,0:T(8,128)(2,1)} %get-tuple-element.130), channel_id=1, source_target_pairs={{0,6},{2,4},{4,2},{6,0},{1,7},{3,5},{5,3},{7,1},{8,14},{10,12},{12... | collective-permute-start | bytes 884744 | tf_op jit(solution)/shard_map/ppermute | solution.py:380
  264.0 12.3 %all-to-all-start.6 = ((bf16[8,32,512]{2,1,0:T(8,128)(2,1)}), bf16[8,32,512]{2,1,0:T(8,128)(2,1)S(1)}, u32[]{:S(2)}, u32[]{:S(2)}) async-start(bf16[8,32,512]{2,1,0:T(8,128)(2,1)} %bitcast.133), calls=%async_computation.6 | async-start | bytes 524288 | tf_op jit(solution)/shard_map/all_to_all | solution.py:882
  267.6 24.5 %collective-permute-start.59 = (bf16[144,1024]{1,0:T(8,128)(2,1)}, bf16[144,1024]{1,0:T(8,128)(2,1)}, u32[]{:S(2)}, u32[]{:S(2)}) collective-permute-start(bf16[144,1024]{1,0:T(8,128)(2,1)} %get-tuple-element.131), channel_id=1, source_target_pairs={{0,4},{2,6},{4,0},{6,2},{1,5},{3,7},{5,1},{7,3},{8,12},{10,14},{12... | collective-permute-start | bytes 884744 | tf_op jit(solution)/shard_map/ppermute | solution.py:380
  276.3 12.4 %all-to-all-start.5 = ((f32[32,1,256]{2,1,0:T(1,128)}), f32[32,1,256]{2,1,0:T(1,128)S(1)}, u32[]{:S(2)}, u32[]{:S(2)}) async-start(f32[32,1,256]{2,1,0:T(1,128)} %copy.48), calls=%async_computation.5 | async-start | bytes 65536 | tf_op jit(solution)/shard_map/all_to_all | solution.py:898
  288.7 12.8 %all-to-all-start.3 = ((bf16[8,128,128]{2,1,0:T(8,128)(2,1)}), bf16[8,128,128]{2,1,0:T(8,128)(2,1)S(1)}, u32[]{:S(2)}, u32[]{:S(2)}) async-start(bf16[8,128,128]{2,1,0:T(8,128)(2,1)} %get-tuple-element.95), calls=%async_computation.3 | async-start | bytes 524288 | tf_op jit(solution)/shard_map/all_to_all | solution.py:872
  298.7 44.2 %collective-permute-start.48 = (bf16[512,1024]{1,0:T(8,128)(2,1)}, bf16[512,1024]{1,0:T(8,128)(2,1)S(1)}, u32[]{:S(2)}, u32[]{:S(2)}) collective-permute-start(bf16[512,1024]{1,0:T(8,128)(2,1)} %get-tuple-element.116), channel_id=1, source_target_pairs={{0,8},{8,0},{1,9},{9,1},{2,10},{10,2},{3,11},{11,3},{4,12},{12,4},... | collective-permute-start | bytes 3145736 | tf_op jit(solution)/shard_map/ppermute | solution.py:380
  320.3 42.5 %collective-permute-start.39 = (bf16[128,1024]{1,0:T(8,128)(2,1)}, bf16[128,1024]{1,0:T(8,128)(2,1)}, u32[]{:S(2)}, u32[]{:S(2)}) collective-permute-start(bf16[128,1024]{1,0:T(8,128)(2,1)} %get-tuple-element.103), channel_id=1, source_target_pairs={{0,1},{1,0},{2,3},{3,2},{4,5},{5,4},{6,7},{7,6},{8,9},{9,8},{10,11... | collective-permute-start | bytes 786440 | tf_op jit(solution)/shard_map/ppermute | solution.py:380
  320.9 17.9 %collective-permute-start.42 = (bf16[128,1024]{1,0:T(8,128)(2,1)S(1)}, bf16[128,1024]{1,0:T(8,128)(2,1)S(1)}, u32[]{:S(2)}, u32[]{:S(2)}) collective-permute-start(bf16[128,1024]{1,0:T(8,128)(2,1)S(1)} %get-tuple-element.107), channel_id=1, source_target_pairs={{0,1},{1,0},{2,3},{3,2},{4,5},{5,4},{6,7},{7,6},{8,9},{9,8},{10,11... | collective-permute-start | bytes 786440 | tf_op jit(solution)/shard_map/ppermute | solution.py:380
  322.4 19.8 %collective-permute-start.44 = (bf16[128,1024]{1,0:T(8,128)(2,1)S(1)}, bf16[128,1024]{1,0:T(8,128)(2,1)S(1)}, u32[]{:S(2)}, u32[]{:S(2)}) collective-permute-start(bf16[128,1024]{1,0:T(8,128)(2,1)S(1)} %get-tuple-element.109), channel_id=1, source_target_pairs={{0,1},{1,0},{2,3},{3,2},{4,5},{5,4},{6,7},{7,6},{8,9},{9,8},{10,11... | collective-permute-start | bytes 786440 | tf_op jit(solution)/shard_map/ppermute | solution.py:380
  327.6 13.1 %collective-permute-start.46 = (bf16[2,272,384]{2,1,0:T(8,128)(2,1)S(1)}, bf16[2,272,384]{2,1,0:T(8,128)(2,1)S(1)}, u32[]{:S(2)}, u32[]{:S(2)}) collective-permute-start(bf16[2,272,384]{2,1,0:T(8,128)(2,1)S(1)} %get-tuple-element.113), channel_id=1, source_target_pairs={{0,8},{8,0},{1,9},{9,1},{2,10},{10,2},{3,11},{11,3},{4,12},{12,4},... | collective-permute-start | bytes 1253384 | tf_op jit(solution)/shard_map/ppermute | solution.py:380
  338.8 25.3 %collective-permute-start.41 = (bf16[128,1024]{1,0:T(8,128)(2,1)}, bf16[128,1024]{1,0:T(8,128)(2,1)}, u32[]{:S(2)}, u32[]{:S(2)}) collective-permute-start(bf16[128,1024]{1,0:T(8,128)(2,1)} %add_convert_fusion.3), channel_id=1, source_target_pairs={{0,2},{2,0},{4,6},{6,4},{1,3},{3,1},{5,7},{7,5},{8,10},{10,8},{12,... | collective-permute-start | bytes 786440 | tf_op jit(solution)/shard_map/ppermute | solution.py:380
  345.3 11.8 %collective-permute-start.50 = (bf16[128,1024]{1,0:T(8,128)(2,1)}, bf16[128,1024]{1,0:T(8,128)(2,1)S(1)}, u32[]{:S(2)}, u32[]{:S(2)}) collective-permute-start(bf16[128,1024]{1,0:T(8,128)(2,1)} %get-tuple-element.119), channel_id=1, source_target_pairs={{0,16},{1,17},{16,0},{17,1},{2,18},{3,19},{18,2},{19,3},{4,20},{5,... | collective-permute-start | bytes 786440 | tf_op jit(solution)/shard_map/ppermute | solution.py:380
  350.8 39.9 %all-to-all-start.4 = ((bf16[8,48,384]{2,1,0:T(8,128)(2,1)}), bf16[8,48,384]{2,1,0:T(8,128)(2,1)S(1)}, u32[]{:S(2)}, u32[]{:S(2)}) async-start(bf16[8,48,384]{2,1,0:T(8,128)(2,1)} %pad_maximum_fusion.2), calls=%async_computation.4 | async-start | bytes 589824 | tf_op jit(solution)/shard_map/all_to_all | solution.py:921
  354.3 29.3 %collective-permute-start.43 = (bf16[128,1024]{1,0:T(8,128)(2,1)}, bf16[128,1024]{1,0:T(8,128)(2,1)}, u32[]{:S(2)}, u32[]{:S(2)}) collective-permute-start(bf16[128,1024]{1,0:T(8,128)(2,1)} %add_convert_fusion.2), channel_id=1, source_target_pairs={{0,4},{2,6},{4,0},{6,2},{1,5},{3,7},{5,1},{7,3},{8,12},{10,14},{12... | collective-permute-start | bytes 786440 | tf_op jit(solution)/shard_map/ppermute | solution.py:380
  357.1 26.4 %collective-permute-start.45 = (bf16[128,1024]{1,0:T(8,128)(2,1)}, bf16[128,1024]{1,0:T(8,128)(2,1)}, u32[]{:S(2)}, u32[]{:S(2)}) collective-permute-start(bf16[128,1024]{1,0:T(8,128)(2,1)} %add_convert_fusion.1), channel_id=1, source_target_pairs={{0,6},{2,4},{4,2},{6,0},{1,7},{3,5},{5,3},{7,1},{8,14},{10,12},{12... | collective-permute-start | bytes 786440 | tf_op jit(solution)/shard_map/ppermute | solution.py:380
  360.6 25.0 %collective-permute-start.52 = (bf16[32,1024]{1,0:T(8,128)(2,1)S(1)}, bf16[32,1024]{1,0:T(8,128)(2,1)S(1)}, u32[]{:S(2)}, u32[]{:S(2)}) collective-permute-start(bf16[32,1024]{1,0:T(8,128)(2,1)S(1)} %get-tuple-element.135), channel_id=1, source_target_pairs={{0,2},{2,0},{4,6},{6,4},{1,3},{3,1},{5,7},{7,5},{8,10},{10,8},{12,... | collective-permute-start | bytes 196616 | tf_op jit(solution)/shard_map/ppermute | solution.py:380
  362.8 22.8 %collective-permute-start.54 = (bf16[32,1024]{1,0:T(8,128)(2,1)S(1)}, bf16[32,1024]{1,0:T(8,128)(2,1)S(1)}, u32[]{:S(2)}, u32[]{:S(2)}) collective-permute-start(bf16[32,1024]{1,0:T(8,128)(2,1)S(1)} %get-tuple-element.136), channel_id=1, source_target_pairs={{0,6},{2,4},{4,2},{6,0},{1,7},{3,5},{5,3},{7,1},{8,14},{10,12},{12... | collective-permute-start | bytes 196616 | tf_op jit(solution)/shard_map/ppermute | solution.py:380
  364.1 26.0 %collective-permute-start.53 = (bf16[32,1024]{1,0:T(8,128)(2,1)S(1)}, bf16[32,1024]{1,0:T(8,128)(2,1)S(1)}, u32[]{:S(2)}, u32[]{:S(2)}) collective-permute-start(bf16[32,1024]{1,0:T(8,128)(2,1)S(1)} %get-tuple-element.137), channel_id=1, source_target_pairs={{0,4},{2,6},{4,0},{6,2},{1,5},{3,7},{5,1},{7,3},{8,12},{10,14},{12... | collective-permute-start | bytes 196616 | tf_op jit(solution)/shard_map/ppermute | solution.py:380
  (99 other events, 895.1 us)
Sparse Core Ops, SparseCore 0:
  20.5 49.2 all-gather.2
  71.3 25.7 all-gather.4

commit v3 on v2

--- a/solution.py
+++ b/solution.py
@@ -1,3 +1,4 @@
+import math
 from functools import partial
 
 import jax
@@ -380,22 +381,62 @@
     return lax.ppermute(member, axes, [(place, place ^ code) for place in range(count)])
 
 
+def after(member, *events):
+    return lax.optimization_barrier((member,) + events)[0]
+
+
 def like(shape, kind):
     return jax.ShapeDtypeStruct(shape, kind)
 
 
-def local(kernel, outs, place, *operands, scratch=(), flops=0):
-    whole = pl.BlockSpec(memory_space=pltpu.VMEM)
-    moved = sum(v.size * v.dtype.itemsize for v in operands)
-    moved += sum(o.size * jnp.dtype(o.dtype).itemsize for o in outs)
+def staged(kernel, n_in, n_out, keep, place, *refs):
+    given, refs = refs[:n_in], refs[n_in:]
+    results, refs = refs[:n_out], refs[n_out:]
+    held, refs = refs[:n_in], refs[n_in:]
+    if keep:
+        out, arrived, refs = results, refs[0], refs[1:]
+    else:
+        out, (arrived, left), refs = refs[:n_out], refs[n_out : n_out + 2], refs[n_out + 2 :]
+    copies = [
+        pltpu.make_async_copy(ref, held[i], arrived.at[i]) for i, ref in enumerate(given)
+    ]
+    for copy in copies:
+        copy.start()
+    for copy in copies:
+        copy.wait()
+    kernel(place, *held, *out, *refs)
+    if keep:
+        return
+    copies = [pltpu.make_async_copy(out[i], ref, left.at[i]) for i, ref in enumerate(results)]
+    for copy in copies:
+        copy.start()
+    for copy in copies:
+        copy.wait()
+
+
+def local(kernel, outs, place, *operands, scratch=(), far=False, keep=False, cost=0):
+    size = sum(math.prod(v.shape) * jnp.dtype(v.dtype).itemsize for v in operands)
+    size += sum(math.prod(v.shape) * jnp.dtype(v.dtype).itemsize for v in outs)
+    size += sum(math.prod(v.shape) * jnp.dtype(v.dtype).itemsize for v in scratch)
+    near = pl.BlockSpec(memory_space=pltpu.VMEM)
+    whole = pl.BlockSpec(memory_space=pltpu.HBM) if far else near
+    if far:
+        kernel = partial(staged, kernel, len(operands), len(outs), keep)
+        held = [pltpu.VMEM(v.shape, v.dtype) for v in (operands if keep else (*operands, *outs))]
+        signals = [pltpu.SemaphoreType.DMA((len(operands),))]
+        if not keep:
+            signals.append(pltpu.SemaphoreType.DMA((len(outs),)))
+            outs = [pltpu.HBM(v.shape, v.dtype) for v in outs]
+        scratch = held + signals + list(scratch)
+        operands = [pltpu.with_memory_space_constraint(v, pltpu.HBM) for v in operands]
     return pl.pallas_call(
         kernel,
         out_shape=list(outs),
         in_specs=[pl.BlockSpec(memory_space=pltpu.SMEM)] + [whole] * len(operands),
-        out_specs=[whole] * len(outs),
+        out_specs=[near if keep else whole] * len(outs),
         scratch_shapes=list(scratch),
-        cost_estimate=pl.CostEstimate(flops=flops, bytes_accessed=moved, transcendentals=0),
-        compiler_params=pltpu.CompilerParams(vmem_limit_bytes=48 << 20),
+        cost_estimate=pl.CostEstimate(flops=cost * 10**9, bytes_accessed=0, transcendentals=0),
+        compiler_params=pltpu.CompilerParams(vmem_limit_bytes=size + (6 << 20)),
     )(place, *operands)
 
 
@@ -425,51 +466,59 @@
             sent[code - 1][...] = total.astype(bf16)
 
 
-def group_scatter(near, far, place):
+def group_scatter(near, far, place, event=None):
     rows, width = near.shape[0] // 4, near.shape[1]
     crossed = swap(far, ("core",), 1)
+    if event is not None:
+        crossed = after(crossed, event)
     outs = [like((rows, width), f32)] + [like((rows, width), bf16)] * 3
     own, *sent = local(merge_kernel, outs, place, near, crossed)
-    return [own] + [swap(sent[code - 1], ("y", "x"), code) for code in range(1, 4)]
-
-
-def sum_over_z(parts):
-    total = parts[0].astype(f32)
-    for code in range(1, 4):
-        total = total + swap(parts[code], ("z",), code).astype(f32)
-    return total
+    parts = [own] + [swap(sent[code - 1], ("y", "x"), code) for code in range(1, 4)]
+    return parts
+
+
+def sum_over_z(near, far, event):
+    total = near.astype(f32) + after(far, event).astype(f32)
+    return total[0] + swap(total[1].astype(bf16), ("z",), 2).astype(f32)
 
 
 def ctx_gather(block):
-    line = [block] + [swap(block, ("z",), code) for code in range(1, 4)]
+    two, one = swap(block, ("z",), 2), swap(block, ("z",), 1)
+    line = [block, one, two, swap(two, ("z",), 1)]
     return [piece for member in line for piece in (member, swap(member, ("x",), 1))]
 
 
-def out_gather(block):
-    line = jnp.stack([block] + [swap(block, ("z",), code) for code in range(1, 4)])
-    both = [line, swap(line, ("y",), 1)]
-    both = jnp.stack(both)
-    far = swap(both, ("x",), 1)
-    return [both, far, swap(both, ("core",), 1), swap(far, ("core",), 1)]
-
-
-def order_kernel(place, p00, p01, p10, p11, up_ref, out_ref, up_out):
-    rows = p00.shape[2]
-    own = place[0]
-    for core in range(2):
-        for x in range(2):
-            piece = ((p00, p01), (p10, p11))[core][x]
-            for y in range(2):
-                for z in range(4):
-                    at = own ^ (y * 16 + core * 8 + z * 2 + x)
-                    out_ref[pl.ds(at * rows, rows), :] = piece[y, z]
-    for y in range(2):
-        for core in range(2):
-            for z in range(4):
-                for x in range(2):
-                    at = y * 16 + core * 8 + z * 2 + x
-                    block = up_ref[pl.ds((z * 8 + y * 4 + core * 2 + x) * rows, rows), :]
-                    up_out[pl.ds(at * rows, rows), :] = block
+def pack_kernel(place, w_qkv, w_up, *refs):
+    vectors, (b_up, segments, pads, qkv_ref, up_ref) = refs[:8], refs[8:]
+    groups, _, wide = qkv_ref.shape
+    shard, cols = w_qkv.shape[0], wide // 3
+    tags = (2 * (segments[...] + 1) + pads[...]).astype(f32)
+    lone = jnp.concatenate([v[...].astype(f32) for v in vectors], axis=0)
+    lone = jnp.concatenate([lone, jnp.zeros((8, 128 - shard), f32)], axis=1)
+    small = jnp.concatenate([lone, b_up[...].astype(f32), tags, jnp.zeros((6, 128), f32)], axis=0)
+    small = jnp.concatenate([small, jnp.zeros((16, wide - 128), f32)], axis=1).astype(bf16)
+    for c in range(groups):
+        for kind in range(3):
+            at = (kind * groups + c) * cols
+            qkv_ref[c, :shard, kind * cols : (kind + 1) * cols] = w_qkv[:, at : at + cols]
+        qkv_ref[c, shard:, :] = small
+    units = b_up.shape[1]
+    own = place[4] * 4 + place[5] * 2 + place[6]
+    for g in range(8):
+        for z in range(4):
+            at = ((g // 2 * 4 + z) * 2 + g % 2) * units
+            up_ref[own ^ g, :, z * units : (z + 1) * units] = w_up[:, at : at + units]
+
+
+def order_up_kernel(place, *refs):
+    up_refs, up_out = refs[:4], refs[4]
+    rows = up_out.shape[0] // 32
+    own, own_z = place[4] * 4 + place[5] * 2 + place[6], place[3]
+    for j in range(8):
+        group = own ^ j
+        for z in range(4):
+            at = ((group >> 1) * 4 + (own_z ^ z)) * 2 + (group & 1)
+            up_out[pl.ds(at * rows, rows), :] = up_refs[z][pl.ds(j * rows, rows), :]
 
 
 def allowed_here(query_tags, query_place, key_tags, key_place):
@@ -489,7 +538,7 @@
 ):
     blocks, refs = refs[:n_blocks], refs[n_blocks:]
     pieces, refs = refs[:4], refs[4:]
-    bias, tags_col, tags_row, q_ref, k_ref, v_ref, att_ref, msg_ref, lse_ref, qkv_ref = refs[:10]
+    bias, tags_row, q_ref, k_ref, v_ref, att_ref, msg_ref, lse_ref, qkv_ref = refs
     own_dp, own_ctx = place[1], place[2]
     shard = 32
     for m, piece in enumerate(pieces):
@@ -508,7 +557,7 @@
     def step(index, carry):
         part = pl.ds(index * chunk, chunk)
         allowed = allowed_here(
-            tags_col[part, :],
+            jnp.broadcast_to(tags_row[:, part], (128, chunk)).T[:, :1],
             places(own_ctx, rows, (chunk, 1), 0, index * chunk),
             tags_row[...],
             places(own_ctx, rows, (1, length), 1),
@@ -600,22 +649,23 @@
         target[pl.ds(pair % 2 * 2 * rows, 2 * rows), :] = cols_product(grad, up[...]).astype(bf16)
 
 
-def ff_grads_kernel(place, *refs):
-    grads, normed = refs[:8], refs[8:16]
-    active, grad_hidden, down_ref, up_ref, lines, sums = refs[16:]
-    own_z = place[3]
+def down_grad_kernel(place, *refs):
+    grads, (active, grad_hidden, parts, lines) = refs[:8], refs[8:]
     rows, width = grads[0].shape
-    units = active.shape[1]
-    shard = units // 4
+    shard = active.shape[1] // 4
     for j in range(8):
         lines[pl.ds(j * rows, rows), :] = grads[j][...]
     total = jnp.sum(grad_hidden[...].astype(f32), axis=0, keepdims=True)
     for z in range(4):
-        at = own_z ^ z
         part = slice(z * shard, (z + 1) * shard)
-        down_ref[at, :shard, :] = pair_product(active[:, part], lines[...]).astype(bf16)
-        down_ref[at, shard:, :shard] = jnp.broadcast_to(total[:, part], (16, shard)).astype(bf16)
-        down_ref[at, shard:, shard:] = jnp.zeros((16, width - shard), bf16)
+        parts[z, :shard, :] = pair_product(active[:, part], lines[...]).astype(bf16)
+        parts[z, shard:, :shard] = jnp.broadcast_to(total[:, part], (16, shard)).astype(bf16)
+        parts[z, shard:, shard:] = jnp.zeros((16, width - shard), bf16)
+
+
+def up_grad_kernel(place, *refs):
+    normed, (grad_hidden, parts, lines) = refs[:8], refs[8:]
+    rows = normed[0].shape[0]
     for j in range(8):
         lines[pl.ds(j * rows, rows), :] = normed[j][...]
     for quarter in range(4):
@@ -625,7 +675,7 @@
         for z in range(4):
             for x in range(2):
                 piece = found[(z * 2 + x) * 32 : (z * 2 + x + 1) * 32]
-                up_ref[own_z ^ z, pl.ds((quarter * 2 + x) * 32, 32), :] = piece
+                parts[z, pl.ds((quarter * 2 + x) * 32, 32), :] = piece
 
 
 def first_kernel(
@@ -650,25 +700,42 @@
     sums_ref[2:3, :] = jnp.sum(grad, axis=0, keepdims=True)
 
 
-def out_grad_kernel(place, moved, low, near, far, parts):
+def out_grad_kernel(place, moved, low, sums_one, sums_two, near, far, parts):
     groups, rows, cols = moved.shape
+    high, width = parts.shape[1:]
     own_y, own_core, own_x = place[4], place[5], place[6]
+    sums = [sums_one[0:3, :], sums_two[0:3, :], jnp.zeros((high - rows - 6, width), f32)]
+    sums = jnp.concatenate(sums, axis=0).astype(bf16)
     for c in range(groups):
         found = pair_product(moved[c], low[...]).astype(bf16)
         for m in range(4):
             y, core, z, x = c // 4, c // 2 % 2, c % 2 * 2 + m // 2, m % 2
             code = (core ^ own_core) * 4 + (y ^ own_y) * 2 + (x ^ own_x)
             parts[code, pl.ds(z * 32, 32), :] = found[m * 32 : (m + 1) * 32]
+            lanes = slice((c * 4 + m) * 32, (c * 4 + m + 1) * 32)
+            parts[code, rows:, z * 32 : (z + 1) * 32] = sums[:, lanes]
     for code in range(4):
-        near[pl.ds(code * rows, rows), :] = parts[code]
-        far[pl.ds(code * rows, rows), :] = parts[code + 4]
+        near[pl.ds(code * high, high), :] = parts[code]
+        far[pl.ds(code * high, high), :] = parts[code + 4]
+
+
+def out_line_kernel(place, own, p1, p2, p3, near, far, parts):
+    total = own[...] + p1[...].astype(f32) + p2[...].astype(f32) + p3[...].astype(f32)
+    own_z = place[3]
+    parts[...] = jnp.zeros(parts.shape, f32)
+    for z in range(4):
+        at = own_z ^ z
+        parts[at, :32, :] = total[z * 32 : (z + 1) * 32]
+        parts[at, 32:, :32] = total[128:, z * 32 : (z + 1) * 32]
+    for half in range(2):
+        near[half], far[half] = parts[2 * half], parts[2 * half + 1].astype(bf16)
 
 
 def attend_grad_kernel(
-    place, moved, q_ref, k_ref, v_ref, att_ref, lse_ref, tags_col, tags_row, qkv_ref,
-    mixed_ref, sums_ref, m0, m1, m2, m3, m4, m5, m6, m7, key_grad, value_grad, back,
+    place, *refs,
 ):
-    messages = (m0, m1, m2, m3, m4, m5, m6, m7)
+    moved, q_ref, k_ref, v_ref, att_ref, lse_ref, tags_row, *refs = refs
+    mixed_ref, key_grad, value_grad, back = refs
     groups, rows, cols = moved.shape
     length = groups * rows
     own_ctx = place[2]
@@ -677,13 +744,14 @@
     key_grad[...] = jnp.zeros(key_grad.shape, f32)
     value_grad[...] = jnp.zeros(value_grad.shape, f32)
     chunk = 2 * rows
+    tags_col = jnp.broadcast_to(tags_row[...], (128, length)).T[:, :1]
 
     def step(index, carry):
         part = pl.ds(index * chunk, chunk)
         allowed = allowed_here(
             tags_row[:, part],
             places(own_ctx, rows, (1, chunk), 1, index * chunk),
-            tags_col[...],
+            tags_col,
             places(own_ctx, rows, (length, 1), 0),
         )
         weighted = (back[part, :].astype(f32) * att_ref[part, :]).T
@@ -704,43 +772,41 @@
     lax.fori_loop(0, length // chunk, step, 0)
     mixed_ref[:, cols : 2 * cols] = (key_grad[...] * 0.125).astype(bf16)
     mixed_ref[:, 2 * cols :] = value_grad[...].astype(bf16)
-    sums_ref[...] = jnp.sum(mixed_ref[...].astype(f32), axis=0, keepdims=True)
+
+
+def leave_kernel(place, *refs):
+    mixed_ref, qkv_ref, even_near, even_far, odd_near, odd_far = refs
+    messages = ((even_near, even_far), (odd_near, odd_far))
+    groups, rows = 8, mixed_ref.shape[0] // 8
     for j in range(groups):
         part = cols_product(mixed_ref[pl.ds(j * rows, rows), :], qkv_ref[...])
-        messages[j][...] = part.astype(messages[j].dtype)
+        target = messages[j // 2 % 2][j % 2]
+        target[pl.ds(j // 4 * rows, rows), :] = part.astype(bf16)
 
 
 def qkv_grad_kernel(place, *refs):
-    blocks = refs[:8]
-    mixed, sums, near, far, lines = refs[8:]
+    blocks, (mixed_ref, near, far, lines) = refs[:8], refs[8:]
+    groups, rows = 8, blocks[0].shape[0]
+    cols = mixed_ref.shape[1] // 3
     own_dp = place[1]
-    rows = blocks[0].shape[0]
-    for j in range(8):
+    for j in range(groups):
         lines[pl.ds(j * rows, rows), :] = blocks[j][...]
+    sums = jnp.sum(mixed_ref[...].astype(f32), axis=0, keepdims=True)
+    sums = jnp.broadcast_to(sums, (16, 3 * cols)).astype(bf16)
     span = lines.shape[1] // 4
     for ky in range(2):
         for kc in range(2):
             start = pl.multiple_of((own_dp ^ (ky * 2 + kc)) * span, span)
-            found = pair_product(lines[:, pl.ds(start, span)], mixed[...]).astype(bf16)
+            found = pair_product(lines[:, pl.ds(start, span)], mixed_ref[...]).astype(bf16)
             target = far if kc else near
             target[ky, :span, :] = found
-            target[ky, span:, :] = jnp.broadcast_to(sums[...], (16, mixed.shape[1])).astype(bf16)
+            target[ky, span:, :] = sums
 
 
 def dp_sum(near, far):
     crossed = swap(far, ("core",), 1).astype(f32)
     total = near.astype(f32) + crossed
     return total[0] + swap(total[1].astype(bf16), ("y",), 1).astype(f32)
-
-
-def ctx_sum(parts):
-    line = [None] * 4
-    for code in (3, 2, 1, 0):
-        crossed = swap(parts[2 * code + 1], ("x",), 1)
-        line[code] = parts[2 * code].astype(f32) + crossed.astype(f32)
-        if code:
-            line[code] = swap(line[code].astype(bf16), ("z",), code).astype(f32)
-    return line[0] + line[1] + line[2] + line[3]
 
 
 def up_final_kernel(place, moved, out):
@@ -782,43 +848,34 @@
         [own, own_dp, own_ctx, lax.axis_index("z")] + [lax.axis_index(a) for a in GROUP]
     ).astype(jnp.int32)
 
+    vectors = (b_query, b_value, b_out, ln1_gain, ln1_bias, b_down, ln2_gain, ln2_bias)
+    qkv_parts, up_parts = local(
+        pack_kernel,
+        [like((n_ctx, shard + 16, 3 * cols), bf16), like((8, shard, wide), bf16)],
+        place, w_qkv, w_up, *[v[None] for v in vectors], b_up[None], segment_ids, pad_mask,
+        far=True,
+    )
     blocks = ctx_gather(inputs)
-    tags_here = (2 * (segment_ids[0] + 1) + pad_mask[0]).astype(bf16)
-    packed = jnp.concatenate(
-        [b_query, b_value, b_out, ln1_gain, ln1_bias, b_down, ln2_gain, ln2_bias, b_up, tags_here]
-    )
-    packed = jnp.pad(packed, (0, 6 * cols - packed.size)).reshape(2, 3 * cols)
-    qkv = w_qkv.reshape(shard, 3, n_ctx, cols).transpose(2, 0, 1, 3).reshape(n_ctx, shard, 3 * cols)
-    packed = jnp.broadcast_to(jnp.pad(packed, ((0, 14), (0, 0))), (n_ctx, 16, 3 * cols))
-    qkv = jnp.concatenate([qkv, packed], axis=1)
+    qkv = after(qkv_parts, blocks[1], blocks[2], blocks[4])
     qkv = lax.all_to_all(qkv, CTX, 0, 0, tiled=True)
-    qkv_y = swap(qkv, ("y",), 1)
-    pieces = [qkv, swap(qkv, ("core",), 1), qkv_y, swap(qkv_y, ("core",), 1)]
-    small = jnp.stack([piece[:, shard : shard + 2] for piece in pieces])
-    small = jnp.take(small, own_dp ^ jnp.arange(n_dp), axis=0).reshape(n_dp * n_ctx, 6 * cols)
-    vectors = small[:, : 8 * shard].reshape(-1, 8, shard).transpose(1, 0, 2).reshape(8, width)
-    vectors = vectors.astype(f32)
-    at = 8 * shard
-    bias_up = small[:, at : at + units].reshape(n_dp, n_z, 2, units)
+    qkv_y = swap(after(qkv, blocks[3], blocks[5]), ("y",), 1)
+    qkv_c, qkv_y = after(qkv, blocks[7]), after(qkv_y, blocks[7])
+    pieces = [qkv, swap(qkv_c, ("core",), 1), qkv_y, swap(qkv_y, ("core",), 1)]
+    up = after(up_parts, blocks[6])
+    up = [up[:1]] + [swap(up[j : j + 1], GROUP, j) for j in range(1, 8)]
+    small = jnp.stack([piece[:, shard : shard + 10, :128] for piece in pieces])
+    small = jnp.take(small, own_dp ^ jnp.arange(n_dp), axis=0).reshape(n_dp * n_ctx, 10, 128)
+    vectors = small[:, :8, :shard].transpose(1, 0, 2).reshape(8, width).astype(f32)
+    bias_up = small[:, 8].reshape(n_dp, n_z, 2, units)
     bias_up = lax.dynamic_slice(bias_up, (own_dp, 0, lax.axis_index("x"), 0), (1, n_z, 1, units))
     bias_up = bias_up.reshape(1, wide).astype(f32)
-    at += units
-    tags = small[:, at : at + rows].reshape(n_dp, n_ctx, rows)
-    tags = lax.dynamic_slice(tags, (own_dp, 0, 0), (1, n_ctx, rows))[0].astype(jnp.int32)
-    tags = jnp.take(tags, own_ctx ^ jnp.arange(n_ctx), axis=0)
-    tags_row, tags_col = tags.reshape(1, length), tags.reshape(length, 1)
+    tags = lax.dynamic_slice(small[:, 9], (own_dp * n_ctx, 0), (n_ctx, rows)).astype(jnp.int32)
+    tags_row = jnp.take(tags, own_ctx ^ jnp.arange(n_ctx), axis=0).reshape(1, length)
     bias = lax.dynamic_slice(vectors, (0, own_ctx * cols), (2, cols))
     bias = jnp.concatenate([bias[:1], jnp.zeros((1, cols), f32), bias[1:]], axis=1)
 
-    up = w_up.reshape(shard, 2, 2, n_z, 2, units).transpose(1, 2, 4, 0, 3, 5)
-    up = lax.all_to_all(up.reshape(8 * shard, wide), GROUP, 0, 0, tiled=True)
-    up = lax.all_gather(up, "z", axis=0, tiled=True)
-    down = lax.all_gather(w_down, "z", axis=0, tiled=True)
-    full_out, full_up = local(
-        order_kernel, [like((width, width), bf16), like((width, wide), bf16)], place,
-        *out_gather(w_out), up,
-    )
-
+    full_out = lax.all_gather(w_out, EVERY, axis=0, tiled=True)
+    down = lax.all_gather(after(w_down, full_out), "z", axis=0, tiled=True)
     queries, keys, values, attended, message, totals, full_qkv = local(
         partial(attend_kernel, n_blocks=n_ctx, rows=rows, cols=cols),
         [like((length, cols), bf16)] * 3
@@ -828,24 +885,31 @@
             like((8, length), f32),
             like((width, 3 * cols), bf16),
         ],
-        place, *blocks, *pieces, bias, tags_col, tags_row,
-        flops=8 * length * length * cols,
-    )
+        place, *blocks, *pieces, bias, tags_row, far=True, cost=10,
+    )
+    up = jnp.concatenate([after(up[0], message)] + up[1:]).reshape(8 * shard, wide)
+    up_z = swap(up, ("z",), 2)
+    up_lines = [up, swap(up, ("z",), 1), up_z, swap(up_z, ("z",), 1)]
     moved = lax.all_to_all(message, CTX, 0, 0, tiled=True).reshape(n_ctx, rows, cols)
     normed, normed_low, hat, rate = local(
         branch_kernel,
         [like((rows, width), f32), like((rows, width), bf16), like((rows, width), f32)]
         + [like((rows, 128), f32)],
-        place, moved, full_out, inputs, vectors, flops=2 * rows * width * width,
+        place, moved, full_out, inputs, vectors,
     )
     normed_all = group_gather(normed_low)
+    (full_up,) = local(
+        order_up_kernel, [like((width, wide), bf16)], place, after(up_lines[0], normed_all[1]),
+        *up_lines[1:], far=True, keep=True,
+    )
     hidden, active, near, far = local(
         forward_kernel,
         [like((8 * rows, wide), f32), like((8 * rows, wide), bf16)]
         + [like((4 * rows, width), bf16)] * 2,
-        place, *normed_all, full_up, bias_up, down, flops=32 * rows * width * wide,
+        place, *normed_all, full_up, bias_up, down,
     )
     parts = group_scatter(near, far, place)
+    hidden = after(hidden, parts[1])
     result, grad_second, grad_z, sums_two = local(
         second_kernel,
         [like((rows, width), bf16), like((rows, width), f32), like((rows, width), bf16)]
@@ -860,68 +924,90 @@
     grad_hidden, near, far = local(
         backward_kernel,
         [like((8 * rows, wide), bf16)] + [like((4 * rows, width), bf16)] * 2,
-        place, *grad_z_all, full_up, down, slope, flops=32 * rows * width * wide,
-    )
-    parts = group_scatter(near, far, place)
+        place, *grad_z_all, full_up, down, slope,
+    )
+    (down_parts,) = local(
+        down_grad_kernel, [like((n_z, units + 16, width), bf16)],
+        place, *grad_z_all, active, grad_hidden, far=True,
+        scratch=[pltpu.VMEM((8 * rows, width), bf16)],
+    )
+    parts = group_scatter(near, far, place, down_parts)
+    down_sum = lax.psum_scatter(
+        down_parts.reshape(-1, width), "z", scatter_dimension=0, tiled=True
+    )
+    (up_parts,) = local(
+        up_grad_kernel, [like((n_z, 8 * shard, wide), bf16)],
+        place, *normed_all, after(grad_hidden, parts[1]), far=True,
+        scratch=[pltpu.VMEM((8 * rows, width), bf16)],
+    )
+    up_sum = lax.psum_scatter(up_parts.reshape(-1, wide), "z", scatter_dimension=0, tiled=True)
     grad_first, grad_branch, message, sums_one = local(
         first_kernel,
         [like((rows, width), f32), like((rows, width), bf16), like((n_ctx, rows, cols), bf16)]
         + [like((8, width), f32)],
-        place, grad_second, *parts, vectors, hat, rate, full_out, flops=2 * rows * width * width,
+        place, after(grad_second, up_parts), *parts, vectors, hat, rate, full_out,
     )
     grad_moved = lax.all_to_all(message, CTX, 0, 0, tiled=True)
-    down_parts, up_parts = local(
-        ff_grads_kernel,
-        [like((n_z, units + 16, width), bf16), like((n_z, 8 * shard, wide), bf16)],
-        place, *grad_z_all, *normed_all, active, grad_hidden,
-        scratch=[pltpu.VMEM((8 * rows, width), bf16), pltpu.VMEM((8, 128), f32)],
-        flops=32 * rows * width * wide,
-    )
-    down_sum = sum_over_z(list(down_parts))
-    up_sum = sum_over_z(list(up_parts)).astype(bf16)
-    up_sum = lax.all_to_all(up_sum, GROUP, 0, 0, tiled=True).reshape(8, shard, wide)
-    (grad_wup,) = local(up_final_kernel, [like((shard, w_up.shape[1]), f32)], place, up_sum)
-
+    high = rows + 16
     near, far = local(
-        out_grad_kernel, [like((4 * rows, width), bf16)] * 2, place, moved, grad_branch,
-        scratch=[pltpu.VMEM((8, rows, width), bf16)], flops=2 * rows * width * width,
-    )
-    own_part, *others = group_scatter(near, far, place)
-    line = own_part + others[0].astype(f32) + others[1].astype(f32) + others[2].astype(f32)
-    line = jnp.take(line.reshape(n_z, shard, width), lax.axis_index("z") ^ jnp.arange(n_z), axis=0)
-    line = [line[0]] + list(line[1:].astype(bf16))
-    grad_wout = sum_over_z(line)
-
-    extra = jnp.concatenate([sums_one[:3], sums_two[:3]], axis=0)
-    extra = extra.reshape(6, 32, shard).transpose(1, 0, 2).reshape(32, 6 * shard)
-    extra = jnp.pad(extra, ((0, 0), (0, 2 * shard)))
-    thin = jnp.sum(lax.all_to_all(extra, EVERY, 0, 0, tiled=True), axis=0).reshape(8, shard)
-
-    mixed, sums, *messages = local(
-        attend_grad_kernel,
-        [like((length, 3 * cols), bf16), like((1, 3 * cols), f32)]
-        + [like((rows, width), bf16)] * n_ctx,
-        place, grad_moved, queries, keys, values, attended, totals, tags_col, tags_row, full_qkv,
+        out_grad_kernel, [like((4 * high, width), bf16)] * 2, place, moved, grad_branch, sums_one,
+        sums_two, far=True, scratch=[pltpu.VMEM((8, high, width), bf16)],
+    )
+    out_sent, *out_parts = group_scatter(near, far, place)
+    out_parts = [out_sent] + out_parts
+
+    (mixed,) = local(
+        attend_grad_kernel, [like((length, 3 * cols), bf16)],
+        place, after(grad_moved, out_sent), queries, keys, values, attended, totals, tags_row,
+        far=True, cost=14,
         scratch=[
             pltpu.VMEM((length, cols), f32),
             pltpu.VMEM((length, cols), f32),
             pltpu.VMEM((length, cols), bf16),
         ],
-        flops=20 * length * length * cols,
-    )
-    grad_inputs = grad_first + ctx_sum(messages)
+    )
+    mixed = after(mixed, *out_parts)
+    even_near, even_far, odd_near, odd_far = local(
+        leave_kernel, [like((2 * rows, width), bf16)] * 4, place, mixed, full_qkv, far=True,
+        cost=3,
+    )
     near, far = local(
-        qkv_grad_kernel, [like((2, width // 4 + 16, 3 * cols), bf16)] * 2, place, *blocks, mixed,
-        sums, scratch=[pltpu.VMEM((length, width), bf16)], flops=6 * length * width * cols,
-    )
+        qkv_grad_kernel, [like((2, width // 4 + 16, 3 * cols), bf16)] * 2,
+        place, *blocks, after(mixed, odd_near), far=True, cost=4,
+        scratch=[pltpu.VMEM((length, width), bf16)],
+    )
+    odd_far = swap(odd_far, ("x",), 1)
+    even_far = swap(after(even_far, odd_far), ("x",), 1)
+    near = after(near, odd_far)
+    odd = odd_near.astype(f32) + odd_far.astype(f32)
+    even = even_near.astype(f32) + even_far.astype(f32)
+    even = even + swap(odd.astype(bf16), ("z",), 1).astype(f32)
+    final = swap(even[rows:].astype(bf16), ("z",), 2)
+    grad_inputs = grad_first + even[:rows] + final.astype(f32)
+
     qkv_sum = dp_sum(near, far)
     qkv_rows = qkv_sum[: n_ctx * shard].reshape(n_ctx, shard, 3 * cols)
     qkv_bias = jnp.broadcast_to(qkv_sum[n_ctx * shard :], (n_ctx, 16, 3 * cols))
     qkv_sum = jnp.concatenate([qkv_rows, qkv_bias], axis=1).astype(bf16)
     qkv_sum = lax.all_to_all(qkv_sum, CTX, 0, 0, tiled=True)
-    (grad_wqkv,) = local(qkv_final_kernel, [like((shard, 3 * width), f32)], place, qkv_sum)
+    (grad_wqkv,) = local(
+        qkv_final_kernel, [like((shard, 3 * width), f32)], place, qkv_sum, far=True
+    )
     bias_sum = qkv_sum[:, shard].reshape(n_ctx, 3, cols).transpose(1, 0, 2).reshape(3, width)
     bias_own = lax.dynamic_slice(bias_sum, (0, own * shard), (3, shard)).astype(f32)
+
+    out_near, out_far = local(
+        out_line_kernel, [like((2, shard + 16, width), f32), like((2, shard + 16, width), bf16)],
+        place, after(out_parts[0], odd_far), *out_parts[1:],
+        scratch=[pltpu.VMEM((4, shard + 16, width), f32)],
+    )
+    up_sum = after(up_sum, odd_far)
+    up_sum = lax.all_to_all(up_sum, GROUP, 0, 0, tiled=True).reshape(8, shard, wide)
+    (grad_wup,) = local(
+        up_final_kernel, [like((shard, w_up.shape[1]), f32)], place, up_sum, far=True
+    )
+    out_sum = sum_over_z(out_near, swap(out_far, ("z",), 1), odd_far)
+    thin = out_sum[shard:, :shard]
 
     return (
         result[None],
@@ -929,13 +1015,13 @@
         grad_wqkv,
         bias_own[0],
         bias_own[2],
-        grad_wout,
+        out_sum[:shard],
         thin[0],
         thin[1],
         thin[2],
         grad_wup,
-        down_sum[units, :units],
-        down_sum[:units],
+        down_sum[units, :units].astype(f32),
+        down_sum[:units].astype(f32),
         thin[3],
         thin[4],
         thin[5],

time: 401 us -> 314 us (0.78)
  waiting for transfers between devices: 173 us -> 112 us
  local copies, waits for them, and re-layouts: 41.1 us -> 21.1 us
  Pallas kernels: 58 us -> 75.3 us
  blocking collectives: 11.5 us -> 0 us
  starting transfers between devices: 87.6 us -> 79.2 us
    ppermute x61 -> x54, waiting for transfers between devices: 128 us -> 72.2 us  [swap(): lax.ppermute(member, axes, [(place, place ^ code) for place in range(coun...]
    all_to_all x1, waiting for transfers between devices: 29.4 us -> 0.01 us  [heads_body(): qkv = lax.all_to_all(qkv, CTX, 0, 0, tiled=True)]
    pallas_call x16 -> x20, Pallas kernels: 58 us -> 75.3 us  [local(): pl.pallas_call(kernel, out_shape=list(outs), in_specs=[pl.BlockSpec(memor...]
    unnamed x159 -> x132, local copies, waits for them, and re-layouts: 30.8 us -> 16.7 us
    all_to_all x1 -> x0, blocking collectives: 11.5 us -> none  [heads_body(): up = lax.all_to_all(up.reshape(8 * shard, wide), GROUP, 0, 0, tiled=True)]
    all_gather x2, waiting for transfers between devices: 0.03 us -> 9.1 us  [the longest x1 9.1 us: heads_body(): full_out = lax.all_gather(w_out, EVERY, axis=0, tiled=True)]
    ppermute x61 -> x54, starting transfers between devices: 63.8 us -> 56.1 us  [swap(): lax.ppermute(member, axes, [(place, place ^ code) for place in range(coun...]
    all_to_all x1, waiting for transfers between devices: 0.01 us -> 7.44 us  [heads_body(): qkv_sum = lax.all_to_all(qkv_sum, CTX, 0, 0, tiled=True)]
  transfers between devices with their start and end apart: 69 -> 63, of which waited for: 25 -> 26; matrix products, arithmetic and copies ran while one was open for 5% -> 4% of each run, Pallas kernels for 11% -> 21%
where the time goes in v3:
time: 314 us; the launch traced here: 313 us
  waiting for transfers between devices  112 us (36%)
  starting transfers between devices  79.2 us (25%)
  Pallas kernels  75.3 us (24%)
  local copies, waits for them, and re-layouts  21.1 us (7%)
  between operations  14.8 us (5%)
  other arithmetic  10.3 us (3%)
    pallas_call x20, Pallas kernels, local(): pl.pallas_call(kernel, out_shape=list(outs), in_specs=[pl.BlockSpec(memor...  75.3 us
    ppermute x54, waiting for transfers between devices, swap(): lax.ppermute(member, axes, [(place, place ^ code) for place in range(coun...  72.2 us
    ppermute x54, starting transfers between devices, swap(): lax.ppermute(member, axes, [(place, place ^ code) for place in range(coun...  56.1 us
    unnamed x132, local copies, waits for them, and re-layouts  16.7 us
    all_to_all x1, waiting for transfers between devices, heads_body(): lax.all_to_all(message, CTX, 0, 0, tiled=True).reshape(n_ctx, rows, cols)  12.7 us
    all_gather x1, waiting for transfers between devices, heads_body(): full_out = lax.all_gather(w_out, EVERY, axis=0, tiled=True)  9.1 us
    all_to_all x1, waiting for transfers between devices, heads_body(): qkv_sum = lax.all_to_all(qkv_sum, CTX, 0, 0, tiled=True)  7.44 us
    all_to_all x1, waiting for transfers between devices, heads_body(): grad_moved = lax.all_to_all(message, CTX, 0, 0, tiled=True)  6.6 us
  transfers between devices with their start and end apart: 63, of which 26 were waited for; matrix products, arithmetic and copies ran while one was open for 4% of the time, Pallas kernels for 21%

profile of v3, /device:TPU:0, one launch (start us, length us, event | category | flops | bytes accessed | tf_op | source)
XLA Modules:
  0.0 312.9 jit_solution(13473232991530666290)
XLA Ops:
  7.9 4.1 %collective-permute-start.3 = (bf16[128,1024]{1,0:T(8,128)(2,1)}, bf16[128,1024]{1,0:T(8,128)(2,1)S(1)}, u32[]{:S(2)}, u32[]{:S(2)}) collective-permute-start(bf16[128,1024]{1,0:T(8,128)(2,1)} %bitcast.91), channel_id=1, source_target_pairs={{0,4},{2,6},{4,0},{6,2},{1,5},{3,7},{5,1},{7,3},{8,12},{10,14},{12... | collective-permute-start | bytes 786440 | tf_op jit(solution)/shard_map/ppermute | solution.py:381
  15.2 2.6 shard_map.280
  17.8 6.5 %collective-permute-done.3.refs_4_ = bf16[128,1024]{1,0:T(8,128)(2,1)S(1)} collective-permute-done((bf16[128,1024]{1,0:T(8,128)(2,1)}, bf16[128,1024]{1,0:T(8,128)(2,1)S(1)}, u32[]{:S(2)}, u32[]{:S(2)}) %collective-permute-start.3) | collective-permute-done | bytes 262176 | tf_op jit(solution)/shard_map/ppermute | solution.py:381
  24.5 5.6 %all-to-all-start = ((bf16[8,48,384]{2,1,0:T(8,128)(2,1)}), bf16[8,48,384]{2,1,0:T(8,128)(2,1)S(1)}, u32[]{:S(2)}, u32[]{:S(2)}) async-start(bf16[8,48,384]{2,1,0:T(8,128)(2,1)} %get-tuple-element.86), calls=%async_computation | async-start | bytes 589824 | tf_op jit(solution)/shard_map/all_to_all | solution.py:860
  30.1 2.0 collective-permute-start.5
  34.2 9.8 %collective-permute-done.5.refs_6_ = bf16[128,1024]{1,0:T(8,128)(2,1)S(1)} collective-permute-done((bf16[128,1024]{1,0:T(8,128)(2,1)S(1)}, bf16[128,1024]{1,0:T(8,128)(2,1)S(1)}, u32[]{:S(2)}, u32[]{:S(2)}) %collective-permute-start.5) | collective-permute-done | bytes 262176 | tf_op jit(solution)/shard_map/ppermute | solution.py:381
  45.7 4.7 %collective-permute-done.2.refs_3_ = bf16[128,1024]{1,0:T(8,128)(2,1)S(1)} collective-permute-done((bf16[128,1024]{1,0:T(8,128)(2,1)S(1)}, bf16[128,1024]{1,0:T(8,128)(2,1)S(1)}, u32[]{:S(2)}, u32[]{:S(2)}) %collective-permute-start.2) | collective-permute-done | bytes 262176 | tf_op jit(solution)/shard_map/ppermute | solution.py:381
  52.0 3.2 %collective-permute-done.6.refs_7_ = bf16[128,1024]{1,0:T(8,128)(2,1)S(1)} collective-permute-done((bf16[128,1024]{1,0:T(8,128)(2,1)S(1)}, bf16[128,1024]{1,0:T(8,128)(2,1)S(1)}, u32[]{:S(2)}, u32[]{:S(2)}) %collective-permute-start.6) | collective-permute-done | bytes 262176 | tf_op jit(solution)/shard_map/ppermute | solution.py:381
  56.3 1.8 collective-permute-start.23
  58.2 2.3 collective-permute-start.21
  65.6 9.1 %all-gather.3.cloned.1.call-done.w_out = bf16[1024,1024]{1,0:T(8,128)(2,1)} async-done(((bf16[32,1024]{1,0:T(8,128)(2,1)}), bf16[1024,1024]{1,0:T(8,128)(2,1)}) %all-gather.3.cloned.1.call-update) | async-done | bytes 2097168 | tf_op jit(solution)/shard_map/all_gather | solution.py:877
  74.7 12.9 %shard_map.281 = (bf16[1024,128]{1,0:T(8,128)(2,1)}, bf16[1024,128]{1,0:T(8,128)(2,1)}, bf16[1024,128]{1,0:T(8,128)(2,1)}, f32[1024,128]{1,0:T(8,128)}, bf16[102...) custom-call(s32[7]{0:T(128)S(1)} %stack.46.place, bf16[128,1024]{1,0:T(8,128)(2,1)} %bitcast.94, ...), custom_call_target="tpu_custom_call" | custom-call | flops 10000000000 | tf_op jit(solution)/shard_map/pallas_call | solution.py:432
  87.7 4.1 %all-to-all-start.1 = ((bf16[8,128,128]{2,1,0:T(8,128)(2,1)}), bf16[8,128,128]{2,1,0:T(8,128)(2,1)S(1)}, u32[]{:S(2)}, u32[]{:S(2)}) async-start(bf16[8,128,128]{2,1,0:T(8,128)(2,1)} %bitcast.106), calls=%async_computation.1 | async-start | bytes 524288 | tf_op jit(solution)/shard_map/all_to_all | solution.py:893
  96.5 3.1 collective-permute-start.25
  101.1 12.7 %all-to-all-done.1.moved.refs_0_ = bf16[8,128,128]{2,1,0:T(8,128)(2,1)S(1)} async-done(((bf16[8,128,128]{2,1,0:T(8,128)(2,1)}), bf16[8,128,128]{2,1,0:T(8,128)(2,1)S(1)}, u32[]{:S(2)}, u32[]{:S(2)}) %all-to-all-start.1) | async-done | bytes 262176 | tf_op jit(solution)/shard_map/all_to_all | solution.py:893
  113.8 2.2 shard_map.282
  118.3 2.1 collective-permute-start.11
  121.2 5.9 %collective-permute-done.12.refs_3_ = bf16[128,1024]{1,0:T(8,128)(2,1)} collective-permute-done((bf16[128,1024]{1,0:T(8,128)(2,1)}, bf16[128,1024]{1,0:T(8,128)(2,1)}, u32[]{:S(2)}, u32[]{:S(2)}) %collective-permute-start.12) | collective-permute-done | bytes 262176 | tf_op jit(solution)/shard_map/ppermute | solution.py:381
  127.1 2.7 collective-permute-done.11.refs_2_
  131.0 1.8 shard_map.283.refs_8_
  140.8 4.1 %shard_map.284 = (f32[1024,512]{1,0:T(8,128)S(1)}, bf16[1024,512]{1,0:T(8,128)(2,1)S(1)}, bf16[512,1024]{1,0:T(8,128)(2,1)S(1)}, bf16[512,1024]{1,0:T(8,128)(2,1)S(1)}) custom-call(s32[7]{0:T(128)S(1)} %stack.46.place, bf16[128,1024]{1,0:T(8,128)(2,1)} %get-tuple-element.92.refs_0_, bf16[128,1024]{1,0:T(8,128)(2,1)} %collective-permute-done.10.refs_1_, ...), custom_call_target="tpu_custom_call" | custom-call | tf_op jit(solution)/shard_map/pallas_call | solution.py:432
  145.0 2.6 collective-permute-done.27.far
  150.2 1.7 collective-permute-start.30
  152.0 5.7 %collective-permute-done.28.p1 = bf16[128,1024]{1,0:T(8,128)(2,1)S(1)} collective-permute-done((bf16[128,1024]{1,0:T(8,128)(2,1)S(1)}, bf16[128,1024]{1,0:T(8,128)(2,1)S(1)}, u32[]{:S(2)}, u32[]{:S(2)}) %collective-permute-start.28) | collective-permute-done | bytes 262176 | tf_op jit(solution)/shard_map/ppermute | solution.py:381
  157.6 5.2 %collective-permute-done.29.p2 = bf16[128,1024]{1,0:T(8,128)(2,1)S(1)} collective-permute-done((bf16[128,1024]{1,0:T(8,128)(2,1)S(1)}, bf16[128,1024]{1,0:T(8,128)(2,1)S(1)}, u32[]{:S(2)}, u32[]{:S(2)}) %collective-permute-start.29) | collective-permute-done | bytes 262176 | tf_op jit(solution)/shard_map/ppermute | solution.py:381
  168.1 6.7 %collective-permute-done.33.refs_3_ = bf16[128,1024]{1,0:T(8,128)(2,1)S(1)} collective-permute-done((bf16[128,1024]{1,0:T(8,128)(2,1)S(1)}, bf16[128,1024]{1,0:T(8,128)(2,1)S(1)}, u32[]{:S(2)}, u32[]{:S(2)}) %collective-permute-start.33) | collective-permute-done | bytes 262176 | tf_op jit(solution)/shard_map/ppermute | solution.py:381
  174.8 3.7 %collective-permute-done.32.refs_2_ = bf16[128,1024]{1,0:T(8,128)(2,1)S(1)} collective-permute-done((bf16[128,1024]{1,0:T(8,128)(2,1)S(1)}, bf16[128,1024]{1,0:T(8,128)(2,1)S(1)}, u32[]{:S(2)}, u32[]{:S(2)}) %collective-permute-start.32) | collective-permute-done | bytes 262176 | tf_op jit(solution)/shard_map/ppermute | solution.py:381
  180.4 4.3 %shard_map.287 = (bf16[1024,512]{1,0:T(8,128)(2,1)S(1)}, bf16[512,1024]{1,0:T(8,128)(2,1)S(1)}, bf16[512,1024]{1,0:T(8,128)(2,1)}) custom-call(s32[7]{0:T(128)S(1)} %stack.46.place, bf16[128,1024]{1,0:T(8,128)(2,1)S(1)} %get-tuple-element.106.refs_0_, bf16[128,1024]{1,0:T(8,128)(2,1)S(1)} %collective-permute-done.31.refs_1_, ...), custom_call_target="tpu_custom_call" | custom-call | tf_op jit(solution)/shard_map/pallas_call | solution.py:432
  185.8 5.1 %shard_map.288 = bf16[4,144,1024]{2,1,0:T(8,128)(2,1)} custom-call(s32[7]{0:T(128)S(1)} %stack.46.place, bf16[128,1024]{1,0:T(8,128)(2,1)} %copy-done.13, bf16[128,1024]{1,0:T(8,128)(2,1)} %copy-done.16, bf16[128,1024]{1,0:T(8,128)(2,1)} %copy-done.15, bf16[128,1024]{1,0:T(8,128)(2,1)} %copy-done.14, bf16[128,1024]{1,0:T(8,128)(2,1)} %copy-done.17, ...), custom_call_target="tpu_custom_call" | custom-call | tf_op jit(solution)/shard_map/pallas_call | solution.py:432
  196.6 5.6 %collective-permute-done.39.p1 = bf16[128,1024]{1,0:T(8,128)(2,1)S(1)} collective-permute-done((bf16[128,1024]{1,0:T(8,128)(2,1)S(1)}, bf16[128,1024]{1,0:T(8,128)(2,1)S(1)}, u32[]{:S(2)}, u32[]{:S(2)}) %collective-permute-start.39) | collective-permute-done | bytes 262176 | tf_op jit(solution)/shard_map/ppermute | solution.py:381
  202.2 4.8 %shard_map.290 = bf16[4,256,512]{2,1,0:T(8,128)(2,1)} custom-call(s32[7]{0:T(128)S(1)} %stack.46.place, bf16[128,1024]{1,0:T(8,128)(2,1)} %get-tuple-element.92.refs_0_, bf16[128,1024]{1,0:T(8,128)(2,1)} %collective-permute-done.10.refs_1_, bf16[128,1024]{1,0:T(8,128)(2,1)} %collective-permute-done.11.refs_2_, ...), custom_call_target="tpu_custom_call" | custom-call | tf_op jit(solution)/shard_map/pallas_call | solution.py:432
  208.5 2.4 shard_map.291
  212.2 3.9 %shard_map.292 = (bf16[576,1024]{1,0:T(8,128)(2,1)}, bf16[576,1024]{1,0:T(8,128)(2,1)}) custom-call(s32[7]{0:T(128)S(1)} %stack.46.place, bf16[8,128,128]{2,1,0:T(8,128)(2,1)} %copy-done.3, bf16[128,1024]{1,0:T(8,128)(2,1)} %copy-done.34, f32[8,1024]{1,0:T(8,128)} %copy-done.36, f32[8,1024]{1,0:T(8,128)} %copy-done.35), custom_call_target="tpu_custom_call" | custom-call | tf_op jit(solution)/shard_map/pallas_call | solution.py:432
  216.2 3.9 %all-to-all-start.2 = ((bf16[8,128,128]{2,1,0:T(8,128)(2,1)}), bf16[8,128,128]{2,1,0:T(8,128)(2,1)S(1)}, u32[]{:S(2)}, u32[]{:S(2)}) async-start(bf16[8,128,128]{2,1,0:T(8,128)(2,1)} %get-tuple-element.123), calls=%async_computation.2 | async-start | bytes 524288 | tf_op jit(solution)/shard_map/all_to_all | solution.py:950
  223.0 6.6 %all-to-all-done.2.refs_0_ = bf16[8,128,128]{2,1,0:T(8,128)(2,1)S(1)} async-done(((bf16[8,128,128]{2,1,0:T(8,128)(2,1)}), bf16[8,128,128]{2,1,0:T(8,128)(2,1)S(1)}, u32[]{:S(2)}, u32[]{:S(2)}) %all-to-all-start.2) | async-done | bytes 262176 | tf_op jit(solution)/shard_map/all_to_all | solution.py:950
  233.0 12.2 %shard_map.294.refs_0_.refs_8_ = bf16[1024,384]{1,0:T(8,128)(2,1)} custom-call(s32[7]{0:T(128)S(1)} %stack.46.place, bf16[8,128,128]{2,1,0:T(8,128)(2,1)} %copy-done.51, bf16[1024,128]{1,0:T(8,128)(2,1)} %get-tuple-element.131.refs_1_, bf16[1024,128]{1,0:T(8,128)(2,1)} %get-tuple-element.132.refs_2_, bf16[1024,128]{1,0:T(8,128)(2,1)} %get-tuple-element.133.refs_3_, ...), custom_call_target="tpu_custom_call" | custom-call | flops 14000000000 | tf_op jit(solution)/shard_map/pallas_call | solution.py:432
  245.3 4.9 %shard_map.295 = (bf16[256,1024]{1,0:T(8,128)(2,1)}, bf16[256,1024]{1,0:T(8,128)(2,1)}, bf16[256,1024]{1,0:T(8,128)(2,1)}, bf16[256,1024]{1,0:T(8,128)(2,1)}) custom-call(s32[7]{0:T(128)S(1)} %stack.46.place, bf16[1024,384]{1,0:T(8,128)(2,1)} %shard_map.294.refs_0_.refs_8_, bf16[1024,384]{1,0:T(8,128)(2,1)} %get-tuple-element.140.refs_1_), custom_call_target="tpu_custom_call" | custom-call | flops 3000000000 | tf_op jit(solution)/shard_map/pallas_call | solution.py:432
  251.6 4.7 %shard_map.296 = (bf16[2,272,384]{2,1,0:T(8,128)(2,1)}, bf16[2,272,384]{2,1,0:T(8,128)(2,1)}) custom-call(s32[7]{0:T(128)S(1)} %stack.46.place, bf16[128,1024]{1,0:T(8,128)(2,1)} %bitcast.95, bf16[128,1024]{1,0:T(8,128)(2,1)} %copy-done.57, bf16[128,1024]{1,0:T(8,128)(2,1)} %copy-done.56, bf16[128,1024]{1,0:T(8,128)(2,1)} %copy-done.60, ...), custom_call_target="tpu_custom_call" | custom-call | flops 4000000000 | tf_op jit(solution)/shard_map/pallas_call | solution.py:432
  257.6 1.9 slice_convert_fusion.3
  259.5 2.6 collective-permute-done.46
  268.4 3.4 %all-to-all-start.4 = ((bf16[8,32,512]{2,1,0:T(8,128)(2,1)}), bf16[8,32,512]{2,1,0:T(8,128)(2,1)S(1)}, u32[]{:S(2)}, u32[]{:S(2)}) async-start(bf16[8,32,512]{2,1,0:T(8,128)(2,1)} %bitcast.105), calls=%async_computation.5 | async-start | bytes 524288 | tf_op jit(solution)/shard_map/all_to_all | solution.py:1005
  272.8 2.5 collective-permute-start.53
  276.2 3.0 all-to-all-done.4.refs_0_
  279.2 5.9 %all-to-all-start.3 = ((bf16[8,48,384]{2,1,0:T(8,128)(2,1)}), bf16[8,48,384]{2,1,0:T(8,128)(2,1)S(1)}, u32[]{:S(2)}, u32[]{:S(2)}) async-start(bf16[8,48,384]{2,1,0:T(8,128)(2,1)} %pad_maximum_fusion), calls=%async_computation.3 | async-start | bytes 589824 | tf_op jit(solution)/shard_map/all_to_all | solution.py:992
  286.4 2.3 shard_map.299
  290.2 3.0 collective-permute-start.49
  293.1 7.4 %all-to-all-done.3.refs_0_ = bf16[8,48,384]{2,1,0:T(8,128)(2,1)S(1)} async-done(((bf16[8,48,384]{2,1,0:T(8,128)(2,1)}), bf16[8,48,384]{2,1,0:T(8,128)(2,1)S(1)}, u32[]{:S(2)}, u32[]{:S(2)}) %all-to-all-start.3) | async-done | bytes 294944 | tf_op jit(solution)/shard_map/all_to_all | solution.py:992
  301.3 2.3 shard_map.297
  (287 shorter events, 76.7 us)
Async XLA Ops:
  7.2 67.5 %all-gather.3.cloned.1.call-start = ((), (), s32[]{:S(2)}) async-start(), calls=%async_computation.7 | async-start | bytes 2162688 | tf_op jit(solution)/shard_map/all_gather | solution.py:877
  7.9 16.3 %collective-permute-start.3 = (bf16[128,1024]{1,0:T(8,128)(2,1)}, bf16[128,1024]{1,0:T(8,128)(2,1)S(1)}, u32[]{:S(2)}, u32[]{:S(2)}) collective-permute-start(bf16[128,1024]{1,0:T(8,128)(2,1)} %bitcast.91), channel_id=1, source_target_pairs={{0,4},{2,6},{4,0},{6,2},{1,5},{3,7},{5,1},{7,3},{8,12},{10,14},{12... | collective-permute-start | bytes 786440 | tf_op jit(solution)/shard_map/ppermute | solution.py:381
  12.0 12.4 %collective-permute-start.1 = (bf16[128,1024]{1,0:T(8,128)(2,1)}, bf16[128,1024]{1,0:T(8,128)(2,1)S(1)}, u32[]{:S(2)}, u32[]{:S(2)}) collective-permute-start(bf16[128,1024]{1,0:T(8,128)(2,1)} %bitcast.92), channel_id=1, source_target_pairs={{0,2},{2,0},{4,6},{6,4},{1,3},{3,1},{5,7},{7,5},{8,10},{10,8},{12,... | collective-permute-start | bytes 786440 | tf_op jit(solution)/shard_map/ppermute | solution.py:381
  13.6 10.9 %collective-permute-start = (bf16[128,1024]{1,0:T(8,128)(2,1)}, bf16[128,1024]{1,0:T(8,128)(2,1)S(1)}, u32[]{:S(2)}, u32[]{:S(2)}) collective-permute-start(bf16[128,1024]{1,0:T(8,128)(2,1)} %bitcast.93), channel_id=1, source_target_pairs={{0,1},{1,0},{2,3},{3,2},{4,5},{5,4},{6,7},{7,6},{8,9},{9,8},{10,11... | collective-permute-start | bytes 786440 | tf_op jit(solution)/shard_map/ppermute | solution.py:381
  24.5 25.9 %all-to-all-start = ((bf16[8,48,384]{2,1,0:T(8,128)(2,1)}), bf16[8,48,384]{2,1,0:T(8,128)(2,1)S(1)}, u32[]{:S(2)}, u32[]{:S(2)}) async-start(bf16[8,48,384]{2,1,0:T(8,128)(2,1)} %get-tuple-element.86), calls=%async_computation | async-start | bytes 589824 | tf_op jit(solution)/shard_map/all_to_all | solution.py:860
  30.1 105.7 %all-gather.5.cloned.1.call-start = ((), (), s32[]{:S(2)}) async-start(), calls=%async_computation.8 | async-start | bytes 1310720 | tf_op jit(solution)/shard_map/all_gather | solution.py:878
  30.1 13.9 %collective-permute-start.5 = (bf16[128,1024]{1,0:T(8,128)(2,1)S(1)}, bf16[128,1024]{1,0:T(8,128)(2,1)S(1)}, u32[]{:S(2)}, u32[]{:S(2)}) collective-permute-start(bf16[128,1024]{1,0:T(8,128)(2,1)S(1)} %collective-permute-done.3.refs_4_), channel_id=1, source_target_pairs={{0,2},{2,0},{4,6},{6,4},{1,3},{3,1},{5,7},{7,5},{8,10},{10,8},{12,... | collective-permute-start | bytes 786440 | tf_op jit(solution)/shard_map/ppermute | solution.py:381
  32.1 13.6 %collective-permute-start.4 = (bf16[128,1024]{1,0:T(8,128)(2,1)S(1)}, bf16[128,1024]{1,0:T(8,128)(2,1)S(1)}, u32[]{:S(2)}, u32[]{:S(2)}) collective-permute-start(bf16[128,1024]{1,0:T(8,128)(2,1)S(1)} %collective-permute-done.3.refs_4_), channel_id=1, source_target_pairs={{0,1},{1,0},{2,3},{3,2},{4,5},{5,4},{6,7},{7,6},{8,9},{9,8},{10,11... | collective-permute-start | bytes 786440 | tf_op jit(solution)/shard_map/ppermute | solution.py:381
  33.6 16.8 %collective-permute-start.2 = (bf16[128,1024]{1,0:T(8,128)(2,1)S(1)}, bf16[128,1024]{1,0:T(8,128)(2,1)S(1)}, u32[]{:S(2)}, u32[]{:S(2)}) collective-permute-start(bf16[128,1024]{1,0:T(8,128)(2,1)S(1)} %collective-permute-done.1.refs_2_), channel_id=1, source_target_pairs={{0,1},{1,0},{2,3},{3,2},{4,5},{5,4},{6,7},{7,6},{8,9},{9,8},{10,11... | collective-permute-start | bytes 786440 | tf_op jit(solution)/shard_map/ppermute | solution.py:381
  44.0 11.2 %collective-permute-start.6 = (bf16[128,1024]{1,0:T(8,128)(2,1)S(1)}, bf16[128,1024]{1,0:T(8,128)(2,1)S(1)}, u32[]{:S(2)}, u32[]{:S(2)}) collective-permute-start(bf16[128,1024]{1,0:T(8,128)(2,1)S(1)} %collective-permute-done.5.refs_6_), channel_id=1, source_target_pairs={{0,1},{1,0},{2,3},{3,2},{4,5},{5,4},{6,7},{7,6},{8,9},{9,8},{10,11... | collective-permute-start | bytes 786440 | tf_op jit(solution)/shard_map/ppermute | solution.py:381
  50.4 10.2 %collective-permute-start.8 = (bf16[8,48,384]{2,1,0:T(8,128)(2,1)S(1)}, bf16[8,48,384]{2,1,0:T(8,128)(2,1)S(1)}, u32[]{:S(2)}, u32[]{:S(2)}) collective-permute-start(bf16[8,48,384]{2,1,0:T(8,128)(2,1)S(1)} %all-to-all-done.refs_8_), channel_id=1, source_target_pairs={{0,16},{16,0},{1,17},{17,1},{2,18},{18,2},{3,19},{19,3},{4,20},{20... | collective-permute-start | bytes 884744 | tf_op jit(solution)/shard_map/ppermute | solution.py:381
  56.3 40.2 %collective-permute-start.23 = (bf16[1,32,512]{2,1,0:T(8,128)(2,1)S(1)}, bf16[1,32,512]{2,1,0:T(8,128)(2,1)S(1)}, u32[]{:S(2)}, u32[]{:S(2)}) collective-permute-start(bf16[1,32,512]{2,1,0:T(8,128)(2,1)S(1)} %get-tuple-element.155), channel_id=1, source_target_pairs={{0,25},{1,24},{8,17},{9,16},{16,9},{17,8},{24,1},{25,0},{2,27},{3,... | collective-permute-start | bytes 98312 | tf_op jit(solution)/shard_map/ppermute | solution.py:381
  58.1 38.4 %collective-permute-start.22 = (bf16[1,32,512]{2,1,0:T(8,128)(2,1)S(1)}, bf16[1,32,512]{2,1,0:T(8,128)(2,1)S(1)}, u32[]{:S(2)}, u32[]{:S(2)}) collective-permute-start(bf16[1,32,512]{2,1,0:T(8,128)(2,1)S(1)} %get-tuple-element.156), channel_id=1, source_target_pairs={{0,24},{1,25},{8,16},{9,17},{16,8},{17,9},{24,0},{25,1},{2,26},{3,... | collective-permute-start | bytes 98312 | tf_op jit(solution)/shard_map/ppermute | solution.py:381
  58.2 38.2 %collective-permute-start.21 = (bf16[1,32,512]{2,1,0:T(8,128)(2,1)S(1)}, bf16[1,32,512]{2,1,0:T(8,128)(2,1)S(1)}, u32[]{:S(2)}, u32[]{:S(2)}) collective-permute-start(bf16[1,32,512]{2,1,0:T(8,128)(2,1)S(1)} %get-tuple-element.157), channel_id=1, source_target_pairs={{0,17},{1,16},{8,25},{9,24},{16,1},{17,0},{24,9},{25,8},{2,19},{3,... | collective-permute-start | bytes 98312 | tf_op jit(solution)/shard_map/ppermute | solution.py:381
  60.8 35.7 %collective-permute-start.20 = (bf16[1,32,512]{2,1,0:T(8,128)(2,1)S(1)}, bf16[1,32,512]{2,1,0:T(8,128)(2,1)S(1)}, u32[]{:S(2)}, u32[]{:S(2)}) collective-permute-start(bf16[1,32,512]{2,1,0:T(8,128)(2,1)S(1)} %get-tuple-element.158), channel_id=1, source_target_pairs={{0,16},{1,17},{8,24},{9,25},{16,0},{17,1},{24,8},{25,9},{2,18},{3,... | collective-permute-start | bytes 98312 | tf_op jit(solution)/shard_map/ppermute | solution.py:381
  62.1 29.6 %collective-permute-start.17 = (bf16[1,32,512]{2,1,0:T(8,128)(2,1)S(1)}, bf16[1,32,512]{2,1,0:T(8,128)(2,1)S(1)}, u32[]{:S(2)}, u32[]{:S(2)}) collective-permute-start(bf16[1,32,512]{2,1,0:T(8,128)(2,1)S(1)} %get-tuple-element.161), channel_id=1, source_target_pairs={{0,1},{1,0},{8,9},{9,8},{16,17},{17,16},{24,25},{25,24},{2,3},{3,2... | collective-permute-start | bytes 98312 | tf_op jit(solution)/shard_map/ppermute | solution.py:381
  87.7 26.1 %all-to-all-start.1 = ((bf16[8,128,128]{2,1,0:T(8,128)(2,1)}), bf16[8,128,128]{2,1,0:T(8,128)(2,1)S(1)}, u32[]{:S(2)}, u32[]{:S(2)}) async-start(bf16[8,128,128]{2,1,0:T(8,128)(2,1)} %bitcast.106), calls=%async_computation.1 | async-start | bytes 524288 | tf_op jit(solution)/shard_map/all_to_all | solution.py:893
  91.7 164.7 %reduce-scatter.5.cloned.1.call-start = ((), (), s32[]{:S(2)}) async-start(), calls=%async_computation.10 | async-start | bytes 1474560 | tf_op jit(solution)/shard_map/reduce_scatter | solution.py:935
  96.5 24.6 %collective-permute-start.25 = (bf16[256,512]{1,0:T(8,128)(2,1)S(1)}, bf16[256,512]{1,0:T(8,128)(2,1)S(1)}, u32[]{:S(2)}, u32[]{:S(2)}) collective-permute-start(bf16[256,512]{1,0:T(8,128)(2,1)S(1)} %bitcast.102), channel_id=1, source_target_pairs={{0,4},{2,6},{4,0},{6,2},{1,5},{3,7},{5,1},{7,3},{8,12},{10,14},{12... | collective-permute-start | bytes 786440 | tf_op jit(solution)/shard_map/ppermute | solution.py:381
  99.6 21.5 %collective-permute-start.24 = (bf16[256,512]{1,0:T(8,128)(2,1)S(1)}, bf16[256,512]{1,0:T(8,128)(2,1)S(1)}, u32[]{:S(2)}, u32[]{:S(2)}) collective-permute-start(bf16[256,512]{1,0:T(8,128)(2,1)S(1)} %bitcast.103), channel_id=1, source_target_pairs={{0,2},{2,0},{4,6},{6,4},{1,3},{3,1},{5,7},{7,5},{8,10},{10,8},{12,... | collective-permute-start | bytes 786440 | tf_op jit(solution)/shard_map/ppermute | solution.py:381
  117.6 9.5 %collective-permute-start.12 = (bf16[128,1024]{1,0:T(8,128)(2,1)}, bf16[128,1024]{1,0:T(8,128)(2,1)}, u32[]{:S(2)}, u32[]{:S(2)}) collective-permute-start(bf16[128,1024]{1,0:T(8,128)(2,1)} %get-tuple-element.92.refs_0_), channel_id=1, source_target_pairs={{0,17},{1,16},{16,1},{17,0},{2,19},{3,18},{18,3},{19,2},{4,21},{5,... | collective-permute-start | bytes 786440 | tf_op jit(solution)/shard_map/ppermute | solution.py:381
  118.3 11.4 %collective-permute-start.11 = (bf16[128,1024]{1,0:T(8,128)(2,1)}, bf16[128,1024]{1,0:T(8,128)(2,1)}, u32[]{:S(2)}, u32[]{:S(2)}) collective-permute-start(bf16[128,1024]{1,0:T(8,128)(2,1)} %get-tuple-element.92.refs_0_), channel_id=1, source_target_pairs={{0,16},{1,17},{16,0},{17,1},{2,18},{3,19},{18,2},{19,3},{4,20},{5,... | collective-permute-start | bytes 786440 | tf_op jit(solution)/shard_map/ppermute | solution.py:381
  120.4 9.3 %collective-permute-start.10 = (bf16[128,1024]{1,0:T(8,128)(2,1)}, bf16[128,1024]{1,0:T(8,128)(2,1)}, u32[]{:S(2)}, u32[]{:S(2)}) collective-permute-start(bf16[128,1024]{1,0:T(8,128)(2,1)} %get-tuple-element.92.refs_0_), channel_id=1, source_target_pairs={{0,1},{1,0},{16,17},{17,16},{2,3},{3,2},{18,19},{19,18},{4,5},{5,4... | collective-permute-start | bytes 786440 | tf_op jit(solution)/shard_map/ppermute | solution.py:381
  121.1 9.2 %collective-permute-start.26 = (bf16[256,512]{1,0:T(8,128)(2,1)S(1)}, bf16[256,512]{1,0:T(8,128)(2,1)S(1)}, u32[]{:S(2)}, u32[]{:S(2)}) collective-permute-start(bf16[256,512]{1,0:T(8,128)(2,1)S(1)} %collective-permute-done.25.refs_2_), channel_id=1, source_target_pairs={{0,2},{2,0},{4,6},{6,4},{1,3},{3,1},{5,7},{7,5},{8,10},{10,8},{12,... | collective-permute-start | bytes 786440 | tf_op jit(solution)/shard_map/ppermute | solution.py:381
  121.1 11.8 %collective-permute-start.13 = (bf16[128,1024]{1,0:T(8,128)(2,1)}, bf16[128,1024]{1,0:T(8,128)(2,1)S(1)}, u32[]{:S(2)}, u32[]{:S(2)}) collective-permute-start(bf16[128,1024]{1,0:T(8,128)(2,1)} %get-tuple-element.92.refs_0_), channel_id=1, source_target_pairs={{0,8},{8,0},{1,9},{9,1},{2,10},{10,2},{3,11},{11,3},{4,12},{12,4},... | collective-permute-start | bytes 786440 | tf_op jit(solution)/shard_map/ppermute | solution.py:381
  148.4 9.2 %collective-permute-start.28 = (bf16[128,1024]{1,0:T(8,128)(2,1)S(1)}, bf16[128,1024]{1,0:T(8,128)(2,1)S(1)}, u32[]{:S(2)}, u32[]{:S(2)}) collective-permute-start(bf16[128,1024]{1,0:T(8,128)(2,1)S(1)} %get-tuple-element.101), channel_id=1, source_target_pairs={{0,1},{1,0},{16,17},{17,16},{2,3},{3,2},{18,19},{19,18},{4,5},{5,4... | collective-permute-start | bytes 786440 | tf_op jit(solution)/shard_map/ppermute | solution.py:381
  149.1 13.7 %collective-permute-start.29 = (bf16[128,1024]{1,0:T(8,128)(2,1)S(1)}, bf16[128,1024]{1,0:T(8,128)(2,1)S(1)}, u32[]{:S(2)}, u32[]{:S(2)}) collective-permute-start(bf16[128,1024]{1,0:T(8,128)(2,1)S(1)} %get-tuple-element.102), channel_id=1, source_target_pairs={{0,16},{1,17},{16,0},{17,1},{2,18},{3,19},{18,2},{19,3},{4,20},{5,... | collective-permute-start | bytes 786440 | tf_op jit(solution)/shard_map/ppermute | solution.py:381
  150.2 12.6 %collective-permute-start.30 = (bf16[128,1024]{1,0:T(8,128)(2,1)S(1)}, bf16[128,1024]{1,0:T(8,128)(2,1)S(1)}, u32[]{:S(2)}, u32[]{:S(2)}) collective-permute-start(bf16[128,1024]{1,0:T(8,128)(2,1)S(1)} %get-tuple-element.103), channel_id=1, source_target_pairs={{0,17},{1,16},{16,1},{17,0},{2,19},{3,18},{18,3},{19,2},{4,21},{5,... | collective-permute-start | bytes 786440 | tf_op jit(solution)/shard_map/ppermute | solution.py:381
  164.5 10.2 %collective-permute-start.33 = (bf16[128,1024]{1,0:T(8,128)(2,1)S(1)}, bf16[128,1024]{1,0:T(8,128)(2,1)S(1)}, u32[]{:S(2)}, u32[]{:S(2)}) collective-permute-start(bf16[128,1024]{1,0:T(8,128)(2,1)S(1)} %get-tuple-element.106.refs_0_), channel_id=1, source_target_pairs={{0,17},{1,16},{16,1},{17,0},{2,19},{3,18},{18,3},{19,2},{4,21},{5,... | collective-permute-start | bytes 786440 | tf_op jit(solution)/shard_map/ppermute | solution.py:381
  165.9 12.5 %collective-permute-start.32 = (bf16[128,1024]{1,0:T(8,128)(2,1)S(1)}, bf16[128,1024]{1,0:T(8,128)(2,1)S(1)}, u32[]{:S(2)}, u32[]{:S(2)}) collective-permute-start(bf16[128,1024]{1,0:T(8,128)(2,1)S(1)} %get-tuple-element.106.refs_0_), channel_id=1, source_target_pairs={{0,16},{1,17},{16,0},{17,1},{2,18},{3,19},{18,2},{19,3},{4,20},{5,... | collective-permute-start | bytes 786440 | tf_op jit(solution)/shard_map/ppermute | solution.py:381
  167.4 11.0 %collective-permute-start.31 = (bf16[128,1024]{1,0:T(8,128)(2,1)S(1)}, bf16[128,1024]{1,0:T(8,128)(2,1)S(1)}, u32[]{:S(2)}, u32[]{:S(2)}) collective-permute-start(bf16[128,1024]{1,0:T(8,128)(2,1)S(1)} %get-tuple-element.106.refs_0_), channel_id=1, source_target_pairs={{0,1},{1,0},{16,17},{17,16},{2,3},{3,2},{18,19},{19,18},{4,5},{5,4... | collective-permute-start | bytes 786440 | tf_op jit(solution)/shard_map/ppermute | solution.py:381
  168.1 11.7 %collective-permute-start.34 = (bf16[128,1024]{1,0:T(8,128)(2,1)S(1)}, bf16[128,1024]{1,0:T(8,128)(2,1)S(1)}, u32[]{:S(2)}, u32[]{:S(2)}) collective-permute-start(bf16[128,1024]{1,0:T(8,128)(2,1)S(1)} %get-tuple-element.106.refs_0_), channel_id=1, source_target_pairs={{0,8},{8,0},{1,9},{9,1},{2,10},{10,2},{3,11},{11,3},{4,12},{12,4},... | collective-permute-start | bytes 786440 | tf_op jit(solution)/shard_map/ppermute | solution.py:381
  193.0 9.2 %collective-permute-start.39 = (bf16[128,1024]{1,0:T(8,128)(2,1)S(1)}, bf16[128,1024]{1,0:T(8,128)(2,1)S(1)}, u32[]{:S(2)}, u32[]{:S(2)}) collective-permute-start(bf16[128,1024]{1,0:T(8,128)(2,1)S(1)} %get-tuple-element.114), channel_id=1, source_target_pairs={{0,1},{1,0},{16,17},{17,16},{2,3},{3,2},{18,19},{19,18},{4,5},{5,4... | collective-permute-start | bytes 786440 | tf_op jit(solution)/shard_map/ppermute | solution.py:381
  194.6 13.9 %collective-permute-start.40 = (bf16[128,1024]{1,0:T(8,128)(2,1)S(1)}, bf16[128,1024]{1,0:T(8,128)(2,1)S(1)}, u32[]{:S(2)}, u32[]{:S(2)}) collective-permute-start(bf16[128,1024]{1,0:T(8,128)(2,1)S(1)} %get-tuple-element.118), channel_id=1, source_target_pairs={{0,16},{1,17},{16,0},{17,1},{2,18},{3,19},{18,2},{19,3},{4,20},{5,... | collective-permute-start | bytes 786440 | tf_op jit(solution)/shard_map/ppermute | solution.py:381
  195.0 13.4 %collective-permute-start.41 = (bf16[128,1024]{1,0:T(8,128)(2,1)S(1)}, bf16[128,1024]{1,0:T(8,128)(2,1)S(1)}, u32[]{:S(2)}, u32[]{:S(2)}) collective-permute-start(bf16[128,1024]{1,0:T(8,128)(2,1)S(1)} %get-tuple-element.119), channel_id=1, source_target_pairs={{0,17},{1,16},{16,1},{17,0},{2,19},{3,18},{18,3},{19,2},{4,21},{5,... | collective-permute-start | bytes 786440 | tf_op jit(solution)/shard_map/ppermute | solution.py:381
  216.2 13.4 %all-to-all-start.2 = ((bf16[8,128,128]{2,1,0:T(8,128)(2,1)}), bf16[8,128,128]{2,1,0:T(8,128)(2,1)S(1)}, u32[]{:S(2)}, u32[]{:S(2)}) async-start(bf16[8,128,128]{2,1,0:T(8,128)(2,1)} %get-tuple-element.123), calls=%async_computation.2 | async-start | bytes 524288 | tf_op jit(solution)/shard_map/all_to_all | solution.py:950
  220.1 48.3 %reduce-scatter.3.cloned.1.call-start = ((), (), s32[]{:S(2)}) async-start(), calls=%async_computation.9 | async-start | bytes 1310720 | tf_op jit(solution)/shard_map/reduce_scatter | solution.py:943
  229.6 15.7 %collective-permute-start.43 = (bf16[144,1024]{1,0:T(8,128)(2,1)}, bf16[144,1024]{1,0:T(8,128)(2,1)S(1)}, u32[]{:S(2)}, u32[]{:S(2)}) collective-permute-start(bf16[144,1024]{1,0:T(8,128)(2,1)} %copy-done.38), channel_id=1, source_target_pairs={{0,1},{1,0},{16,17},{17,16},{2,3},{3,2},{18,19},{19,18},{4,5},{5,4... | collective-permute-start | bytes 884744 | tf_op jit(solution)/shard_map/ppermute | solution.py:381
  231.0 14.3 %collective-permute-start.44 = (bf16[144,1024]{1,0:T(8,128)(2,1)}, bf16[144,1024]{1,0:T(8,128)(2,1)S(1)}, u32[]{:S(2)}, u32[]{:S(2)}) collective-permute-start(bf16[144,1024]{1,0:T(8,128)(2,1)} %copy-done.37), channel_id=1, source_target_pairs={{0,16},{1,17},{16,0},{17,1},{2,18},{3,19},{18,2},{19,3},{4,20},{5,... | collective-permute-start | bytes 884744 | tf_op jit(solution)/shard_map/ppermute | solution.py:381
  231.9 13.4 %collective-permute-start.45 = (bf16[144,1024]{1,0:T(8,128)(2,1)S(1)}, bf16[144,1024]{1,0:T(8,128)(2,1)S(1)}, u32[]{:S(2)}, u32[]{:S(2)}) collective-permute-start(bf16[144,1024]{1,0:T(8,128)(2,1)S(1)} %get-tuple-element.138), channel_id=1, source_target_pairs={{0,17},{1,16},{16,1},{17,0},{2,19},{3,18},{18,3},{19,2},{4,21},{5,... | collective-permute-start | bytes 884744 | tf_op jit(solution)/shard_map/ppermute | solution.py:381
  250.2 11.9 %collective-permute-start.46 = (bf16[256,1024]{1,0:T(8,128)(2,1)}, bf16[256,1024]{1,0:T(8,128)(2,1)S(1)}, u32[]{:S(2)}, u32[]{:S(2)}) collective-permute-start(bf16[256,1024]{1,0:T(8,128)(2,1)} %get-tuple-element.143), channel_id=1, source_target_pairs={{0,1},{1,0},{2,3},{3,2},{4,5},{5,4},{6,7},{7,6},{8,9},{9,8},{10,11... | collective-permute-start | bytes 1572872 | tf_op jit(solution)/shard_map/ppermute | solution.py:381
  264.2 11.2 %collective-permute-start.51 = (bf16[272,384]{1,0:T(8,128)(2,1)S(1)}, bf16[272,384]{1,0:T(8,128)(2,1)S(1)}, u32[]{:S(2)}, u32[]{:S(2)}) collective-permute-start(bf16[272,384]{1,0:T(8,128)(2,1)S(1)} %fusion.8), channel_id=1, source_target_pairs={{0,16},{16,0},{1,17},{17,1},{2,18},{18,2},{3,19},{19,3},{4,20},{20... | collective-permute-start | bytes 626696 | tf_op jit(solution)/shard_map/ppermute | solution.py:381
  265.3 23.4 %collective-permute-start.47 = (bf16[256,1024]{1,0:T(8,128)(2,1)}, bf16[256,1024]{1,0:T(8,128)(2,1)S(1)}, u32[]{:S(2)}, u32[]{:S(2)}) collective-permute-start(bf16[256,1024]{1,0:T(8,128)(2,1)} %get-tuple-element.144), channel_id=1, source_target_pairs={{0,1},{1,0},{2,3},{3,2},{4,5},{5,4},{6,7},{7,6},{8,9},{9,8},{10,11... | collective-permute-start | bytes 1572872 | tf_op jit(solution)/shard_map/ppermute | solution.py:381
  267.8 21.0 %collective-permute-start.48 = (bf16[256,1024]{1,0:T(8,128)(2,1)}, bf16[256,1024]{1,0:T(8,128)(2,1)}, u32[]{:S(2)}, u32[]{:S(2)}) collective-permute-start(bf16[256,1024]{1,0:T(8,128)(2,1)} %add_convert_fusion), channel_id=1, source_target_pairs={{0,2},{2,0},{4,6},{6,4},{1,3},{3,1},{5,7},{7,5},{8,10},{10,8},{12,... | collective-permute-start | bytes 1572872 | tf_op jit(solution)/shard_map/ppermute | solution.py:381
  268.4 10.8 %all-to-all-start.4 = ((bf16[8,32,512]{2,1,0:T(8,128)(2,1)}), bf16[8,32,512]{2,1,0:T(8,128)(2,1)S(1)}, u32[]{:S(2)}, u32[]{:S(2)}) async-start(bf16[8,32,512]{2,1,0:T(8,128)(2,1)} %bitcast.105), calls=%async_computation.5 | async-start | bytes 524288 | tf_op jit(solution)/shard_map/all_to_all | solution.py:1005
  272.8 12.3 %collective-permute-start.53 = (bf16[48,1024]{1,0:T(8,128)(2,1)S(1)}, bf16[48,1024]{1,0:T(8,128)(2,1)S(1)}, u32[]{:S(2)}, u32[]{:S(2)}) collective-permute-start(bf16[48,1024]{1,0:T(8,128)(2,1)S(1)} %fusion.10), channel_id=1, source_target_pairs={{0,4},{2,6},{4,0},{6,2},{1,5},{3,7},{5,1},{7,3},{8,12},{10,14},{12... | collective-permute-start | bytes 294920 | tf_op jit(solution)/shard_map/ppermute | solution.py:381
  279.2 21.4 %all-to-all-start.3 = ((bf16[8,48,384]{2,1,0:T(8,128)(2,1)}), bf16[8,48,384]{2,1,0:T(8,128)(2,1)S(1)}, u32[]{:S(2)}, u32[]{:S(2)}) async-start(bf16[8,48,384]{2,1,0:T(8,128)(2,1)} %pad_maximum_fusion), calls=%async_computation.3 | async-start | bytes 589824 | tf_op jit(solution)/shard_map/all_to_all | solution.py:992
  290.2 15.4 %collective-permute-start.49 = (bf16[128,1024]{1,0:T(8,128)(2,1)S(1)}, bf16[128,1024]{1,0:T(8,128)(2,1)S(1)}, u32[]{:S(2)}, u32[]{:S(2)}) collective-permute-start(bf16[128,1024]{1,0:T(8,128)(2,1)S(1)} %slice.226), channel_id=1, source_target_pairs={{0,4},{2,6},{4,0},{6,2},{1,5},{3,7},{5,1},{7,3},{8,12},{10,14},{12... | collective-permute-start | bytes 786440 | tf_op jit(solution)/shard_map/ppermute | solution.py:381
  (77 other events, 687.0 us)
Sparse Core Ops, SparseCore 0:
  11.0 63.6 all-gather.2
  76.2 39.7 all-gather.4
  191.1 28.5 reduce-scatter.4
  222.9 27.9 reduce-scatter.2
